TPU v7x, 256 devices: a whole 4x4x8 slice. The times are simulated.
256 devices in a mesh: row: 8 (over x, core), col: 32 (over y, z).
Axes of the slice: x: 4, y: 4, z: 8, core: 2. Of those that a mesh axis runs over, the one named last changes fastest.
Arguments:
- strand_layout: float32 [7, 131072], P(None, ('row', 'col')), may hold values from -0.0034938562 to 1, as said below
- strand_amperes_panel: float32 [16, 131072], P(None, ('row', 'col')), may hold values from -7 to 7
- krylov_vectors: float32 [64, 131072], P(None, ('row', 'col')), may hold values from -0.015625 to 0.015625
- strand_kelvin: float32 [131072], P(('row', 'col')), may hold values from 1.9 to 10
- strand_ohmic_value: float32 [131072], P(('row', 'col')), may hold values from 0.2 to 1
- strand_warmer_slot: int32 [131072], P(('row', 'col')), may hold values from 0 to 7
- warmer_kelvin_gain: float32 [8], replicated, may hold values from 0 to 6
- strand_region_slot: int32 [131072], P(('row', 'col')), may hold values from 0 to 31
- region_threshold_kelvin: float32 [32], replicated, may hold values from 5 to 12
Outputs:
- q_next: float32 [16, 131072], P(None, ('row', 'col'))
- hess: float32 [64, 16], replicated
- chol: float32 [16, 16], replicated
- joule: float32 [131072], P(('row', 'col'))
Inputs may be any that keep to these rules, and one draw needn't show every extreme that they name: `strand_layout`: rows 0-2 lie in the unit cube, rows 3-5 within -0.4 * sqrt(10 / 131072) to sqrt(10 / 131072), row 6 in 0.005 to 0.05.
All inputs are finite; a program needn't handle non-finite values.
Results may differ from a plain program's by a relative error of at most 0.0007.
Values may be sent and summed in bfloat16 or wider, within the bound.
No kernel may reach another device: no remote copies, remote signals or barrier semaphores. Data moves between devices by JAX's collectives and lax.ppermute only.
A program may use at most 64 MiB of HBM per device.

v0:
```python
import math

import jax
import jax.numpy as jnp
from jax import lax
from jax.sharding import PartitionSpec as P


def make_tile(rows_geom, cols_geom):
    dist = (rows_geom[0][:, None] - cols_geom[0][None, :]) ** 2
    dist = dist + (rows_geom[1][:, None] - cols_geom[1][None, :]) ** 2
    dist = dist + (rows_geom[2][:, None] - cols_geom[2][None, :]) ** 2
    soft = rows_geom[6][:, None] ** 2 + cols_geom[6][None, :] ** 2
    inner = rows_geom[3][:, None] * cols_geom[3][None, :]
    inner = inner + rows_geom[4][:, None] * cols_geom[4][None, :]
    inner = inner + rows_geom[5][:, None] * cols_geom[5][None, :]
    return (inner / jnp.sqrt(dist + soft)).astype(jnp.bfloat16)


def block_product(rows_geom, cols_geom, cols_vec):
    count = rows_geom.shape[1]
    width = math.gcd(count, 1024)
    blocks = rows_geom.reshape(7, count // width, width).transpose(1, 0, 2)

    def one_block(geom):
        tile = make_tile(geom, cols_geom)
        return jnp.einsum("kc,rc->kr", cols_vec, tile, preferred_element_type=jnp.float32)

    out = lax.map(one_block, blocks)
    return out.transpose(1, 0, 2).reshape(cols_vec.shape[0], count)


def gathered_entries(ids, table):
    levels = jnp.arange(table.shape[0], dtype=jnp.int32)
    match = ids[None, :] == levels[:, None]
    return jnp.sum(jnp.where(match, table[:, None], jnp.float32(0.0)), axis=0)


def local(
    strand_layout,
    strand_amperes_panel,
    krylov_vectors,
    strand_kelvin,
    strand_ohmic_value,
    strand_warmer_slot,
    warmer_kelvin_gain,
    strand_region_slot,
    region_threshold_kelvin,
):
    hi = lax.Precision.HIGHEST
    owned = strand_amperes_panel.shape[1]
    rows_geom = lax.all_gather(strand_layout, "col", axis=1, tiled=True)
    cols_geom = lax.all_gather(strand_layout, "row", axis=1, tiled=True)
    q_wire = strand_amperes_panel.astype(jnp.bfloat16)
    partial_flux = block_product(
        rows_geom, cols_geom, lax.all_gather(q_wire, "row", axis=1, tiled=True)
    )
    totals = lax.psum(partial_flux, "col")
    flux = lax.dynamic_slice_in_dim(totals, lax.axis_index("col") * owned, owned, 1)
    warmer_increment = gathered_entries(strand_warmer_slot, warmer_kelvin_gain)
    threshold_kelvin = gathered_entries(strand_region_slot, region_threshold_kelvin)
    ohmic_specific_value = strand_ohmic_value * jax.nn.sigmoid(
        strand_kelvin + warmer_increment - threshold_kelvin
    )
    joule = ohmic_specific_value * jnp.mean(strand_amperes_panel * strand_amperes_panel, axis=0)
    image = ohmic_specific_value[None, :] * strand_amperes_panel + flux
    local_proj = jnp.dot(krylov_vectors, image.T, precision=hi)
    hess = lax.psum(local_proj, ("row", "col"))
    resid = image - jnp.dot(hess.T, krylov_vectors, precision=hi)
    gram = lax.psum(jnp.dot(resid, resid.T, precision=hi), ("row", "col"))
    chol = jnp.linalg.cholesky(gram)
    q_next = jax.scipy.linalg.solve_triangular(chol, resid, lower=True)
    return (q_next, hess, chol, joule)


def solution(mesh):
    return jax.shard_map(
        local,
        mesh=mesh,
        in_specs=(
            P(None, ("row", "col")),
            P(None, ("row", "col")),
            P(None, ("row", "col")),
            P(("row", "col")),
            P(("row", "col")),
            P(("row", "col")),
            P(),
            P(("row", "col")),
            P(),
        ),
        out_specs=(P(None, ("row", "col")), P(), P(), P(("row", "col"))),
        check_vma=False,
    )
```

profile of v0, /device:TPU:32, one launch (start us, length us, event | category | flops | bytes accessed | tf_op | source)
XLA Modules:
  0.0 557.2 jit_solution(18074517379338583647)
XLA Ops:
  7.2 13.3 %all_gather.10 = f32[7,4096]{1,0:T(8,128)S(1)} all-gather(f32[7,512]{1,0:T(8,128)} %param.11), channel_id=1, replica_groups=mesh['row'=8,'col'=32] {'row'}, dimensions={1}, use_global_device_ids=true | all-gather | bytes 129024 | tf_op jit(solution)/shard_map/all_gather | solution.py:53
  20.5 51.9 %all_gather.9 = f32[7,16384]{1,0:T(8,128)S(1)} all-gather(f32[7,512]{1,0:T(8,128)} %param.11), channel_id=1, replica_groups=mesh['row'=8,'col'=32] {'col'}, dimensions={1}, use_global_device_ids=true | all-gather | bytes 473088 | tf_op jit(solution)/shard_map/all_gather | solution.py:52
  72.4 0.9 multiply_reduce_fusion
  73.3 12.8 %all_gather.11 = bf16[16,4096]{1,0:T(8,128)(2,1)S(1)} all-gather(bf16[16,512]{1,0:T(8,128)(2,1)S(1)} %get-tuple-element.87), channel_id=1, replica_groups=mesh['row'=8,'col'=32] {'row'}, dimensions={1}, use_global_device_ids=true | all-gather | bytes 147456 | tf_op jit(solution)/shard_map/all_gather | solution.py:56
  86.1 160.7 %while.11 = (s32[]{:T(128)}, f32[16,16,1024]{2,1,0:T(8,128)S(1)}, f32[16,7,1024]{2,1,0:T(8,128)S(1)}, f32[7,4096]{1,0:T(8,128)S(1)}, f32[1,4096]{1,0:T(1,128)S(1...) while((s32[]{:T(128)}, f32[16,16,1024]{2,1,0:T(8,128)S(1)}, ...), condition=%wide.region_3.4_spmd, body=%wide.region_2.3_spmd.sunk | while | flops 205521920 | bytes 594157 | solution.py:29
  86.2 9.9 %fusion.21 = f32[16,16,1024]{2,1,0:T(8,128)S(1)} fusion(f32[16,16,1024]{2,1,0:T(8,128)S(1)} %get-tuple-element.166, s32[]{:T(128)} %get-tuple-element.165, bf16[16,4096]{1,0:T(8,128)(2,1)S(1)} %get-tuple-element.184, f32[4096]{0:T(1024)S(1)} %bitcast.92, f32[1024]{0:T(1024)S(1)} %bitcast.91, f32[4096]{0:T(1024)S(1)} %bitcast.80, ...), kind=kOutput, calls=%fused_computation.3.clone.1 | convolution fusion | flops 205520896 | bytes 339972 | tf_op jit(solution)/shard_map/while/body/eval_jaxpr/kc,rc->kr/dot_general | solution.py:27
  96.3 9.9 %fusion.21 = f32[16,16,1024]{2,1,0:T(8,128)S(1)} fusion(f32[16,16,1024]{2,1,0:T(8,128)S(1)} %get-tuple-element.166, s32[]{:T(128)} %get-tuple-element.165, bf16[16,4096]{1,0:T(8,128)(2,1)S(1)} %get-tuple-element.184, f32[4096]{0:T(1024)S(1)} %bitcast.92, f32[1024]{0:T(1024)S(1)} %bitcast.91, f32[4096]{0:T(1024)S(1)} %bitcast.80, ...), kind=kOutput, calls=%fused_computation.3.clone.1 | convolution fusion | flops 205520896 | bytes 339972 | tf_op jit(solution)/shard_map/while/body/eval_jaxpr/kc,rc->kr/dot_general | solution.py:27
  106.3 9.9 %fusion.21 = f32[16,16,1024]{2,1,0:T(8,128)S(1)} fusion(f32[16,16,1024]{2,1,0:T(8,128)S(1)} %get-tuple-element.166, s32[]{:T(128)} %get-tuple-element.165, bf16[16,4096]{1,0:T(8,128)(2,1)S(1)} %get-tuple-element.184, f32[4096]{0:T(1024)S(1)} %bitcast.92, f32[1024]{0:T(1024)S(1)} %bitcast.91, f32[4096]{0:T(1024)S(1)} %bitcast.80, ...), kind=kOutput, calls=%fused_computation.3.clone.1 | convolution fusion | flops 205520896 | bytes 339972 | tf_op jit(solution)/shard_map/while/body/eval_jaxpr/kc,rc->kr/dot_general | solution.py:27
  116.3 9.9 %fusion.21 = f32[16,16,1024]{2,1,0:T(8,128)S(1)} fusion(f32[16,16,1024]{2,1,0:T(8,128)S(1)} %get-tuple-element.166, s32[]{:T(128)} %get-tuple-element.165, bf16[16,4096]{1,0:T(8,128)(2,1)S(1)} %get-tuple-element.184, f32[4096]{0:T(1024)S(1)} %bitcast.92, f32[1024]{0:T(1024)S(1)} %bitcast.91, f32[4096]{0:T(1024)S(1)} %bitcast.80, ...), kind=kOutput, calls=%fused_computation.3.clone.1 | convolution fusion | flops 205520896 | bytes 339972 | tf_op jit(solution)/shard_map/while/body/eval_jaxpr/kc,rc->kr/dot_general | solution.py:27
  126.4 9.9 %fusion.21 = f32[16,16,1024]{2,1,0:T(8,128)S(1)} fusion(f32[16,16,1024]{2,1,0:T(8,128)S(1)} %get-tuple-element.166, s32[]{:T(128)} %get-tuple-element.165, bf16[16,4096]{1,0:T(8,128)(2,1)S(1)} %get-tuple-element.184, f32[4096]{0:T(1024)S(1)} %bitcast.92, f32[1024]{0:T(1024)S(1)} %bitcast.91, f32[4096]{0:T(1024)S(1)} %bitcast.80, ...), kind=kOutput, calls=%fused_computation.3.clone.1 | convolution fusion | flops 205520896 | bytes 339972 | tf_op jit(solution)/shard_map/while/body/eval_jaxpr/kc,rc->kr/dot_general | solution.py:27
  136.4 9.9 %fusion.21 = f32[16,16,1024]{2,1,0:T(8,128)S(1)} fusion(f32[16,16,1024]{2,1,0:T(8,128)S(1)} %get-tuple-element.166, s32[]{:T(128)} %get-tuple-element.165, bf16[16,4096]{1,0:T(8,128)(2,1)S(1)} %get-tuple-element.184, f32[4096]{0:T(1024)S(1)} %bitcast.92, f32[1024]{0:T(1024)S(1)} %bitcast.91, f32[4096]{0:T(1024)S(1)} %bitcast.80, ...), kind=kOutput, calls=%fused_computation.3.clone.1 | convolution fusion | flops 205520896 | bytes 339972 | tf_op jit(solution)/shard_map/while/body/eval_jaxpr/kc,rc->kr/dot_general | solution.py:27
  146.5 9.9 %fusion.21 = f32[16,16,1024]{2,1,0:T(8,128)S(1)} fusion(f32[16,16,1024]{2,1,0:T(8,128)S(1)} %get-tuple-element.166, s32[]{:T(128)} %get-tuple-element.165, bf16[16,4096]{1,0:T(8,128)(2,1)S(1)} %get-tuple-element.184, f32[4096]{0:T(1024)S(1)} %bitcast.92, f32[1024]{0:T(1024)S(1)} %bitcast.91, f32[4096]{0:T(1024)S(1)} %bitcast.80, ...), kind=kOutput, calls=%fused_computation.3.clone.1 | convolution fusion | flops 205520896 | bytes 339972 | tf_op jit(solution)/shard_map/while/body/eval_jaxpr/kc,rc->kr/dot_general | solution.py:27
  156.5 9.9 %fusion.21 = f32[16,16,1024]{2,1,0:T(8,128)S(1)} fusion(f32[16,16,1024]{2,1,0:T(8,128)S(1)} %get-tuple-element.166, s32[]{:T(128)} %get-tuple-element.165, bf16[16,4096]{1,0:T(8,128)(2,1)S(1)} %get-tuple-element.184, f32[4096]{0:T(1024)S(1)} %bitcast.92, f32[1024]{0:T(1024)S(1)} %bitcast.91, f32[4096]{0:T(1024)S(1)} %bitcast.80, ...), kind=kOutput, calls=%fused_computation.3.clone.1 | convolution fusion | flops 205520896 | bytes 339972 | tf_op jit(solution)/shard_map/while/body/eval_jaxpr/kc,rc->kr/dot_general | solution.py:27
  166.6 9.9 %fusion.21 = f32[16,16,1024]{2,1,0:T(8,128)S(1)} fusion(f32[16,16,1024]{2,1,0:T(8,128)S(1)} %get-tuple-element.166, s32[]{:T(128)} %get-tuple-element.165, bf16[16,4096]{1,0:T(8,128)(2,1)S(1)} %get-tuple-element.184, f32[4096]{0:T(1024)S(1)} %bitcast.92, f32[1024]{0:T(1024)S(1)} %bitcast.91, f32[4096]{0:T(1024)S(1)} %bitcast.80, ...), kind=kOutput, calls=%fused_computation.3.clone.1 | convolution fusion | flops 205520896 | bytes 339972 | tf_op jit(solution)/shard_map/while/body/eval_jaxpr/kc,rc->kr/dot_general | solution.py:27
  176.6 9.9 %fusion.21 = f32[16,16,1024]{2,1,0:T(8,128)S(1)} fusion(f32[16,16,1024]{2,1,0:T(8,128)S(1)} %get-tuple-element.166, s32[]{:T(128)} %get-tuple-element.165, bf16[16,4096]{1,0:T(8,128)(2,1)S(1)} %get-tuple-element.184, f32[4096]{0:T(1024)S(1)} %bitcast.92, f32[1024]{0:T(1024)S(1)} %bitcast.91, f32[4096]{0:T(1024)S(1)} %bitcast.80, ...), kind=kOutput, calls=%fused_computation.3.clone.1 | convolution fusion | flops 205520896 | bytes 339972 | tf_op jit(solution)/shard_map/while/body/eval_jaxpr/kc,rc->kr/dot_general | solution.py:27
  186.7 9.9 %fusion.21 = f32[16,16,1024]{2,1,0:T(8,128)S(1)} fusion(f32[16,16,1024]{2,1,0:T(8,128)S(1)} %get-tuple-element.166, s32[]{:T(128)} %get-tuple-element.165, bf16[16,4096]{1,0:T(8,128)(2,1)S(1)} %get-tuple-element.184, f32[4096]{0:T(1024)S(1)} %bitcast.92, f32[1024]{0:T(1024)S(1)} %bitcast.91, f32[4096]{0:T(1024)S(1)} %bitcast.80, ...), kind=kOutput, calls=%fused_computation.3.clone.1 | convolution fusion | flops 205520896 | bytes 339972 | tf_op jit(solution)/shard_map/while/body/eval_jaxpr/kc,rc->kr/dot_general | solution.py:27
  196.7 9.9 %fusion.21 = f32[16,16,1024]{2,1,0:T(8,128)S(1)} fusion(f32[16,16,1024]{2,1,0:T(8,128)S(1)} %get-tuple-element.166, s32[]{:T(128)} %get-tuple-element.165, bf16[16,4096]{1,0:T(8,128)(2,1)S(1)} %get-tuple-element.184, f32[4096]{0:T(1024)S(1)} %bitcast.92, f32[1024]{0:T(1024)S(1)} %bitcast.91, f32[4096]{0:T(1024)S(1)} %bitcast.80, ...), kind=kOutput, calls=%fused_computation.3.clone.1 | convolution fusion | flops 205520896 | bytes 339972 | tf_op jit(solution)/shard_map/while/body/eval_jaxpr/kc,rc->kr/dot_general | solution.py:27
  206.8 9.9 %fusion.21 = f32[16,16,1024]{2,1,0:T(8,128)S(1)} fusion(f32[16,16,1024]{2,1,0:T(8,128)S(1)} %get-tuple-element.166, s32[]{:T(128)} %get-tuple-element.165, bf16[16,4096]{1,0:T(8,128)(2,1)S(1)} %get-tuple-element.184, f32[4096]{0:T(1024)S(1)} %bitcast.92, f32[1024]{0:T(1024)S(1)} %bitcast.91, f32[4096]{0:T(1024)S(1)} %bitcast.80, ...), kind=kOutput, calls=%fused_computation.3.clone.1 | convolution fusion | flops 205520896 | bytes 339972 | tf_op jit(solution)/shard_map/while/body/eval_jaxpr/kc,rc->kr/dot_general | solution.py:27
  216.8 9.9 %fusion.21 = f32[16,16,1024]{2,1,0:T(8,128)S(1)} fusion(f32[16,16,1024]{2,1,0:T(8,128)S(1)} %get-tuple-element.166, s32[]{:T(128)} %get-tuple-element.165, bf16[16,4096]{1,0:T(8,128)(2,1)S(1)} %get-tuple-element.184, f32[4096]{0:T(1024)S(1)} %bitcast.92, f32[1024]{0:T(1024)S(1)} %bitcast.91, f32[4096]{0:T(1024)S(1)} %bitcast.80, ...), kind=kOutput, calls=%fused_computation.3.clone.1 | convolution fusion | flops 205520896 | bytes 339972 | tf_op jit(solution)/shard_map/while/body/eval_jaxpr/kc,rc->kr/dot_general | solution.py:27
  226.8 9.9 %fusion.21 = f32[16,16,1024]{2,1,0:T(8,128)S(1)} fusion(f32[16,16,1024]{2,1,0:T(8,128)S(1)} %get-tuple-element.166, s32[]{:T(128)} %get-tuple-element.165, bf16[16,4096]{1,0:T(8,128)(2,1)S(1)} %get-tuple-element.184, f32[4096]{0:T(1024)S(1)} %bitcast.92, f32[1024]{0:T(1024)S(1)} %bitcast.91, f32[4096]{0:T(1024)S(1)} %bitcast.80, ...), kind=kOutput, calls=%fused_computation.3.clone.1 | convolution fusion | flops 205520896 | bytes 339972 | tf_op jit(solution)/shard_map/while/body/eval_jaxpr/kc,rc->kr/dot_general | solution.py:27
  236.9 9.9 %fusion.21 = f32[16,16,1024]{2,1,0:T(8,128)S(1)} fusion(f32[16,16,1024]{2,1,0:T(8,128)S(1)} %get-tuple-element.166, s32[]{:T(128)} %get-tuple-element.165, bf16[16,4096]{1,0:T(8,128)(2,1)S(1)} %get-tuple-element.184, f32[4096]{0:T(1024)S(1)} %bitcast.92, f32[1024]{0:T(1024)S(1)} %bitcast.91, f32[4096]{0:T(1024)S(1)} %bitcast.80, ...), kind=kOutput, calls=%fused_computation.3.clone.1 | convolution fusion | flops 205520896 | bytes 339972 | tf_op jit(solution)/shard_map/while/body/eval_jaxpr/kc,rc->kr/dot_general | solution.py:27
  246.8 1.1 copy.20
  249.4 144.8 %all-reduce.2.cloned.1.call-done = f32[16,16384]{1,0:T(8,128)} async-done(((f32[16,16384]{1,0:T(8,128)}), f32[16,16384]{1,0:T(8,128)}) %all-reduce.2.cloned.1.call-update) | async-done | bytes 1048592 | tf_op jit(solution)/shard_map/psum | solution.py:58
  394.3 0.9 convolution_bitcast_fusion
  395.2 75.4 %psum.22 = f32[64,16]{0,1:T(8,128)S(1)} all-reduce(f32[64,16]{0,1:T(8,128)S(1)} %convolution_bitcast_fusion), channel_id=1, replica_groups=mesh['row'=8,'col'=32] {'row','col'}, use_global_device_ids=true, to_apply=%region_5.6 | all-reduce | flops 1024 | bytes 8192 | tf_op jit(solution)/shard_map/psum | solution.py:68
  470.6 0.9 convolution_subtract_fusion
  471.7 73.2 %psum.23 = f32[16,16]{0,1:T(8,128)S(1)} all-reduce(f32[16,16]{0,1:T(8,128)S(1)} %fusion.8), channel_id=1, replica_groups=mesh['row'=8,'col'=32] {'row','col'}, use_global_device_ids=true, to_apply=%region_6.7 | all-reduce | flops 256 | bytes 2048 | tf_op jit(solution)/shard_map/psum | solution.py:70
  544.9 1.5 cholesky.16
  546.4 0.6 compare_reduce_fusion
  547.1 1.2 select_bitcast_fusion
  548.3 1.2 custom-call.7
  549.5 0.9 fusion.3
  (61 shorter events, 3.5 us)
Async XLA Ops:
  7.2 387.1 %copy-start = (f32[64,512]{1,0:T(8,128)S(1)}, f32[64,512]{1,0:T(8,128)}, u32[]{:S(2)}) copy-start(f32[64,512]{1,0:T(8,128)} %param.13) | copy-start | bytes 393220
  7.2 387.1 %all-reduce.2.cloned.1.call-start = ((), (), s32[]{:S(2)}) async-start(), calls=%async_computation | async-start | bytes 2097152 | tf_op jit(solution)/shard_map/psum | solution.py:58
  247.9 0.7 copy-start.5
  247.9 0.7 copy-start.7
  247.9 0.8 copy-start.6
  247.9 0.8 copy-start.8
  247.9 0.9 copy-start.3
  248.0 0.8 copy-start.4
  248.0 146.3 %copy-start.1 = (f32[16,512]{1,0:T(8,128)S(1)}, f32[16,512]{1,0:T(8,128)}, u32[]{:S(2)}) copy-start(f32[16,512]{1,0:T(8,128)} %param.12) | copy-start | bytes 98308
  470.6 79.8 %copy-start.2 = (f32[64,16]{0,1:T(8,128)}, f32[64,16]{0,1:T(8,128)S(1)}, u32[]{:S(2)}) copy-start(f32[64,16]{0,1:T(8,128)S(1)} %psum.22) | copy-start | bytes 12292
Sparse Core Ops, SparseCore 0:
  248.1 146.0 all-reduce.1
where the time goes:
time: 559 us; the launch traced here: 557 us
  blocking collectives  227 us (41%)
  matrix products  162 us (29%)
  waiting for transfers between devices  145 us (26%)
  between operations  14.1 us (3%)
  other arithmetic  6.86 us (1%)
    dot_general x16, matrix products, one_block(): jnp.einsum('kc,rc->kr', cols_vec, tile, preferred_element_type=jnp.float32)  159 us
    psum x1, waiting for transfers between devices, local(): totals = lax.psum(partial_flux, 'col')  145 us
    psum x1, blocking collectives, local(): hess = lax.psum(local_proj, ('row', 'col'))  75.4 us
    psum x1, blocking collectives, local(): gram = lax.psum(jnp.dot(resid, resid.T, precision=hi), ('row', 'col'))  73.2 us
    all_gather x1, blocking collectives, local(): rows_geom = lax.all_gather(strand_layout, 'col', axis=1, tiled=True)  51.9 us
    all_gather x1, blocking collectives, local(): cols_geom = lax.all_gather(strand_layout, 'row', axis=1, tiled=True)  13.3 us
    all_gather x1, blocking collectives, local(): lax.all_gather(q_wire, 'row', axis=1, tiled=True)  12.8 us
  transfers between devices with their start and end apart: 1, of which 1 were waited for; matrix products, arithmetic and copies ran while one was open for 0% of the time, Pallas kernels for 0%

commit v1 on v0

v1 whole, which is shorter than its diff:
```python
import functools

import jax
import jax.numpy as jnp
from jax import lax
from jax.experimental import pallas as pl
from jax.experimental.pallas import tpu as pltpu
from jax.sharding import PartitionSpec as P

HI = lax.Precision.HIGHEST
F32 = jnp.float32
BF16 = jnp.bfloat16
NT = (((1,), (1,)), ((), ()))
SECTIONS = 16
ROW_GROUP = 1024
ROW_TILE = 256
COL_TILE = 1024
COL_STEP = 2048
BLOCKS = ((1, 0), (1, 1), (3, 0), (3, 1), (2, 0), (2, 1), (0, 1), (0, 0))


def small_call(body, args, shapes, name, scalars=0):
    whole = pl.BlockSpec(memory_space=pltpu.VMEM)
    scalar = pl.BlockSpec(memory_space=pltpu.SMEM)
    return pl.pallas_call(
        body,
        in_specs=[whole] * (len(args) - scalars) + [scalar] * scalars,
        out_specs=[whole] * len(shapes),
        out_shape=[jax.ShapeDtypeStruct(shape, dtype) for shape, dtype in shapes],
        compiler_params=pltpu.CompilerParams(vmem_limit_bytes=16 * 2**20),
        name=name,
    )(*args)


def pieces(value, count):
    out = []
    for _ in range(count):
        piece = value.astype(BF16).astype(F32)
        out.append(piece)
        value = value - piece
    return out


def payload_body(layout_ref, amps_ref, out_ref):
    layout = layout_ref[...]
    high, low = pieces(layout[0:3] - 0.5, 2)
    centre = high + low
    square = centre * centre
    soft = square[0:1] + square[1:2] + square[2:3] + layout[6:7] * layout[6:7]
    parts = [high, low, *pieces(soft, 3), *pieces(layout[3:6], 2), jnp.ones_like(soft)]
    out_ref[0:16, :] = jnp.concatenate(parts, axis=0).astype(BF16)
    out_ref[16:32, :] = amps_ref[...].astype(BF16)


def heat_body(kelvin_ref, ohmic_ref, warmer_ref, region_ref, amps_ref, gain_ref, limit_ref, rho_ref, joule_ref):
    def entries(ids, table_ref):
        out = jnp.zeros(ids.shape, F32)
        for level in range(table_ref.shape[0]):
            out = jnp.where(ids == level, table_ref[level], out)
        return out

    warm = entries(warmer_ref[...], gain_ref)
    limit = entries(region_ref[...], limit_ref)
    rho = ohmic_ref[...] / (1.0 + jnp.exp(limit - (kelvin_ref[...] + warm)))
    amps = amps_ref[...]
    rho_ref[...] = rho
    joule_ref[...] = rho * jnp.mean(amps * amps, axis=0, keepdims=True)


def row_features(rows):
    high, low = rows[0:3], rows[3:6]
    zero = jnp.zeros_like(rows[0:1])
    one = jnp.ones_like(zero)
    first = [-2 * high, -2 * high, one, one, one] + [zero] * 6 + [rows[6:7]]
    second = [-2 * low, -2 * low] + [zero] * 9 + [rows[7:8]]
    third = [zero] * 15 + [rows[8:9]]
    return jnp.concatenate(first + second + third, axis=0).T


def flux_body(has_acc, finish, row0, cols_ref, a_ref, *refs):
    acc_ref = s_ref = krylov_ref = None
    if has_acc:
        acc_ref, refs = refs[0], refs[1:]
    if finish:
        s_ref, krylov_ref, refs = refs[0], refs[1], refs[2:]
    out_ref, b_scr, w_scr = refs[:3]
    total = refs[3] if finish else out_ref
    step, group = pl.program_id(0), pl.program_id(1)
    width = cols_ref.shape[2]
    span = b_scr.shape[1]
    chunks = span // width
    base = pl.multiple_of(group * ROW_GROUP, ROW_GROUP)

    @pl.when(group == 0)
    def _():
        for y in range(chunks):
            at = slice(y * width, (y + 1) * width)
            geo = cols_ref[step * chunks + y, 0:16, :]
            b_scr[0:16, at] = geo
            b_scr[16:32, at] = geo
            b_scr[32:48, at] = geo
            wide = geo.astype(F32)
            wire = cols_ref[step * chunks + y, 16:32, :].astype(F32)
            for c in range(3):
                seg = wide[9 + c : 10 + c] + wide[12 + c : 13 + c]
                w_scr[16 * c : 16 * (c + 1), at] = (wire * seg).astype(BF16)

    @pl.when(step == 0)
    def _():
        here = pl.ds(base, ROW_GROUP)
        if has_acc:
            total[here, :] = acc_ref[pl.ds(pl.multiple_of(row0 + base, ROW_GROUP), ROW_GROUP), :]
        else:
            total[here, :] = jnp.zeros((ROW_GROUP, total.shape[1]), F32)

    for k in range(ROW_GROUP // ROW_TILE):
        here = pl.ds(pl.multiple_of(base + k * ROW_TILE, ROW_TILE), ROW_TILE)
        there = pl.ds(pl.multiple_of(row0 + base + k * ROW_TILE, ROW_TILE), ROW_TILE)
        a = a_ref[there, :]
        sums = None
        for j in range(span // COL_TILE):
            at = slice(j * COL_TILE, (j + 1) * COL_TILE)
            r2 = jnp.dot(a, b_scr[:, at], preferred_element_type=F32)
            tile = lax.rsqrt(r2).astype(BF16)
            part = lax.dot_general(tile, w_scr[:, at], NT, preferred_element_type=F32)
            sums = part if sums is None else sums + part
        total[here, :] += sums

    if finish:

        @pl.when(step == pl.num_programs(0) - 1)
        def _():
            for k in range(ROW_GROUP // width):
                here = pl.ds(pl.multiple_of(base + k * width, width), width)
                turned = total[here, :].T
                block = group * (ROW_GROUP // width) + k
                seg = s_ref[row0 // width + block]
                out_ref[block, 0:16, :] = (
                    turned[0:16] * seg[0:1] + turned[16:32] * seg[1:2] + turned[32:48] * seg[2:3]
                )

        @pl.when((step == 0) & (group == 0))
        def _():
            krylov = krylov_ref[...]
            kk_scr = refs[4]
            kk_scr[...] = lax.dot_general(
                krylov, krylov, NT, precision=HI, preferred_element_type=F32
            )
            me = lax.axis_index("row")
            for n in range(out_ref.shape[0]):
                shift, swap = BLOCKS[row0 // width + n]
                owner = (me // 2 + 4 - shift) % 4 * 2 + (me + swap) % 2
                out_ref[n, 16:24, :] = jnp.zeros((8, width), F32)
                out_ref[n, 16:24, 0:64] = kk_scr[pl.ds(pl.multiple_of(owner * 8, 8), 8), :]


def flux_call(cols, a, acc=None, seg=None, krylov=None, row0=0, rows=None):
    rows = a.shape[0] if rows is None else rows
    chunks, _, width = cols.shape
    finish = seg is not None
    whole = pl.BlockSpec(memory_space=pltpu.VMEM)
    args = [cols, a]
    if acc is not None:
        args.append(acc)
    if finish:
        args += [seg, krylov]
        shape = jax.ShapeDtypeStruct((rows // width, SECTIONS + 8, width), F32)
    else:
        shape = jax.ShapeDtypeStruct((rows, 3 * SECTIONS), F32)
    scratch = [pltpu.VMEM((48, COL_STEP), BF16), pltpu.VMEM((48, COL_STEP), BF16)]
    if finish:
        scratch += [pltpu.VMEM((rows, 3 * SECTIONS), F32), pltpu.VMEM((64, 64), F32)]
    pairs = rows * chunks * width
    return pl.pallas_call(
        functools.partial(flux_body, acc is not None, finish, row0),
        grid=(chunks * width // COL_STEP, rows // ROW_GROUP),
        in_specs=[whole] * len(args),
        out_specs=whole,
        out_shape=shape,
        scratch_shapes=scratch,
        compiler_params=pltpu.CompilerParams(vmem_limit_bytes=40 * 2**20),
        cost_estimate=pl.CostEstimate(
            flops=pairs * 2 * 512, bytes_accessed=4 * rows * 128, transcendentals=pairs
        ),
        name="flux",
    )(*args)


def image_body(sent1, sent3, sent2, mine_ref, swap_ref, rho_ref, amps_ref, krylov_ref, image_ref, stats_ref):
    flux = (sent1[0] + sent3[0] + sent2[0] + mine_ref[1]) + swap_ref[...]
    image = rho_ref[...] * amps_ref[...] + flux[0:16]
    image_ref[...] = image
    kk = flux[16:24, 0:64]
    dot = functools.partial(
        lax.dot_general, dimension_numbers=NT, precision=HI, preferred_element_type=F32
    )
    parts = [
        dot(image, krylov_ref[...]),
        dot(image, image),
        jnp.concatenate([kk[:, 0:32], kk[:, 32:64]], axis=0),
        jnp.zeros((SECTIONS, 16), F32),
    ]
    stats = jnp.concatenate(parts, axis=1)
    for n in range(stats_ref.shape[0]):
        stats_ref[n] = stats


def end_body(krylov_ref, image_ref, stats_ref, q_ref, hess_ref, chol_ref, kk_scr):
    dot = functools.partial(lax.dot_general, precision=HI, preferred_element_type=F32)
    nn = (((1,), (0,)), ((), ()))
    stats = stats_ref[0]
    for n in range(1, stats_ref.shape[0]):
        stats = stats + stats_ref[n]
    for n in range(stats_ref.shape[0]):
        kk_scr[8 * n : 8 * n + 8, 0:32] = stats_ref[n, 0:8, 80:112]
        kk_scr[8 * n : 8 * n + 8, 32:64] = stats_ref[n, 8:16, 80:112]
    turned = stats[:, 0:64]
    hess_ref[...] = turned
    kh = dot(turned, kk_scr[...], nn)
    gram = stats[:, 64:80] + dot(kh - 2.0 * turned, turned, NT)
    resid = image_ref[...] - dot(turned, krylov_ref[...], nn)
    row = lax.broadcasted_iota(jnp.int32, gram.shape, 0)
    col = lax.broadcasted_iota(jnp.int32, gram.shape, 1)
    tall = lax.broadcasted_iota(jnp.int32, resid.shape, 0)
    chol = jnp.zeros_like(gram)
    for j in range(SECTIONS):
        root = jnp.sqrt(gram[j : j + 1, j : j + 1])
        column = gram[:, j : j + 1] / root
        across = gram[j : j + 1, :] / root
        column = jnp.where(row[:, 0:1] >= j, column, 0.0)
        chol = jnp.where(col == j, column, chol)
        solved = resid[j : j + 1, :] / root
        gram = gram - column * across
        resid = jnp.where(tall == j, solved, resid - jnp.where(tall > j, column * solved, 0.0))
    q_ref[...] = resid
    chol_ref[...] = chol


def end_call(krylov, image, stats):
    whole = pl.BlockSpec(memory_space=pltpu.VMEM)
    return pl.pallas_call(
        end_body,
        in_specs=[whole] * 3,
        out_specs=[whole] * 3,
        out_shape=[
            jax.ShapeDtypeStruct(image.shape, F32),
            jax.ShapeDtypeStruct((SECTIONS, krylov.shape[0]), F32),
            jax.ShapeDtypeStruct((SECTIONS, SECTIONS), F32),
        ],
        scratch_shapes=[pltpu.VMEM((64, 64), F32)],
        compiler_params=pltpu.CompilerParams(vmem_limit_bytes=16 * 2**20),
        name="finish",
    )(krylov, image, stats)


def core_swap(value):
    return lax.ppermute(value, "row", [(i, i ^ 1) for i in range(8)])


def shift_x(value, k):
    return lax.ppermute(value, "row", [(i, (i + 2 * k) % 8) for i in range(8)])


def shift_y(value, k):
    return lax.ppermute(value, "col", [(i, (i + 8 * k) % 32) for i in range(32)])


def swap_z(value, k):
    return lax.ppermute(value, "col", [(i, i ^ k) for i in range(32)])


def local(
    strand_layout,
    strand_amperes_panel,
    krylov_vectors,
    strand_kelvin,
    strand_ohmic_value,
    strand_warmer_slot,
    warmer_kelvin_gain,
    strand_region_slot,
    region_threshold_kelvin,
):
    width = strand_kelvin.shape[0]
    own = small_call(
        payload_body, (strand_layout, strand_amperes_panel), [((32, width), BF16)], "payload"
    )[0]
    pair = jnp.stack([own, core_swap(own)])
    others = [shift_x(pair, k) for k in (1, 3, 2)]
    column = jnp.stack([own] + [shift_y(own, k) for k in (1, 3, 2)])

    rows = jnp.concatenate(others + [pair[::-1]], axis=0)
    seg = rows[:, 9:12].astype(F32) + rows[:, 12:15].astype(F32)
    seg = jnp.concatenate([seg, jnp.zeros((8, 5, seg.shape[2]), F32)], axis=1)
    a = row_features(rows.transpose(1, 0, 2).reshape(32, -1))

    far = swap_z(column, 4)
    acc = flux_call(column, a)
    column = jnp.concatenate([column, far], axis=0)
    middle = swap_z(column, 2)
    acc = flux_call(far, a, acc)
    column = jnp.concatenate([column, middle], axis=0)
    near = swap_z(column, 1)
    acc = flux_call(middle, a, acc)
    away = flux_call(near, a, acc, seg, krylov_vectors, 0, 3072)
    sent = [shift_x(away[2 * n : 2 * n + 2], -k) for n, k in enumerate((1, 3, 2))]
    mine = flux_call(near, a, acc, seg, krylov_vectors, 3072, 1024)
    swapped = core_swap(sent[0][1] + sent[1][1] + sent[2][1] + mine[0])

    flat = (strand_kelvin, strand_ohmic_value, strand_warmer_slot, strand_region_slot)
    rho, joule = small_call(
        heat_body,
        (*(v[None] for v in flat), strand_amperes_panel, warmer_kelvin_gain, region_threshold_kelvin),
        [((1, width), F32)] * 2,
        "heat",
        2,
    )
    image, stats = small_call(
        image_body,
        (*sent, mine, swapped, rho, strand_amperes_panel, krylov_vectors),
        [((SECTIONS, width), F32), ((32, SECTIONS, 128), F32)],
        "image",
    )
    stats = jnp.sum(lax.all_to_all(stats, "col", 0, 0), axis=0)
    stats = lax.all_to_all(jnp.broadcast_to(stats[None], (8, *stats.shape)), "row", 0, 0)
    q_next, hess, chol = end_call(krylov_vectors, image, stats)
    return (q_next, hess.T, chol, joule[0])


def solution(mesh):
    return jax.shard_map(
        local,
        mesh=mesh,
        in_specs=(
            P(None, ("row", "col")),
            P(None, ("row", "col")),
            P(None, ("row", "col")),
            P(("row", "col")),
            P(("row", "col")),
            P(("row", "col")),
            P(),
            P(("row", "col")),
            P(),
        ),
        out_specs=(P(None, ("row", "col")), P(), P(), P(("row", "col"))),
        check_vma=False,
    )
```

time: 559 us -> 140 us (0.25)
  blocking collectives: 227 us -> 28.1 us
  matrix products: 162 us -> 0 us
  waiting for transfers between devices: 145 us -> 0.54 us
  Pallas kernels: 0 us -> 80.6 us
  starting transfers between devices: 0.04 us -> 25.6 us
  between operations: 14.1 us -> 1.03 us
  other arithmetic: 6.86 us -> 0.2 us
    dot_general x19 -> x0, matrix products: 161 us -> none  [the longest x16 159 us: one_block(): jnp.einsum('kc,rc->kr', cols_vec, tile, preferred_element_type=jnp.float32)]
    psum x2 -> x0, blocking collectives: 149 us -> none  [the longest x1 75.4 us: local(): hess = lax.psum(local_proj, ('row', 'col'))]
    psum x1 -> x0, waiting for transfers between devices: 145 us -> none  [local(): totals = lax.psum(partial_flux, 'col')]
    pallas_call x0 -> x9, Pallas kernels: none -> 80.6 us  [the longest x5 76.5 us: flux_call(): pl.pallas_call(functools.partial(flux_body, acc is not None, finish, row0...]
    all_gather x3 -> x0, blocking collectives: 78 us -> none  [the longest x1 51.9 us: local(): rows_geom = lax.all_gather(strand_layout, 'col', axis=1, tiled=True)]
    all_to_all x0 -> x2, blocking collectives: none -> 28.1 us  [the longest x1 19 us: local(): stats = jnp.sum(lax.all_to_all(stats, 'col', 0, 0), axis=0)]
    ppermute x0 -> x14, starting transfers between devices: none -> 25.6 us  [the longest x3 11.1 us: swap_z(): return lax.ppermute(value, 'col', [(i, i ^ k) for i in range(32)])]
  transfers between devices with their start and end apart: 1 -> 14, of which waited for: 1 -> 1; matrix products, arithmetic and copies ran while one was open for 0% -> 1% of each run, Pallas kernels for 0% -> 35%
where the time goes in v1:
time: 140 us; the launch traced here: 139 us
  Pallas kernels  80.6 us (58%)
  blocking collectives  28.1 us (20%)
  starting transfers between devices  25.6 us (18%)
  local copies, waits for them, and re-layouts  2.91 us (2%)
    pallas_call x5, Pallas kernels, flux_call(): pl.pallas_call(functools.partial(flux_body, acc is not None, finish, row0...  76.5 us
    all_to_all x1, blocking collectives, local(): stats = jnp.sum(lax.all_to_all(stats, 'col', 0, 0), axis=0)  19 us
    ppermute x3, starting transfers between devices, swap_z(): return lax.ppermute(value, 'col', [(i, i ^ k) for i in range(32)])  11.1 us
    all_to_all x1, blocking collectives, local(): lax.all_to_all(jnp.broadcast_to(stats[None], (8, *stats.shape)), 'row', 0...  9.07 us
    ppermute x6, starting transfers between devices, shift_x(): return lax.ppermute(value, 'row', [(i, (i + 2 * k) % 8) for i in range(8)])  9.03 us
    ppermute x3, starting transfers between devices, shift_y(): lax.ppermute(value, 'col', [(i, (i + 8 * k) % 32) for i in range(32)])  5.3 us
  transfers between devices with their start and end apart: 14, of which 1 were waited for; matrix products, arithmetic and copies ran while one was open for 1% of the time, Pallas kernels for 35%

profile of v1, /device:TPU:32, one launch (start us, length us, event | category | flops | bytes accessed | tf_op | source)
XLA Modules:
  0.0 138.9 jit_solution(18130117331388777590)
XLA Ops:
  0.6 0.7 copy-done.1
  1.4 0.7 copy-done.3
  2.1 0.1 collective-permute-start.6
  2.2 1.7 %collective-permute-start = (bf16[32,512]{1,0:T(8,128)(2,1)S(1)}, bf16[32,512]{1,0:T(8,128)(2,1)S(1)}, u32[]{:S(2)}, u32[]{:S(2)}) collective-permute-start(bf16[32,512]{1,0:T(8,128)(2,1)S(1)} %payload.1), channel_id=1, source_target_pairs={{0,8},{1,9},{2,10},{3,11},{4,12},{5,13},{6,14},{7,15},{8,16},{9,17... | collective-permute-start | bytes 98312 | tf_op jit(solution)/shard_map/ppermute | solution.py:265
  3.9 1.7 %collective-permute-start.1 = (bf16[32,512]{1,0:T(8,128)(2,1)S(1)}, bf16[32,512]{1,0:T(8,128)(2,1)S(1)}, u32[]{:S(2)}, u32[]{:S(2)}) collective-permute-start(bf16[32,512]{1,0:T(8,128)(2,1)S(1)} %payload.1), channel_id=1, source_target_pairs={{0,24},{1,25},{2,26},{3,27},{4,28},{5,29},{6,30},{7,31},{8,0},{9,1... | collective-permute-start | bytes 98312 | tf_op jit(solution)/shard_map/ppermute | solution.py:265
  5.6 2.0 %collective-permute-start.2 = (bf16[32,512]{1,0:T(8,128)(2,1)S(1)}, bf16[32,512]{1,0:T(8,128)(2,1)S(1)}, u32[]{:S(2)}, u32[]{:S(2)}) collective-permute-start(bf16[32,512]{1,0:T(8,128)(2,1)S(1)} %payload.1), channel_id=1, source_target_pairs={{0,16},{1,17},{2,18},{3,19},{4,20},{5,21},{6,22},{7,23},{8,24},{9,... | collective-permute-start | bytes 98312 | tf_op jit(solution)/shard_map/ppermute | solution.py:265
  7.6 1.6 %collective-permute-start.7 = (bf16[2,32,512]{2,1,0:T(8,128)(2,1)S(1)}, bf16[2,32,512]{2,1,0:T(8,128)(2,1)S(1)}, u32[]{:S(2)}, u32[]{:S(2)}) collective-permute-start(bf16[2,32,512]{2,1,0:T(8,128)(2,1)S(1)} %pad_maximum_fusion.2), channel_id=1, source_target_pairs={{0,64},{32,96},{64,128},{96,160},{128,192},{160,224},{192,0},{224,... | collective-permute-start | bytes 196616 | tf_op jit(solution)/shard_map/ppermute | solution.py:261
  9.1 1.7 %collective-permute-start.8 = (bf16[2,32,512]{2,1,0:T(8,128)(2,1)S(1)}, bf16[2,32,512]{2,1,0:T(8,128)(2,1)S(1)}, u32[]{:S(2)}, u32[]{:S(2)}) collective-permute-start(bf16[2,32,512]{2,1,0:T(8,128)(2,1)S(1)} %pad_maximum_fusion.2), channel_id=1, source_target_pairs={{0,192},{32,224},{64,0},{96,32},{128,64},{160,96},{192,128},{224,1... | collective-permute-start | bytes 196616 | tf_op jit(solution)/shard_map/ppermute | solution.py:261
  10.9 1.8 %collective-permute-start.9 = (bf16[2,32,512]{2,1,0:T(8,128)(2,1)S(1)}, bf16[2,32,512]{2,1,0:T(8,128)(2,1)S(1)}, u32[]{:S(2)}, u32[]{:S(2)}) collective-permute-start(bf16[2,32,512]{2,1,0:T(8,128)(2,1)S(1)} %pad_maximum_fusion.2), channel_id=1, source_target_pairs={{0,128},{32,160},{64,192},{96,224},{128,0},{160,32},{192,64},{224,... | collective-permute-start | bytes 196616 | tf_op jit(solution)/shard_map/ppermute | solution.py:261
  12.7 6.4 %collective-permute-start.3 = (bf16[4,32,512]{2,1,0:T(8,128)(2,1)S(1)}, bf16[4,32,512]{2,1,0:T(8,128)(2,1)S(1)}, u32[]{:S(2)}, u32[]{:S(2)}) collective-permute-start(bf16[4,32,512]{2,1,0:T(8,128)(2,1)S(1)} %pad_maximum_fusion.1.cols_ref), channel_id=1, source_target_pairs={{0,4},{1,5},{2,6},{3,7},{4,0},{5,1},{6,2},{7,3},{8,12},{9,13},{10,... | collective-permute-start | bytes 393224 | tf_op jit(solution)/shard_map/ppermute | solution.py:269
  19.4 0.7 concatenate.36
  20.1 0.5 copy.23
  20.6 9.5 %flux.5.refs_0_ = f32[4096,48]{1,0:T(8,128)S(1)} custom-call(bf16[4,32,512]{2,1,0:T(8,128)(2,1)S(1)} %pad_maximum_fusion.1.cols_ref, bf16[4096,48]{1,0:T(8,128)(2,1)S(1)} %bitcast.29), custom_call_target="tpu_custom_call" | custom-call | flops 8589934592 | bytes 2097152 | tf_op jit(solution)/shard_map/flux/pallas_call | solution.py:174
  30.2 1.6 %collective-permute-start.4 = (bf16[8,32,512]{2,1,0:T(8,128)(2,1)S(1)}, bf16[8,32,512]{2,1,0:T(8,128)(2,1)S(1)}, u32[]{:S(2)}, u32[]{:S(2)}) collective-permute-start(bf16[8,32,512]{2,1,0:T(8,128)(2,1)S(1)} %get-tuple-element.28), channel_id=1, source_target_pairs={{0,2},{1,3},{2,0},{3,1},{4,6},{5,7},{6,4},{7,5},{8,10},{9,11},{10,... | collective-permute-start | bytes 786440 | tf_op jit(solution)/shard_map/ppermute | solution.py:269
  31.8 9.3 %flux.6.refs_0_ = f32[4096,48]{1,0:T(8,128)S(1)} custom-call(bf16[4,32,512]{2,1,0:T(8,128)(2,1)S(1)} %collective-permute-done.3.cols_ref, bf16[4096,48]{1,0:T(8,128)(2,1)S(1)} %bitcast.30, f32[4096,48]{1,0:T(8,128)S(1)} %flux.5.refs_0_), custom_call_target="tpu_custom_call" | custom-call | flops 8589934592 | bytes 2097152 | tf_op jit(solution)/shard_map/flux/pallas_call | solution.py:174
  41.1 0.5 collective-permute-done.4.cols_ref
  41.6 0.0 copy-start
  41.6 3.2 %collective-permute-start.5 = (bf16[16,32,512]{2,1,0:T(8,128)(2,1)S(1)}, bf16[16,32,512]{2,1,0:T(8,128)(2,1)S(1)}, u32[]{:S(2)}, u32[]{:S(2)}) collective-permute-start(bf16[16,32,512]{2,1,0:T(8,128)(2,1)S(1)} %constant_dynamic-update-slice_fusion.5), channel_id=1, source_target_pairs={{0,1},{1,0},{2,3},{3,2},{4,5},{5,4},{6,7},{7,6},{8,9},{9,8},{10,11... | collective-permute-start | bytes 1572872 | tf_op jit(solution)/shard_map/ppermute | solution.py:269
  44.8 18.8 %flux.7.refs_0_ = f32[4096,48]{1,0:T(8,128)S(1)} custom-call(bf16[8,32,512]{2,1,0:T(8,128)(2,1)S(1)} %collective-permute-done.4.cols_ref, bf16[4096,48]{1,0:T(8,128)(2,1)S(1)} %bitcast.31, f32[4096,48]{1,0:T(8,128)S(1)} %flux.6.refs_0_), custom_call_target="tpu_custom_call" | custom-call | flops 17179869184 | bytes 2097152 | tf_op jit(solution)/shard_map/flux/pallas_call | solution.py:174
  63.6 29.0 %flux.8 = f32[6,24,512]{2,1,0:T(8,128)S(1)} custom-call(bf16[16,32,512]{2,1,0:T(8,128)(2,1)S(1)} %collective-permute-done.5.cols_ref, bf16[4096,48]{1,0:T(8,128)(2,1)S(1)} %bitcast.32, f32[4096,48]{1,0:T(8,128)S(1)} %flux.7.refs_0_, f32[8,8,512]{2,1,0:T(8,128)S(1)} %concatenate.37.refs_1_, f32[64,512]{1,0:T(8,128)S(1)} %copy-done), custom_call_target="tpu_custom_call" | custom-call | flops 25769803776 | bytes 1572864 | tf_op jit(solution)/shard_map/flux/pallas_call | solution.py:174
  92.7 1.2 collective-permute-start.10
  93.9 0.9 collective-permute-start.11
  94.8 0.0 copy-start.7
  94.8 0.0 copy-start.8
  94.8 1.8 %collective-permute-start.12 = (f32[2,24,512]{2,1,0:T(8,128)S(1)}, f32[2,24,512]{2,1,0:T(8,128)S(1)}, u32[]{:S(2)}, u32[]{:S(2)}) collective-permute-start(f32[2,24,512]{2,1,0:T(8,128)S(1)} %get-tuple-element.18), channel_id=1, source_target_pairs={{0,128},{32,160},{64,192},{96,224},{128,0},{160,32},{192,64},{224,... | collective-permute-start | bytes 294920 | tf_op jit(solution)/shard_map/ppermute | solution.py:261
  96.6 9.9 %flux.9.mine_ref = f32[2,24,512]{2,1,0:T(8,128)S(1)} custom-call(bf16[16,32,512]{2,1,0:T(8,128)(2,1)S(1)} %collective-permute-done.5.cols_ref, bf16[4096,48]{1,0:T(8,128)(2,1)S(1)} %bitcast.33, f32[4096,48]{1,0:T(8,128)S(1)} %flux.7.refs_0_, f32[8,8,512]{2,1,0:T(8,128)S(1)} %concatenate.37.refs_1_, f32[64,512]{1,0:T(8,128)S(1)} %copy-done), custom_call_target="tpu_custom_call" | custom-call | flops 8589934592 | bytes 524288 | tf_op jit(solution)/shard_map/flux/pallas_call | solution.py:174
  106.6 0.1 collective-permute-start.13
  106.8 1.2 heat.1
  107.9 0.4 image.1
  108.3 19.0 %all_to_all.10 = f32[32,16,128]{2,1,0:T(8,128)S(1)} all-to-all(f32[32,16,128]{2,1,0:T(8,128)S(1)} %get-tuple-element.13), channel_id=1, replica_groups=mesh['row'=8,'col'=32] {'col'}, dimensions={0} | all-to-all | bytes 524288 | tf_op jit(solution)/shard_map/all_to_all | solution.py:323
  127.4 9.1 %all_to_all.11.stats_ref = f32[8,16,128]{2,1,0:T(8,128)S(1)} all-to-all(f32[8,16,128]{2,1,0:T(8,128)S(1)} %broadcast_in_dim.23), channel_id=1, replica_groups=mesh['row'=8,'col'=32] {'row'}, dimensions={0} | all-to-all | bytes 131072 | tf_op jit(solution)/shard_map/all_to_all | solution.py:324
  136.4 2.5 %finish.1 = (f32[16,512]{1,0:T(8,128)}, f32[16,64]{1,0:T(8,128)}, f32[16,16]{1,0:T(8,128)}) custom-call(f32[64,512]{1,0:T(8,128)S(1)} %copy-done, f32[16,512]{1,0:T(8,128)S(1)} %get-tuple-element.12.image_ref, f32[8,16,128]{2,1,0:T(8,128)S(1)} %all_to_all.11.stats_ref), custom_call_target="tpu_custom_call" | custom-call | tf_op jit(solution)/shard_map/finish/pallas_call | solution.py:241
  (51 shorter events, 0.5 us)
Async XLA Ops:
  0.6 0.8 copy-start.1
  1.4 0.7 copy-start.3
  2.1 5.4 %collective-permute-start.6 = (bf16[32,512]{1,0:T(8,128)(2,1)S(1)}, bf16[32,512]{1,0:T(8,128)(2,1)S(1)}, u32[]{:S(2)}, u32[]{:S(2)}) collective-permute-start(bf16[32,512]{1,0:T(8,128)(2,1)S(1)} %payload.1), channel_id=1, source_target_pairs={{0,32},{32,0},{64,96},{96,64},{128,160},{160,128},{192,224},{224,1... | collective-permute-start | bytes 98312 | tf_op jit(solution)/shard_map/ppermute | solution.py:257
  2.2 8.6 %collective-permute-start = (bf16[32,512]{1,0:T(8,128)(2,1)S(1)}, bf16[32,512]{1,0:T(8,128)(2,1)S(1)}, u32[]{:S(2)}, u32[]{:S(2)}) collective-permute-start(bf16[32,512]{1,0:T(8,128)(2,1)S(1)} %payload.1), channel_id=1, source_target_pairs={{0,8},{1,9},{2,10},{3,11},{4,12},{5,13},{6,14},{7,15},{8,16},{9,17... | collective-permute-start | bytes 98312 | tf_op jit(solution)/shard_map/ppermute | solution.py:265
  3.9 8.8 %collective-permute-start.1 = (bf16[32,512]{1,0:T(8,128)(2,1)S(1)}, bf16[32,512]{1,0:T(8,128)(2,1)S(1)}, u32[]{:S(2)}, u32[]{:S(2)}) collective-permute-start(bf16[32,512]{1,0:T(8,128)(2,1)S(1)} %payload.1), channel_id=1, source_target_pairs={{0,24},{1,25},{2,26},{3,27},{4,28},{5,29},{6,30},{7,31},{8,0},{9,1... | collective-permute-start | bytes 98312 | tf_op jit(solution)/shard_map/ppermute | solution.py:265
  5.6 7.2 %collective-permute-start.2 = (bf16[32,512]{1,0:T(8,128)(2,1)S(1)}, bf16[32,512]{1,0:T(8,128)(2,1)S(1)}, u32[]{:S(2)}, u32[]{:S(2)}) collective-permute-start(bf16[32,512]{1,0:T(8,128)(2,1)S(1)} %payload.1), channel_id=1, source_target_pairs={{0,16},{1,17},{2,18},{3,19},{4,20},{5,21},{6,22},{7,23},{8,24},{9,... | collective-permute-start | bytes 98312 | tf_op jit(solution)/shard_map/ppermute | solution.py:265
  7.6 11.6 %collective-permute-start.7 = (bf16[2,32,512]{2,1,0:T(8,128)(2,1)S(1)}, bf16[2,32,512]{2,1,0:T(8,128)(2,1)S(1)}, u32[]{:S(2)}, u32[]{:S(2)}) collective-permute-start(bf16[2,32,512]{2,1,0:T(8,128)(2,1)S(1)} %pad_maximum_fusion.2), channel_id=1, source_target_pairs={{0,64},{32,96},{64,128},{96,160},{128,192},{160,224},{192,0},{224,... | collective-permute-start | bytes 196616 | tf_op jit(solution)/shard_map/ppermute | solution.py:261
  9.1 10.0 %collective-permute-start.8 = (bf16[2,32,512]{2,1,0:T(8,128)(2,1)S(1)}, bf16[2,32,512]{2,1,0:T(8,128)(2,1)S(1)}, u32[]{:S(2)}, u32[]{:S(2)}) collective-permute-start(bf16[2,32,512]{2,1,0:T(8,128)(2,1)S(1)} %pad_maximum_fusion.2), channel_id=1, source_target_pairs={{0,192},{32,224},{64,0},{96,32},{128,64},{160,96},{192,128},{224,1... | collective-permute-start | bytes 196616 | tf_op jit(solution)/shard_map/ppermute | solution.py:261
  10.9 8.3 %collective-permute-start.9 = (bf16[2,32,512]{2,1,0:T(8,128)(2,1)S(1)}, bf16[2,32,512]{2,1,0:T(8,128)(2,1)S(1)}, u32[]{:S(2)}, u32[]{:S(2)}) collective-permute-start(bf16[2,32,512]{2,1,0:T(8,128)(2,1)S(1)} %pad_maximum_fusion.2), channel_id=1, source_target_pairs={{0,128},{32,160},{64,192},{96,224},{128,0},{160,32},{192,64},{224,... | collective-permute-start | bytes 196616 | tf_op jit(solution)/shard_map/ppermute | solution.py:261
  12.7 17.5 %collective-permute-start.3 = (bf16[4,32,512]{2,1,0:T(8,128)(2,1)S(1)}, bf16[4,32,512]{2,1,0:T(8,128)(2,1)S(1)}, u32[]{:S(2)}, u32[]{:S(2)}) collective-permute-start(bf16[4,32,512]{2,1,0:T(8,128)(2,1)S(1)} %pad_maximum_fusion.1.cols_ref), channel_id=1, source_target_pairs={{0,4},{1,5},{2,6},{3,7},{4,0},{5,1},{6,2},{7,3},{8,12},{9,13},{10,... | collective-permute-start | bytes 393224 | tf_op jit(solution)/shard_map/ppermute | solution.py:269
  30.2 11.4 %collective-permute-start.4 = (bf16[8,32,512]{2,1,0:T(8,128)(2,1)S(1)}, bf16[8,32,512]{2,1,0:T(8,128)(2,1)S(1)}, u32[]{:S(2)}, u32[]{:S(2)}) collective-permute-start(bf16[8,32,512]{2,1,0:T(8,128)(2,1)S(1)} %get-tuple-element.28), channel_id=1, source_target_pairs={{0,2},{1,3},{2,0},{3,1},{4,6},{5,7},{6,4},{7,5},{8,10},{9,11},{10,... | collective-permute-start | bytes 786440 | tf_op jit(solution)/shard_map/ppermute | solution.py:269
  41.6 22.0 %copy-start = (f32[64,512]{1,0:T(8,128)S(1)}, f32[64,512]{1,0:T(8,128)}, u32[]{:S(2)}) copy-start(f32[64,512]{1,0:T(8,128)} %krylov_ref.3) | copy-start | bytes 393220
  41.6 22.0 %collective-permute-start.5 = (bf16[16,32,512]{2,1,0:T(8,128)(2,1)S(1)}, bf16[16,32,512]{2,1,0:T(8,128)(2,1)S(1)}, u32[]{:S(2)}, u32[]{:S(2)}) collective-permute-start(bf16[16,32,512]{2,1,0:T(8,128)(2,1)S(1)} %constant_dynamic-update-slice_fusion.5), channel_id=1, source_target_pairs={{0,1},{1,0},{2,3},{3,2},{4,5},{5,4},{6,7},{7,6},{8,9},{9,8},{10,11... | collective-permute-start | bytes 1572872 | tf_op jit(solution)/shard_map/ppermute | solution.py:269
  92.7 13.9 %collective-permute-start.10 = (f32[2,24,512]{2,1,0:T(8,128)S(1)}, f32[2,24,512]{2,1,0:T(8,128)S(1)}, u32[]{:S(2)}, u32[]{:S(2)}) collective-permute-start(f32[2,24,512]{2,1,0:T(8,128)S(1)} %get-tuple-element.20), channel_id=1, source_target_pairs={{0,192},{32,224},{64,0},{96,32},{128,64},{160,96},{192,128},{224,1... | collective-permute-start | bytes 294920 | tf_op jit(solution)/shard_map/ppermute | solution.py:261
  93.9 12.7 %collective-permute-start.11 = (f32[2,24,512]{2,1,0:T(8,128)S(1)}, f32[2,24,512]{2,1,0:T(8,128)S(1)}, u32[]{:S(2)}, u32[]{:S(2)}) collective-permute-start(f32[2,24,512]{2,1,0:T(8,128)S(1)} %get-tuple-element.19), channel_id=1, source_target_pairs={{0,64},{32,96},{64,128},{96,160},{128,192},{160,224},{192,0},{224,... | collective-permute-start | bytes 294920 | tf_op jit(solution)/shard_map/ppermute | solution.py:261
  94.8 11.9 %copy-start.2 = (f32[16,512]{1,0:T(8,128)S(1)}, f32[16,512]{1,0:T(8,128)}, u32[]{:S(2)}) copy-start(f32[16,512]{1,0:T(8,128)} %amps_ref.5) | copy-start | bytes 98308
  94.8 11.9 %copy-start.4 = (f32[512]{0:T(512)S(1)}, f32[512]{0:T(512)}, u32[]{:S(2)}) copy-start(f32[512]{0:T(512)} %param.12) | copy-start | bytes 6148
  94.8 11.9 %copy-start.5 = (f32[512]{0:T(512)S(1)}, f32[512]{0:T(512)}, u32[]{:S(2)}) copy-start(f32[512]{0:T(512)} %param.13) | copy-start | bytes 6148
  94.8 11.9 %copy-start.6 = (s32[512]{0:T(512)S(1)}, s32[512]{0:T(512)}, u32[]{:S(2)}) copy-start(s32[512]{0:T(512)} %param.14) | copy-start | bytes 6148
  94.8 11.9 %copy-start.7 = (s32[512]{0:T(512)S(1)}, s32[512]{0:T(512)}, u32[]{:S(2)}) copy-start(s32[512]{0:T(512)} %param.16) | copy-start | bytes 6148
  94.8 11.9 %copy-start.8 = (f32[8]{0:T(128)S(1)}, f32[8]{0:T(128)}, u32[]{:S(2)}) copy-start(f32[8]{0:T(128)} %gain_ref.1) | copy-start | bytes 100
  94.8 11.9 %copy-start.9 = (f32[32]{0:T(128)S(1)}, f32[32]{0:T(128)}, u32[]{:S(2)}) copy-start(f32[32]{0:T(128)} %limit_ref.1) | copy-start | bytes 388
  94.8 11.7 %collective-permute-start.12 = (f32[2,24,512]{2,1,0:T(8,128)S(1)}, f32[2,24,512]{2,1,0:T(8,128)S(1)}, u32[]{:S(2)}, u32[]{:S(2)}) collective-permute-start(f32[2,24,512]{2,1,0:T(8,128)S(1)} %get-tuple-element.18), channel_id=1, source_target_pairs={{0,128},{32,160},{64,192},{96,224},{128,0},{160,32},{192,64},{224,... | collective-permute-start | bytes 294920 | tf_op jit(solution)/shard_map/ppermute | solution.py:261
  106.6 1.3 collective-permute-start.13

commit v2 on v1

--- a/solution.py
+++ b/solution.py
@@ -12,10 +12,18 @@
 BF16 = jnp.bfloat16
 NT = (((1,), (1,)), ((), ()))
 SECTIONS = 16
-ROW_GROUP = 1024
 ROW_TILE = 256
 COL_TILE = 1024
-COL_STEP = 2048
+CORE_Z = [
+    [(2 * x + c) * 32 + 8 * y + z for c in range(2) for z in range(8)]
+    for x in range(4)
+    for y in range(4)
+]
+X_Y = [
+    [(2 * x + c) * 32 + 8 * y + z for x in range(4) for y in range(4)]
+    for c in range(2)
+    for z in range(8)
+]
 BLOCKS = ((1, 0), (1, 1), (3, 0), (3, 1), (2, 0), (2, 1), (0, 1), (0, 0))
 
 
@@ -52,7 +60,7 @@
     out_ref[16:32, :] = amps_ref[...].astype(BF16)
 
 
-def heat_body(kelvin_ref, ohmic_ref, warmer_ref, region_ref, amps_ref, gain_ref, limit_ref, rho_ref, joule_ref):
+def heat(kelvin_ref, ohmic_ref, warmer_ref, region_ref, amps_ref, gain_ref, limit_ref, rho_ref, joule_ref):
     def entries(ids, table_ref):
         out = jnp.zeros(ids.shape, F32)
         for level in range(table_ref.shape[0]):
@@ -77,19 +85,26 @@
     return jnp.concatenate(first + second + third, axis=0).T
 
 
-def flux_body(has_acc, finish, row0, cols_ref, a_ref, *refs):
+def flux_body(kind, row0, group_rows, cols_ref, a_ref, *refs):
+    finish = kind in ("away", "mine")
     acc_ref = s_ref = krylov_ref = None
-    if has_acc:
+    heat_in = heat_out = ()
+    if kind != "first":
         acc_ref, refs = refs[0], refs[1:]
     if finish:
         s_ref, krylov_ref, refs = refs[0], refs[1], refs[2:]
-    out_ref, b_scr, w_scr = refs[:3]
-    total = refs[3] if finish else out_ref
+    if kind == "mine":
+        heat_in, refs = refs[:7], refs[7:]
+    out_ref, refs = refs[0], refs[1:]
+    if kind == "mine":
+        heat_out, refs = refs[:2], refs[2:]
+    b_scr, w_scr = refs[:2]
+    total = refs[2] if finish else out_ref
     step, group = pl.program_id(0), pl.program_id(1)
     width = cols_ref.shape[2]
     span = b_scr.shape[1]
     chunks = span // width
-    base = pl.multiple_of(group * ROW_GROUP, ROW_GROUP)
+    base = pl.multiple_of(group * group_rows, group_rows)
 
     @pl.when(group == 0)
     def _():
@@ -107,33 +122,40 @@
 
     @pl.when(step == 0)
     def _():
-        here = pl.ds(base, ROW_GROUP)
-        if has_acc:
-            total[here, :] = acc_ref[pl.ds(pl.multiple_of(row0 + base, ROW_GROUP), ROW_GROUP), :]
+        here = pl.ds(base, group_rows)
+        if acc_ref is None:
+            total[here, :] = jnp.zeros((group_rows, total.shape[1]), F32)
         else:
-            total[here, :] = jnp.zeros((ROW_GROUP, total.shape[1]), F32)
-
-    for k in range(ROW_GROUP // ROW_TILE):
-        here = pl.ds(pl.multiple_of(base + k * ROW_TILE, ROW_TILE), ROW_TILE)
-        there = pl.ds(pl.multiple_of(row0 + base + k * ROW_TILE, ROW_TILE), ROW_TILE)
-        a = a_ref[there, :]
-        sums = None
-        for j in range(span // COL_TILE):
-            at = slice(j * COL_TILE, (j + 1) * COL_TILE)
-            r2 = jnp.dot(a, b_scr[:, at], preferred_element_type=F32)
-            tile = lax.rsqrt(r2).astype(BF16)
-            part = lax.dot_general(tile, w_scr[:, at], NT, preferred_element_type=F32)
-            sums = part if sums is None else sums + part
-        total[here, :] += sums
+            total[here, :] = acc_ref[pl.ds(pl.multiple_of(row0 + base, ROW_TILE), group_rows), :]
+
+    def rows_at(k, offset):
+        return pl.ds(pl.multiple_of(offset + base + k * ROW_TILE, ROW_TILE), ROW_TILE)
+
+    def product(tile, at):
+        return lax.dot_general(tile, w_scr[:, at], NT, preferred_element_type=F32)
+
+    tiles = [
+        (k, slice(j, j + COL_TILE))
+        for k in range(group_rows // ROW_TILE)
+        for j in range(0, span, COL_TILE)
+    ]
+    held = None
+    for k, at in tiles:
+        r2 = jnp.dot(a_ref[rows_at(k, row0), :], b_scr[:, at], preferred_element_type=F32)
+        tile = lax.rsqrt(r2).astype(BF16)
+        if held is not None:
+            total[rows_at(held[0], 0), :] += product(*held[1:])
+        held = (k, tile, at)
+    total[rows_at(held[0], 0), :] += product(*held[1:])
 
     if finish:
 
         @pl.when(step == pl.num_programs(0) - 1)
         def _():
-            for k in range(ROW_GROUP // width):
+            for k in range(group_rows // width):
                 here = pl.ds(pl.multiple_of(base + k * width, width), width)
                 turned = total[here, :].T
-                block = group * (ROW_GROUP // width) + k
+                block = group * (group_rows // width) + k
                 seg = s_ref[row0 // width + block]
                 out_ref[block, 0:16, :] = (
                     turned[0:16] * seg[0:1] + turned[16:32] * seg[1:2] + turned[32:48] * seg[2:3]
@@ -142,7 +164,7 @@
         @pl.when((step == 0) & (group == 0))
         def _():
             krylov = krylov_ref[...]
-            kk_scr = refs[4]
+            kk_scr = refs[3]
             kk_scr[...] = lax.dot_general(
                 krylov, krylov, NT, precision=HI, preferred_element_type=F32
             )
@@ -152,31 +174,35 @@
                 owner = (me // 2 + 4 - shift) % 4 * 2 + (me + swap) % 2
                 out_ref[n, 16:24, :] = jnp.zeros((8, width), F32)
                 out_ref[n, 16:24, 0:64] = kk_scr[pl.ds(pl.multiple_of(owner * 8, 8), 8), :]
-
-
-def flux_call(cols, a, acc=None, seg=None, krylov=None, row0=0, rows=None):
-    rows = a.shape[0] if rows is None else rows
+            if heat_in:
+                heat(*heat_in, *heat_out)
+
+
+def flux_call(kind, cols, a, *more, row0=0, rows, group_rows, step_chunks):
     chunks, _, width = cols.shape
-    finish = seg is not None
+    finish = kind in ("away", "mine")
     whole = pl.BlockSpec(memory_space=pltpu.VMEM)
-    args = [cols, a]
-    if acc is not None:
-        args.append(acc)
+    scalar = pl.BlockSpec(memory_space=pltpu.SMEM)
+    args = [cols, a, *more]
+    specs = [whole] * len(args)
     if finish:
-        args += [seg, krylov]
-        shape = jax.ShapeDtypeStruct((rows // width, SECTIONS + 8, width), F32)
+        shapes = [jax.ShapeDtypeStruct((rows // width, SECTIONS + 8, width), F32)]
     else:
-        shape = jax.ShapeDtypeStruct((rows, 3 * SECTIONS), F32)
-    scratch = [pltpu.VMEM((48, COL_STEP), BF16), pltpu.VMEM((48, COL_STEP), BF16)]
+        shapes = [jax.ShapeDtypeStruct((rows, 3 * SECTIONS), F32)]
+    if kind == "mine":
+        specs[-2:] = [scalar] * 2
+        shapes += [jax.ShapeDtypeStruct((1, width), F32)] * 2
+    span = step_chunks * width
+    scratch = [pltpu.VMEM((48, span), BF16), pltpu.VMEM((48, span), BF16)]
     if finish:
         scratch += [pltpu.VMEM((rows, 3 * SECTIONS), F32), pltpu.VMEM((64, 64), F32)]
     pairs = rows * chunks * width
-    return pl.pallas_call(
-        functools.partial(flux_body, acc is not None, finish, row0),
-        grid=(chunks * width // COL_STEP, rows // ROW_GROUP),
-        in_specs=[whole] * len(args),
-        out_specs=whole,
-        out_shape=shape,
+    out = pl.pallas_call(
+        functools.partial(flux_body, kind, row0, group_rows),
+        grid=(chunks // step_chunks, rows // group_rows),
+        in_specs=specs,
+        out_specs=[whole] * len(shapes),
+        out_shape=shapes,
         scratch_shapes=scratch,
         compiler_params=pltpu.CompilerParams(vmem_limit_bytes=40 * 2**20),
         cost_estimate=pl.CostEstimate(
@@ -184,6 +210,7 @@
         ),
         name="flux",
     )(*args)
+    return out if kind == "mine" else out[0]
 
 
 def image_body(sent1, sent3, sent2, mine_ref, swap_ref, rho_ref, amps_ref, krylov_ref, image_ref, stats_ref):
@@ -205,15 +232,36 @@
         stats_ref[n] = stats
 
 
+def middle_body(in_ref, out_ref):
+    halves = []
+    for c in range(2):
+        half = in_ref[8 * c]
+        for z in range(1, 8):
+            half = half + in_ref[8 * c + z]
+        halves.append(half)
+    lane = lax.broadcasted_iota(jnp.int32, halves[0].shape, 1)
+    main = jnp.where(lane < 80, halves[0] + halves[1], halves[0])
+    other = halves[1]
+    parts = [other[0:8, 80:112], other[8:16, 80:112], jnp.zeros((8, 64), F32)]
+    extra = jnp.concatenate(parts, axis=1)
+    for n in range(16):
+        out_ref[n, 0:16, :] = main
+        out_ref[n, 16:24, :] = extra
+
+
 def end_body(krylov_ref, image_ref, stats_ref, q_ref, hess_ref, chol_ref, kk_scr):
     dot = functools.partial(lax.dot_general, precision=HI, preferred_element_type=F32)
     nn = (((1,), (0,)), ((), ()))
-    stats = stats_ref[0]
-    for n in range(1, stats_ref.shape[0]):
-        stats = stats + stats_ref[n]
-    for n in range(stats_ref.shape[0]):
-        kk_scr[8 * n : 8 * n + 8, 0:32] = stats_ref[n, 0:8, 80:112]
-        kk_scr[8 * n : 8 * n + 8, 32:64] = stats_ref[n, 8:16, 80:112]
+    stats = None
+    for x in range(4):
+        part = stats_ref[4 * x]
+        for y in range(1, 4):
+            part = part + stats_ref[4 * x + y]
+        kk_scr[16 * x : 16 * x + 8, 0:32] = part[0:8, 80:112]
+        kk_scr[16 * x : 16 * x + 8, 32:64] = part[8:16, 80:112]
+        kk_scr[16 * x + 8 : 16 * x + 16, :] = part[16:24, 0:64]
+        stats = part if stats is None else stats + part
+    stats = stats[0:16]
     turned = stats[:, 0:64]
     hess_ref[...] = turned
     kh = dot(turned, kk_scr[...], nn)
@@ -224,12 +272,11 @@
     tall = lax.broadcasted_iota(jnp.int32, resid.shape, 0)
     chol = jnp.zeros_like(gram)
     for j in range(SECTIONS):
-        root = jnp.sqrt(gram[j : j + 1, j : j + 1])
-        column = gram[:, j : j + 1] / root
-        across = gram[j : j + 1, :] / root
-        column = jnp.where(row[:, 0:1] >= j, column, 0.0)
+        scale = 1.0 / jnp.sqrt(gram[j : j + 1, j : j + 1])
+        column = jnp.where(row[:, 0:1] >= j, gram[:, j : j + 1] * scale, 0.0)
+        across = gram[j : j + 1, :] * scale
         chol = jnp.where(col == j, column, chol)
-        solved = resid[j : j + 1, :] / root
+        solved = resid[j : j + 1, :] * scale
         gram = gram - column * across
         resid = jnp.where(tall == j, solved, resid - jnp.where(tall > j, column * solved, 0.0))
     q_ref[...] = resid
@@ -293,35 +340,36 @@
     seg = jnp.concatenate([seg, jnp.zeros((8, 5, seg.shape[2]), F32)], axis=1)
     a = row_features(rows.transpose(1, 0, 2).reshape(32, -1))
 
+    count = a.shape[0]
     far = swap_z(column, 4)
-    acc = flux_call(column, a)
-    column = jnp.concatenate([column, far], axis=0)
-    middle = swap_z(column, 2)
-    acc = flux_call(far, a, acc)
-    column = jnp.concatenate([column, middle], axis=0)
-    near = swap_z(column, 1)
-    acc = flux_call(middle, a, acc)
-    away = flux_call(near, a, acc, seg, krylov_vectors, 0, 3072)
+    acc = flux_call("first", column[:2], a, rows=count, group_rows=2048, step_chunks=2)
+    whole = jnp.concatenate([column, far], axis=0)
+    middle = swap_z(whole, 2)
+    acc = flux_call("next", whole[2:], a, acc, rows=count, group_rows=1024, step_chunks=6)
+    whole = jnp.concatenate([whole, middle], axis=0)
+    near = swap_z(whole, 1)
+    acc = flux_call("next", middle, a, acc, rows=count, group_rows=1024, step_chunks=8)
+    away = flux_call(
+        "away", near, a, acc, seg, krylov_vectors, rows=3072, group_rows=1024, step_chunks=8
+    )
     sent = [shift_x(away[2 * n : 2 * n + 2], -k) for n, k in enumerate((1, 3, 2))]
-    mine = flux_call(near, a, acc, seg, krylov_vectors, 3072, 1024)
+    flat = (strand_kelvin, strand_ohmic_value, strand_warmer_slot, strand_region_slot)
+    mine, rho, joule = flux_call(
+        "mine", near, a, acc, seg, krylov_vectors, *(v[None] for v in flat), strand_amperes_panel,
+        warmer_kelvin_gain, region_threshold_kelvin,
+        row0=3072, rows=1024, group_rows=1024, step_chunks=8,
+    )
     swapped = core_swap(sent[0][1] + sent[1][1] + sent[2][1] + mine[0])
 
-    flat = (strand_kelvin, strand_ohmic_value, strand_warmer_slot, strand_region_slot)
-    rho, joule = small_call(
-        heat_body,
-        (*(v[None] for v in flat), strand_amperes_panel, warmer_kelvin_gain, region_threshold_kelvin),
-        [((1, width), F32)] * 2,
-        "heat",
-        2,
-    )
     image, stats = small_call(
         image_body,
         (*sent, mine, swapped, rho, strand_amperes_panel, krylov_vectors),
-        [((SECTIONS, width), F32), ((32, SECTIONS, 128), F32)],
+        [((SECTIONS, width), F32), ((16, SECTIONS, 128), F32)],
         "image",
     )
-    stats = jnp.sum(lax.all_to_all(stats, "col", 0, 0), axis=0)
-    stats = lax.all_to_all(jnp.broadcast_to(stats[None], (8, *stats.shape)), "row", 0, 0)
+    stats = lax.all_to_all(stats, ("row", "col"), 0, 0, axis_index_groups=CORE_Z)
+    stats = small_call(middle_body, (stats,), [((16, 24, 128), F32)], "middle")[0]
+    stats = lax.all_to_all(stats, ("row", "col"), 0, 0, axis_index_groups=X_Y)
     q_next, hess, chol = end_call(krylov_vectors, image, stats)
     return (q_next, hess.T, chol, joule[0])
 

time: 140 us -> 135 us (0.964)
  starting transfers between devices: 25.6 us -> 23.6 us
  Pallas kernels: 80.6 us -> 78.8 us
  blocking collectives: 28.1 us -> 26.5 us
    ppermute x3, starting transfers between devices: 11.1 us -> 9.21 us  [swap_z(): return lax.ppermute(value, 'col', [(i, i ^ k) for i in range(32)])]
    all_to_all x2, blocking collectives: 28.1 us -> 26.5 us  [the longest x1 14.5 us: local(): lax.all_to_all(stats, ('row', 'col'), 0, 0, axis_index_groups=CORE_Z)]
where the time goes in v2:
time: 135 us; the launch traced here: 134 us
  Pallas kernels  78.8 us (58%)
  blocking collectives  26.5 us (20%)
  starting transfers between devices  23.6 us (17%)
  local copies, waits for them, and re-layouts  2.92 us (2%)
    pallas_call x5, Pallas kernels, flux_call(): pl.pallas_call(functools.partial(flux_body, kind, row0, group_rows), grid...  75.8 us
    all_to_all x1, blocking collectives, local(): lax.all_to_all(stats, ('row', 'col'), 0, 0, axis_index_groups=CORE_Z)  14.5 us
    all_to_all x1, blocking collectives, local(): stats = lax.all_to_all(stats, ('row', 'col'), 0, 0, axis_index_groups=X_Y)  12 us
    ppermute x3, starting transfers between devices, swap_z(): return lax.ppermute(value, 'col', [(i, i ^ k) for i in range(32)])  9.21 us
    ppermute x6, starting transfers between devices, shift_x(): return lax.ppermute(value, 'row', [(i, (i + 2 * k) % 8) for i in range(8)])  8.94 us
    ppermute x3, starting transfers between devices, shift_y(): lax.ppermute(value, 'col', [(i, (i + 8 * k) % 32) for i in range(32)])  5.3 us
  transfers between devices with their start and end apart: 14, of which 1 were waited for; matrix products, arithmetic and copies ran while one was open for 1% of the time, Pallas kernels for 35%

profile of v2, /device:TPU:32, one launch (start us, length us, event | category | flops | bytes accessed | tf_op | source)
XLA Modules:
  0.0 134.2 jit_solution(5839717849687337271)
XLA Ops:
  0.6 0.7 copy-done.1
  1.4 0.7 copy-done.3
  2.1 1.7 %collective-permute-start = (bf16[32,512]{1,0:T(8,128)(2,1)S(1)}, bf16[32,512]{1,0:T(8,128)(2,1)S(1)}, u32[]{:S(2)}, u32[]{:S(2)}) collective-permute-start(bf16[32,512]{1,0:T(8,128)(2,1)S(1)} %payload.1), channel_id=1, source_target_pairs={{0,8},{1,9},{2,10},{3,11},{4,12},{5,13},{6,14},{7,15},{8,16},{9,17... | collective-permute-start | bytes 98312 | tf_op jit(solution)/shard_map/ppermute | solution.py:312
  3.8 1.7 %collective-permute-start.1 = (bf16[32,512]{1,0:T(8,128)(2,1)S(1)}, bf16[32,512]{1,0:T(8,128)(2,1)S(1)}, u32[]{:S(2)}, u32[]{:S(2)}) collective-permute-start(bf16[32,512]{1,0:T(8,128)(2,1)S(1)} %payload.1), channel_id=1, source_target_pairs={{0,24},{1,25},{2,26},{3,27},{4,28},{5,29},{6,30},{7,31},{8,0},{9,1... | collective-permute-start | bytes 98312 | tf_op jit(solution)/shard_map/ppermute | solution.py:312
  5.5 2.0 %collective-permute-start.2 = (bf16[32,512]{1,0:T(8,128)(2,1)S(1)}, bf16[32,512]{1,0:T(8,128)(2,1)S(1)}, u32[]{:S(2)}, u32[]{:S(2)}) collective-permute-start(bf16[32,512]{1,0:T(8,128)(2,1)S(1)} %payload.1), channel_id=1, source_target_pairs={{0,16},{1,17},{2,18},{3,19},{4,20},{5,21},{6,22},{7,23},{8,24},{9,... | collective-permute-start | bytes 98312 | tf_op jit(solution)/shard_map/ppermute | solution.py:312
  7.5 1.6 %collective-permute-start.7 = (bf16[2,32,512]{2,1,0:T(8,128)(2,1)S(1)}, bf16[2,32,512]{2,1,0:T(8,128)(2,1)S(1)}, u32[]{:S(2)}, u32[]{:S(2)}) collective-permute-start(bf16[2,32,512]{2,1,0:T(8,128)(2,1)S(1)} %get-tuple-element.33), channel_id=1, source_target_pairs={{0,64},{32,96},{64,128},{96,160},{128,192},{160,224},{192,0},{224,... | collective-permute-start | bytes 196616 | tf_op jit(solution)/shard_map/ppermute | solution.py:308
  9.1 1.7 %collective-permute-start.8 = (bf16[2,32,512]{2,1,0:T(8,128)(2,1)S(1)}, bf16[2,32,512]{2,1,0:T(8,128)(2,1)S(1)}, u32[]{:S(2)}, u32[]{:S(2)}) collective-permute-start(bf16[2,32,512]{2,1,0:T(8,128)(2,1)S(1)} %get-tuple-element.33), channel_id=1, source_target_pairs={{0,192},{32,224},{64,0},{96,32},{128,64},{160,96},{192,128},{224,1... | collective-permute-start | bytes 196616 | tf_op jit(solution)/shard_map/ppermute | solution.py:308
  10.8 1.8 %collective-permute-start.9 = (bf16[2,32,512]{2,1,0:T(8,128)(2,1)S(1)}, bf16[2,32,512]{2,1,0:T(8,128)(2,1)S(1)}, u32[]{:S(2)}, u32[]{:S(2)}) collective-permute-start(bf16[2,32,512]{2,1,0:T(8,128)(2,1)S(1)} %get-tuple-element.33), channel_id=1, source_target_pairs={{0,128},{32,160},{64,192},{96,224},{128,0},{160,32},{192,64},{224,... | collective-permute-start | bytes 196616 | tf_op jit(solution)/shard_map/ppermute | solution.py:308
  12.6 6.4 %collective-permute-start.3 = (bf16[4,32,512]{2,1,0:T(8,128)(2,1)S(1)}, bf16[4,32,512]{2,1,0:T(8,128)(2,1)S(1)}, u32[]{:S(2)}, u32[]{:S(2)}) collective-permute-start(bf16[4,32,512]{2,1,0:T(8,128)(2,1)S(1)} %pad_maximum_fusion.2), channel_id=1, source_target_pairs={{0,4},{1,5},{2,6},{3,7},{4,0},{5,1},{6,2},{7,3},{8,12},{9,13},{10,... | collective-permute-start | bytes 393224 | tf_op jit(solution)/shard_map/ppermute | solution.py:316
  19.3 0.7 concatenate.40
  20.1 0.5 copy.23
  20.5 4.9 %flux.5.refs_0_ = f32[4096,48]{1,0:T(8,128)S(1)} custom-call(bf16[2,32,512]{2,1,0:T(8,128)(2,1)S(1)} %get-tuple-element.32.cols_ref, bf16[4096,48]{1,0:T(8,128)(2,1)S(1)} %bitcast.29), custom_call_target="tpu_custom_call" | custom-call | flops 4294967296 | bytes 2097152 | tf_op jit(solution)/shard_map/flux/pallas_call | solution.py:200
  25.5 1.7 %collective-permute-start.4 = (bf16[8,32,512]{2,1,0:T(8,128)(2,1)S(1)}, bf16[8,32,512]{2,1,0:T(8,128)(2,1)S(1)}, u32[]{:S(2)}, u32[]{:S(2)}) collective-permute-start(bf16[8,32,512]{2,1,0:T(8,128)(2,1)S(1)} %get-tuple-element.30), channel_id=1, source_target_pairs={{0,2},{1,3},{2,0},{3,1},{4,6},{5,7},{6,4},{7,5},{8,10},{9,11},{10,... | collective-permute-start | bytes 786440 | tf_op jit(solution)/shard_map/ppermute | solution.py:316
  27.3 13.8 %flux.6.refs_0_ = f32[4096,48]{1,0:T(8,128)S(1)} custom-call(bf16[6,32,512]{2,1,0:T(8,128)(2,1)S(1)} %pad_maximum_fusion.1.cols_ref, bf16[4096,48]{1,0:T(8,128)(2,1)S(1)} %bitcast.30, f32[4096,48]{1,0:T(8,128)S(1)} %flux.5.refs_0_), custom_call_target="tpu_custom_call" | custom-call | flops 12884901888 | bytes 2097152 | tf_op jit(solution)/shard_map/flux/pallas_call | solution.py:200
  41.1 0.0 copy-start
  41.1 1.1 collective-permute-start.5
  42.2 18.2 %flux.7.refs_0_ = f32[4096,48]{1,0:T(8,128)S(1)} custom-call(bf16[8,32,512]{2,1,0:T(8,128)(2,1)S(1)} %collective-permute-done.4.cols_ref, bf16[4096,48]{1,0:T(8,128)(2,1)S(1)} %bitcast.31, f32[4096,48]{1,0:T(8,128)S(1)} %flux.6.refs_0_), custom_call_target="tpu_custom_call" | custom-call | flops 17179869184 | bytes 2097152 | tf_op jit(solution)/shard_map/flux/pallas_call | solution.py:200
  60.4 0.0 copy-start.4
  60.4 0.0 copy-start.5
  60.5 0.0 copy-start.8
  60.5 28.2 %flux.8 = f32[6,24,512]{2,1,0:T(8,128)S(1)} custom-call(bf16[16,32,512]{2,1,0:T(8,128)(2,1)S(1)} %collective-permute-done.5.cols_ref, bf16[4096,48]{1,0:T(8,128)(2,1)S(1)} %bitcast.32, f32[4096,48]{1,0:T(8,128)S(1)} %flux.7.refs_0_, f32[8,8,512]{2,1,0:T(8,128)S(1)} %concatenate.42.refs_1_, f32[64,512]{1,0:T(8,128)S(1)} %copy-done), custom_call_target="tpu_custom_call" | custom-call | flops 25769803776 | bytes 1572864 | tf_op jit(solution)/shard_map/flux/pallas_call | solution.py:200
  88.7 1.2 collective-permute-start.10
  90.0 0.9 collective-permute-start.11
  90.8 1.7 %collective-permute-start.12 = (f32[2,24,512]{2,1,0:T(8,128)S(1)}, f32[2,24,512]{2,1,0:T(8,128)S(1)}, u32[]{:S(2)}, u32[]{:S(2)}) collective-permute-start(f32[2,24,512]{2,1,0:T(8,128)S(1)} %get-tuple-element.20), channel_id=1, source_target_pairs={{0,128},{32,160},{64,192},{96,224},{128,0},{160,32},{192,64},{224,... | collective-permute-start | bytes 294920 | tf_op jit(solution)/shard_map/ppermute | solution.py:308
  92.6 10.8 %flux.9 = (f32[2,24,512]{2,1,0:T(8,128)S(1)}, f32[1,512]{1,0:T(1,128)S(1)}, f32[1,512]{1,0:T(1,128)}) custom-call(bf16[16,32,512]{2,1,0:T(8,128)(2,1)S(1)} %collective-permute-done.5.cols_ref, bf16[4096,48]{1,0:T(8,128)(2,1)S(1)} %bitcast.33, f32[4096,48]{1,0:T(8,128)S(1)} %flux.7.refs_0_, f32[8,8,512]{2,1,0:T(8,128)S(1)} %concatenate.42.refs_1_, ...), custom_call_target="tpu_custom_call" | custom-call | flops 8589934592 | bytes 524288 | tf_op jit(solution)/shard_map/flux/pallas_call | solution.py:200
  103.5 0.1 collective-permute-start.13
  103.6 1.2 collective-permute-done.13.swap_ref
  104.8 0.3 image.1
  105.1 14.5 %all_to_all.10.in_ref = f32[16,16,128]{2,1,0:T(8,128)S(1)} all-to-all(f32[16,16,128]{2,1,0:T(8,128)S(1)} %get-tuple-element.15), channel_id=1, replica_groups={{0,1,2,3,4,5,6,7,32,33,34,35,36,37,38,39},{8,9,10,11,12,13,14,15,40,41,..., dimensions={0} | all-to-all | bytes 262144 | tf_op jit(solution)/shard_map/all_to_all | solution.py:370
  119.7 0.1 middle.1
  119.7 12.0 %all_to_all.11.stats_ref = f32[16,24,128]{2,1,0:T(8,128)S(1)} all-to-all(f32[16,24,128]{2,1,0:T(8,128)S(1)} %middle.1), channel_id=1, replica_groups={{0,8,16,24,64,72,80,88,128,136,144,152,192,200,208,216},{1,9,17,25,65,7..., dimensions={0} | all-to-all | bytes 393216 | tf_op jit(solution)/shard_map/all_to_all | solution.py:372
  131.7 2.5 %finish.1 = (f32[16,512]{1,0:T(8,128)}, f32[16,64]{1,0:T(8,128)}, f32[16,16]{1,0:T(8,128)}) custom-call(f32[64,512]{1,0:T(8,128)S(1)} %copy-done, f32[16,512]{1,0:T(8,128)S(1)} %get-tuple-element.14.image_ref, f32[16,24,128]{2,1,0:T(8,128)S(1)} %all_to_all.11.stats_ref), custom_call_target="tpu_custom_call" | custom-call | tf_op jit(solution)/shard_map/finish/pallas_call | solution.py:288
  (50 shorter events, 0.5 us)
Async XLA Ops:
  0.6 0.8 copy-start.1
  1.4 0.7 copy-start.3
  2.1 5.3 %collective-permute-start = (bf16[32,512]{1,0:T(8,128)(2,1)S(1)}, bf16[32,512]{1,0:T(8,128)(2,1)S(1)}, u32[]{:S(2)}, u32[]{:S(2)}) collective-permute-start(bf16[32,512]{1,0:T(8,128)(2,1)S(1)} %payload.1), channel_id=1, source_target_pairs={{0,8},{1,9},{2,10},{3,11},{4,12},{5,13},{6,14},{7,15},{8,16},{9,17... | collective-permute-start | bytes 98312 | tf_op jit(solution)/shard_map/ppermute | solution.py:312
  3.8 3.7 %collective-permute-start.6 = (bf16[32,512]{1,0:T(8,128)(2,1)S(1)}, bf16[32,512]{1,0:T(8,128)(2,1)S(1)}, u32[]{:S(2)}, u32[]{:S(2)}) collective-permute-start(bf16[32,512]{1,0:T(8,128)(2,1)S(1)} %payload.1), channel_id=1, source_target_pairs={{0,32},{32,0},{64,96},{96,64},{128,160},{160,128},{192,224},{224,1... | collective-permute-start | bytes 98312 | tf_op jit(solution)/shard_map/ppermute | solution.py:304
  3.8 8.8 %collective-permute-start.1 = (bf16[32,512]{1,0:T(8,128)(2,1)S(1)}, bf16[32,512]{1,0:T(8,128)(2,1)S(1)}, u32[]{:S(2)}, u32[]{:S(2)}) collective-permute-start(bf16[32,512]{1,0:T(8,128)(2,1)S(1)} %payload.1), channel_id=1, source_target_pairs={{0,24},{1,25},{2,26},{3,27},{4,28},{5,29},{6,30},{7,31},{8,0},{9,1... | collective-permute-start | bytes 98312 | tf_op jit(solution)/shard_map/ppermute | solution.py:312
  5.5 7.2 %collective-permute-start.2 = (bf16[32,512]{1,0:T(8,128)(2,1)S(1)}, bf16[32,512]{1,0:T(8,128)(2,1)S(1)}, u32[]{:S(2)}, u32[]{:S(2)}) collective-permute-start(bf16[32,512]{1,0:T(8,128)(2,1)S(1)} %payload.1), channel_id=1, source_target_pairs={{0,16},{1,17},{2,18},{3,19},{4,20},{5,21},{6,22},{7,23},{8,24},{9,... | collective-permute-start | bytes 98312 | tf_op jit(solution)/shard_map/ppermute | solution.py:312
  7.5 11.6 %collective-permute-start.7 = (bf16[2,32,512]{2,1,0:T(8,128)(2,1)S(1)}, bf16[2,32,512]{2,1,0:T(8,128)(2,1)S(1)}, u32[]{:S(2)}, u32[]{:S(2)}) collective-permute-start(bf16[2,32,512]{2,1,0:T(8,128)(2,1)S(1)} %get-tuple-element.33), channel_id=1, source_target_pairs={{0,64},{32,96},{64,128},{96,160},{128,192},{160,224},{192,0},{224,... | collective-permute-start | bytes 196616 | tf_op jit(solution)/shard_map/ppermute | solution.py:308
  9.1 10.0 %collective-permute-start.8 = (bf16[2,32,512]{2,1,0:T(8,128)(2,1)S(1)}, bf16[2,32,512]{2,1,0:T(8,128)(2,1)S(1)}, u32[]{:S(2)}, u32[]{:S(2)}) collective-permute-start(bf16[2,32,512]{2,1,0:T(8,128)(2,1)S(1)} %get-tuple-element.33), channel_id=1, source_target_pairs={{0,192},{32,224},{64,0},{96,32},{128,64},{160,96},{192,128},{224,1... | collective-permute-start | bytes 196616 | tf_op jit(solution)/shard_map/ppermute | solution.py:308
  10.8 8.3 %collective-permute-start.9 = (bf16[2,32,512]{2,1,0:T(8,128)(2,1)S(1)}, bf16[2,32,512]{2,1,0:T(8,128)(2,1)S(1)}, u32[]{:S(2)}, u32[]{:S(2)}) collective-permute-start(bf16[2,32,512]{2,1,0:T(8,128)(2,1)S(1)} %get-tuple-element.33), channel_id=1, source_target_pairs={{0,128},{32,160},{64,192},{96,224},{128,0},{160,32},{192,64},{224,... | collective-permute-start | bytes 196616 | tf_op jit(solution)/shard_map/ppermute | solution.py:308
  12.6 12.8 %collective-permute-start.3 = (bf16[4,32,512]{2,1,0:T(8,128)(2,1)S(1)}, bf16[4,32,512]{2,1,0:T(8,128)(2,1)S(1)}, u32[]{:S(2)}, u32[]{:S(2)}) collective-permute-start(bf16[4,32,512]{2,1,0:T(8,128)(2,1)S(1)} %pad_maximum_fusion.2), channel_id=1, source_target_pairs={{0,4},{1,5},{2,6},{3,7},{4,0},{5,1},{6,2},{7,3},{8,12},{9,13},{10,... | collective-permute-start | bytes 393224 | tf_op jit(solution)/shard_map/ppermute | solution.py:316
  25.5 15.6 %collective-permute-start.4 = (bf16[8,32,512]{2,1,0:T(8,128)(2,1)S(1)}, bf16[8,32,512]{2,1,0:T(8,128)(2,1)S(1)}, u32[]{:S(2)}, u32[]{:S(2)}) collective-permute-start(bf16[8,32,512]{2,1,0:T(8,128)(2,1)S(1)} %get-tuple-element.30), channel_id=1, source_target_pairs={{0,2},{1,3},{2,0},{3,1},{4,6},{5,7},{6,4},{7,5},{8,10},{9,11},{10,... | collective-permute-start | bytes 786440 | tf_op jit(solution)/shard_map/ppermute | solution.py:316
  41.1 19.4 %copy-start = (f32[64,512]{1,0:T(8,128)S(1)}, f32[64,512]{1,0:T(8,128)}, u32[]{:S(2)}) copy-start(f32[64,512]{1,0:T(8,128)} %krylov_ref.3) | copy-start | bytes 393220
  41.1 19.4 %collective-permute-start.5 = (bf16[16,32,512]{2,1,0:T(8,128)(2,1)S(1)}, bf16[16,32,512]{2,1,0:T(8,128)(2,1)S(1)}, u32[]{:S(2)}, u32[]{:S(2)}) collective-permute-start(bf16[16,32,512]{2,1,0:T(8,128)(2,1)S(1)} %constant_dynamic-update-slice_fusion.5), channel_id=1, source_target_pairs={{0,1},{1,0},{2,3},{3,2},{4,5},{5,4},{6,7},{7,6},{8,9},{9,8},{10,11... | collective-permute-start | bytes 1572872 | tf_op jit(solution)/shard_map/ppermute | solution.py:316
  60.4 32.2 %copy-start.2 = (f32[16,512]{1,0:T(8,128)S(1)}, f32[16,512]{1,0:T(8,128)}, u32[]{:S(2)}) copy-start(f32[16,512]{1,0:T(8,128)} %amps_ref.3) | copy-start | bytes 98308
  60.4 32.2 %copy-start.4 = (f32[512]{0:T(512)S(1)}, f32[512]{0:T(512)}, u32[]{:S(2)}) copy-start(f32[512]{0:T(512)} %param.12) | copy-start | bytes 6148
  60.4 32.2 %copy-start.5 = (f32[512]{0:T(512)S(1)}, f32[512]{0:T(512)}, u32[]{:S(2)}) copy-start(f32[512]{0:T(512)} %param.13) | copy-start | bytes 6148
  60.4 32.1 %copy-start.6 = (s32[512]{0:T(512)S(1)}, s32[512]{0:T(512)}, u32[]{:S(2)}) copy-start(s32[512]{0:T(512)} %param.14) | copy-start | bytes 6148
  60.4 32.1 %copy-start.7 = (s32[512]{0:T(512)S(1)}, s32[512]{0:T(512)}, u32[]{:S(2)}) copy-start(s32[512]{0:T(512)} %param.16) | copy-start | bytes 6148
  60.5 32.1 %copy-start.8 = (f32[8]{0:T(128)S(1)}, f32[8]{0:T(128)}, u32[]{:S(2)}) copy-start(f32[8]{0:T(128)} %refs_8_.1) | copy-start | bytes 100
  60.5 32.1 %copy-start.9 = (f32[32]{0:T(128)S(1)}, f32[32]{0:T(128)}, u32[]{:S(2)}) copy-start(f32[32]{0:T(128)} %refs_9_.1) | copy-start | bytes 388
  88.7 14.7 %collective-permute-start.10 = (f32[2,24,512]{2,1,0:T(8,128)S(1)}, f32[2,24,512]{2,1,0:T(8,128)S(1)}, u32[]{:S(2)}, u32[]{:S(2)}) collective-permute-start(f32[2,24,512]{2,1,0:T(8,128)S(1)} %get-tuple-element.22), channel_id=1, source_target_pairs={{0,192},{32,224},{64,0},{96,32},{128,64},{160,96},{192,128},{224,1... | collective-permute-start | bytes 294920 | tf_op jit(solution)/shard_map/ppermute | solution.py:308
  90.0 13.5 %collective-permute-start.11 = (f32[2,24,512]{2,1,0:T(8,128)S(1)}, f32[2,24,512]{2,1,0:T(8,128)S(1)}, u32[]{:S(2)}, u32[]{:S(2)}) collective-permute-start(f32[2,24,512]{2,1,0:T(8,128)S(1)} %get-tuple-element.21), channel_id=1, source_target_pairs={{0,64},{32,96},{64,128},{96,160},{128,192},{160,224},{192,0},{224,... | collective-permute-start | bytes 294920 | tf_op jit(solution)/shard_map/ppermute | solution.py:308
  90.8 12.6 %collective-permute-start.12 = (f32[2,24,512]{2,1,0:T(8,128)S(1)}, f32[2,24,512]{2,1,0:T(8,128)S(1)}, u32[]{:S(2)}, u32[]{:S(2)}) collective-permute-start(f32[2,24,512]{2,1,0:T(8,128)S(1)} %get-tuple-element.20), channel_id=1, source_target_pairs={{0,128},{32,160},{64,192},{96,224},{128,0},{160,32},{192,64},{224,... | collective-permute-start | bytes 294920 | tf_op jit(solution)/shard_map/ppermute | solution.py:308
  103.5 1.3 collective-permute-start.13

commit v3 on v2

--- a/solution.py
+++ b/solution.py
@@ -12,8 +12,8 @@
 BF16 = jnp.bfloat16
 NT = (((1,), (1,)), ((), ()))
 SECTIONS = 16
-ROW_TILE = 256
-COL_TILE = 1024
+ROW_TILE = 1024
+COL_TILE = 256
 CORE_Z = [
     [(2 * x + c) * 32 + 8 * y + z for c in range(2) for z in range(8)]
     for x in range(4)
@@ -27,15 +27,14 @@
 BLOCKS = ((1, 0), (1, 1), (3, 0), (3, 1), (2, 0), (2, 1), (0, 1), (0, 0))
 
 
-def small_call(body, args, shapes, name, scalars=0):
+def small_call(body, args, shapes, name, limit=16):
     whole = pl.BlockSpec(memory_space=pltpu.VMEM)
-    scalar = pl.BlockSpec(memory_space=pltpu.SMEM)
     return pl.pallas_call(
         body,
-        in_specs=[whole] * (len(args) - scalars) + [scalar] * scalars,
+        in_specs=[whole] * len(args),
         out_specs=[whole] * len(shapes),
         out_shape=[jax.ShapeDtypeStruct(shape, dtype) for shape, dtype in shapes],
-        compiler_params=pltpu.CompilerParams(vmem_limit_bytes=16 * 2**20),
+        compiler_params=pltpu.CompilerParams(vmem_limit_bytes=limit * 2**20),
         name=name,
     )(*args)
 
@@ -82,27 +81,28 @@
     first = [-2 * high, -2 * high, one, one, one] + [zero] * 6 + [rows[6:7]]
     second = [-2 * low, -2 * low] + [zero] * 9 + [rows[7:8]]
     third = [zero] * 15 + [rows[8:9]]
-    return jnp.concatenate(first + second + third, axis=0).T
+    return jnp.concatenate(first + second + third, axis=0)
 
 
 def flux_body(kind, row0, group_rows, cols_ref, a_ref, *refs):
     finish = kind in ("away", "mine")
-    acc_ref = s_ref = krylov_ref = None
-    heat_in = heat_out = ()
+    acc_ref = None
     if kind != "first":
         acc_ref, refs = refs[0], refs[1:]
     if finish:
-        s_ref, krylov_ref, refs = refs[0], refs[1], refs[2:]
+        s_ref, refs = refs[0], refs[1:]
+    if kind == "away":
+        krylov_ref, heat_in, refs = refs[0], refs[1:8], refs[8:]
     if kind == "mine":
-        heat_in, refs = refs[:7], refs[7:]
+        kk_ref, refs = refs[0], refs[1:]
     out_ref, refs = refs[0], refs[1:]
-    if kind == "mine":
-        heat_out, refs = refs[:2], refs[2:]
+    if kind == "away":
+        kk_ref, heat_out, refs = refs[0], refs[1:3], refs[3:]
     b_scr, w_scr = refs[:2]
     total = refs[2] if finish else out_ref
     step, group = pl.program_id(0), pl.program_id(1)
     width = cols_ref.shape[2]
-    span = b_scr.shape[1]
+    span = w_scr.shape[1]
     chunks = span // width
     base = pl.multiple_of(group * group_rows, group_rows)
 
@@ -110,43 +110,42 @@
     def _():
         for y in range(chunks):
             at = slice(y * width, (y + 1) * width)
-            geo = cols_ref[step * chunks + y, 0:16, :]
-            b_scr[0:16, at] = geo
-            b_scr[16:32, at] = geo
-            b_scr[32:48, at] = geo
-            wide = geo.astype(F32)
+            geo = cols_ref[step * chunks + y, 0:16, :].astype(F32)
             wire = cols_ref[step * chunks + y, 16:32, :].astype(F32)
+            b_scr[at, :] = jnp.concatenate([geo, geo, geo], axis=0).T.astype(BF16)
             for c in range(3):
-                seg = wide[9 + c : 10 + c] + wide[12 + c : 13 + c]
+                seg = geo[9 + c : 10 + c] + geo[12 + c : 13 + c]
                 w_scr[16 * c : 16 * (c + 1), at] = (wire * seg).astype(BF16)
+
+    def rows_at(k, offset):
+        return pl.ds(pl.multiple_of(offset + base + k * ROW_TILE, ROW_TILE), ROW_TILE)
 
     @pl.when(step == 0)
     def _():
-        here = pl.ds(base, group_rows)
-        if acc_ref is None:
-            total[here, :] = jnp.zeros((group_rows, total.shape[1]), F32)
-        else:
-            total[here, :] = acc_ref[pl.ds(pl.multiple_of(row0 + base, ROW_TILE), group_rows), :]
-
-    def rows_at(k, offset):
-        return pl.ds(pl.multiple_of(offset + base + k * ROW_TILE, ROW_TILE), ROW_TILE)
-
-    def product(tile, at):
-        return lax.dot_general(tile, w_scr[:, at], NT, preferred_element_type=F32)
-
-    tiles = [
-        (k, slice(j, j + COL_TILE))
-        for k in range(group_rows // ROW_TILE)
-        for j in range(0, span, COL_TILE)
-    ]
+        for k in range(group_rows // ROW_TILE):
+            if acc_ref is None:
+                total[:, rows_at(k, 0)] = jnp.zeros((3 * SECTIONS, ROW_TILE), F32)
+            else:
+                total[:, rows_at(k, 0)] = acc_ref[:, rows_at(k, row0)]
+
+    sums = {}
+
+    def add(k, at, tile):
+        part = jnp.dot(w_scr[:, at], tile, preferred_element_type=F32)
+        sums[k] = sums[k] + part if k in sums else part
+        if at.stop == span:
+            total[:, rows_at(k, 0)] += sums[k]
+
     held = None
-    for k, at in tiles:
-        r2 = jnp.dot(a_ref[rows_at(k, row0), :], b_scr[:, at], preferred_element_type=F32)
-        tile = lax.rsqrt(r2).astype(BF16)
-        if held is not None:
-            total[rows_at(held[0], 0), :] += product(*held[1:])
-        held = (k, tile, at)
-    total[rows_at(held[0], 0), :] += product(*held[1:])
+    for k in range(group_rows // ROW_TILE):
+        for j in range(0, span, COL_TILE):
+            at = slice(j, j + COL_TILE)
+            r2 = jnp.dot(b_scr[at, :], a_ref[:, rows_at(k, row0)], preferred_element_type=F32)
+            tile = lax.rsqrt(r2).astype(BF16)
+            if held is not None:
+                add(*held)
+            held = (k, at, tile)
+    add(*held)
 
     if finish:
 
@@ -154,7 +153,7 @@
         def _():
             for k in range(group_rows // width):
                 here = pl.ds(pl.multiple_of(base + k * width, width), width)
-                turned = total[here, :].T
+                turned = total[:, here]
                 block = group * (group_rows // width) + k
                 seg = s_ref[row0 // width + block]
                 out_ref[block, 0:16, :] = (
@@ -163,19 +162,18 @@
 
         @pl.when((step == 0) & (group == 0))
         def _():
-            krylov = krylov_ref[...]
-            kk_scr = refs[3]
-            kk_scr[...] = lax.dot_general(
-                krylov, krylov, NT, precision=HI, preferred_element_type=F32
-            )
+            if kind == "away":
+                krylov = krylov_ref[...]
+                kk_ref[...] = lax.dot_general(
+                    krylov, krylov, NT, precision=HI, preferred_element_type=F32
+                )
+                heat(*heat_in, *heat_out)
             me = lax.axis_index("row")
             for n in range(out_ref.shape[0]):
                 shift, swap = BLOCKS[row0 // width + n]
                 owner = (me // 2 + 4 - shift) % 4 * 2 + (me + swap) % 2
                 out_ref[n, 16:24, :] = jnp.zeros((8, width), F32)
-                out_ref[n, 16:24, 0:64] = kk_scr[pl.ds(pl.multiple_of(owner * 8, 8), 8), :]
-            if heat_in:
-                heat(*heat_in, *heat_out)
+                out_ref[n, 16:24, 0:64] = kk_ref[pl.ds(pl.multiple_of(owner * 8, 8), 8), :]
 
 
 def flux_call(kind, cols, a, *more, row0=0, rows, group_rows, step_chunks):
@@ -188,14 +186,15 @@
     if finish:
         shapes = [jax.ShapeDtypeStruct((rows // width, SECTIONS + 8, width), F32)]
     else:
-        shapes = [jax.ShapeDtypeStruct((rows, 3 * SECTIONS), F32)]
-    if kind == "mine":
+        shapes = [jax.ShapeDtypeStruct((3 * SECTIONS, rows), F32)]
+    if kind == "away":
         specs[-2:] = [scalar] * 2
+        shapes += [jax.ShapeDtypeStruct((64, 64), F32)]
         shapes += [jax.ShapeDtypeStruct((1, width), F32)] * 2
     span = step_chunks * width
-    scratch = [pltpu.VMEM((48, span), BF16), pltpu.VMEM((48, span), BF16)]
+    scratch = [pltpu.VMEM((span, 48), BF16), pltpu.VMEM((48, span), BF16)]
     if finish:
-        scratch += [pltpu.VMEM((rows, 3 * SECTIONS), F32), pltpu.VMEM((64, 64), F32)]
+        scratch.append(pltpu.VMEM((3 * SECTIONS, rows), F32))
     pairs = rows * chunks * width
     out = pl.pallas_call(
         functools.partial(flux_body, kind, row0, group_rows),
@@ -210,7 +209,7 @@
         ),
         name="flux",
     )(*args)
-    return out if kind == "mine" else out[0]
+    return out if kind == "away" else out[0]
 
 
 def image_body(sent1, sent3, sent2, mine_ref, swap_ref, rho_ref, amps_ref, krylov_ref, image_ref, stats_ref):
@@ -269,18 +268,17 @@
     resid = image_ref[...] - dot(turned, krylov_ref[...], nn)
     row = lax.broadcasted_iota(jnp.int32, gram.shape, 0)
     col = lax.broadcasted_iota(jnp.int32, gram.shape, 1)
-    tall = lax.broadcasted_iota(jnp.int32, resid.shape, 0)
     chol = jnp.zeros_like(gram)
     for j in range(SECTIONS):
-        scale = 1.0 / jnp.sqrt(gram[j : j + 1, j : j + 1])
-        column = jnp.where(row[:, 0:1] >= j, gram[:, j : j + 1] * scale, 0.0)
-        across = gram[j : j + 1, :] * scale
+        column = gram[:, j : j + 1]
         chol = jnp.where(col == j, column, chol)
-        solved = resid[j : j + 1, :] * scale
-        gram = gram - column * across
-        resid = jnp.where(tall == j, solved, resid - jnp.where(tall > j, column * solved, 0.0))
-    q_ref[...] = resid
-    chol_ref[...] = chol
+        ratio = column / gram[j : j + 1, j : j + 1]
+        resid = resid - jnp.where(row[:, 0:1] > j, ratio, 0.0) * resid[j : j + 1, :]
+        gram = gram - ratio * gram[j : j + 1, :]
+    chol = jnp.where(row >= col, chol, 0.0)
+    pivot = jnp.where(row == col, chol, 0.0)
+    q_ref[...] = resid / jnp.sqrt(jnp.sum(pivot, axis=1, keepdims=True))
+    chol_ref[...] = chol / jnp.sqrt(jnp.sum(pivot, axis=0, keepdims=True))
 
 
 def end_call(krylov, image, stats):
@@ -331,16 +329,17 @@
     own = small_call(
         payload_body, (strand_layout, strand_amperes_panel), [((32, width), BF16)], "payload"
     )[0]
+    ys = [shift_y(own, k) for k in (1, 3)]
     pair = jnp.stack([own, core_swap(own)])
+    late, pair = lax.optimization_barrier((own, pair))
     others = [shift_x(pair, k) for k in (1, 3, 2)]
-    column = jnp.stack([own] + [shift_y(own, k) for k in (1, 3, 2)])
+    column = jnp.stack([late] + ys + [shift_y(late, 2)])
 
     rows = jnp.concatenate(others + [pair[::-1]], axis=0)
     seg = rows[:, 9:12].astype(F32) + rows[:, 12:15].astype(F32)
     seg = jnp.concatenate([seg, jnp.zeros((8, 5, seg.shape[2]), F32)], axis=1)
     a = row_features(rows.transpose(1, 0, 2).reshape(32, -1))
-
-    count = a.shape[0]
+    count = a.shape[1]
     far = swap_z(column, 4)
     acc = flux_call("first", column[:2], a, rows=count, group_rows=2048, step_chunks=2)
     whole = jnp.concatenate([column, far], axis=0)
@@ -349,15 +348,15 @@
     whole = jnp.concatenate([whole, middle], axis=0)
     near = swap_z(whole, 1)
     acc = flux_call("next", middle, a, acc, rows=count, group_rows=1024, step_chunks=8)
-    away = flux_call(
-        "away", near, a, acc, seg, krylov_vectors, rows=3072, group_rows=1024, step_chunks=8
+    flat = (strand_kelvin, strand_ohmic_value, strand_warmer_slot, strand_region_slot)
+    away, kk, rho, joule = flux_call(
+        "away", near, a, acc, seg, krylov_vectors, *(v[None] for v in flat), strand_amperes_panel,
+        warmer_kelvin_gain, region_threshold_kelvin,
+        rows=3072, group_rows=1024, step_chunks=8,
     )
     sent = [shift_x(away[2 * n : 2 * n + 2], -k) for n, k in enumerate((1, 3, 2))]
-    flat = (strand_kelvin, strand_ohmic_value, strand_warmer_slot, strand_region_slot)
-    mine, rho, joule = flux_call(
-        "mine", near, a, acc, seg, krylov_vectors, *(v[None] for v in flat), strand_amperes_panel,
-        warmer_kelvin_gain, region_threshold_kelvin,
-        row0=3072, rows=1024, group_rows=1024, step_chunks=8,
+    mine = flux_call(
+        "mine", near, a, acc, seg, kk, row0=3072, rows=1024, group_rows=1024, step_chunks=8
     )
     swapped = core_swap(sent[0][1] + sent[1][1] + sent[2][1] + mine[0])
 

time: 135 us -> 122 us (0.904)
  Pallas kernels: 78.8 us -> 64 us
  starting transfers between devices: 23.6 us -> 26 us
    pallas_call x5, Pallas kernels: 75.8 us -> 61.1 us  [flux_call(): pl.pallas_call(functools.partial(flux_body, kind, row0, group_rows), grid...]
    ppermute x6, starting transfers between devices: 8.94 us -> 11 us  [shift_x(): return lax.ppermute(value, 'row', [(i, (i + 2 * k) % 8) for i in range(8)])]
  transfers between devices with their start and end apart: 14 -> 14, of which waited for: 1 -> 2; matrix products, arithmetic and copies ran while one was open for 1% -> 1% of each run, Pallas kernels for 35% -> 31%
where the time goes in v3:
time: 122 us
  Pallas kernels  64 us (52%)
  starting transfers between devices  26 us (21%)
  blocking collectives  25.9 us (21%)
  local copies, waits for them, and re-layouts  3.03 us (2%)
  waiting for transfers between devices  1.54 us (1%)
    pallas_call x5, Pallas kernels, flux_call(): pl.pallas_call(functools.partial(flux_body, kind, row0, group_rows), grid...  61.1 us
    all_to_all x1, blocking collectives, local(): lax.all_to_all(stats, ('row', 'col'), 0, 0, axis_index_groups=CORE_Z)  15 us
    ppermute x6, starting transfers between devices, shift_x(): return lax.ppermute(value, 'row', [(i, (i + 2 * k) % 8) for i in range(8)])  11 us
    all_to_all x1, blocking collectives, local(): stats = lax.all_to_all(stats, ('row', 'col'), 0, 0, axis_index_groups=X_Y)  10.9 us
    ppermute x3, starting transfers between devices, swap_z(): return lax.ppermute(value, 'col', [(i, i ^ k) for i in range(32)])  9.47 us
    ppermute x3, starting transfers between devices, shift_y(): lax.ppermute(value, 'col', [(i, (i + 8 * k) % 32) for i in range(32)])  5.38 us
  transfers between devices with their start and end apart: 14, of which 2 were waited for; matrix products, arithmetic and copies ran while one was open for 1% of the time, Pallas kernels for 31%

profile of v3, /device:TPU:32, one launch (start us, length us, event | category | flops | bytes accessed | tf_op | source)
XLA Modules:
  0.0 121.6 jit_solution(14017535839022053259)
XLA Ops:
  0.6 0.7 copy-done.1
  1.4 0.7 copy-done.3
  2.1 0.1 collective-permute-start
  2.2 3.1 %collective-permute-start.2 = (bf16[32,512]{1,0:T(8,128)(2,1)S(1)}, bf16[32,512]{1,0:T(8,128)(2,1)S(1)}, u32[]{:S(2)}, u32[]{:S(2)}) collective-permute-start(bf16[32,512]{1,0:T(8,128)(2,1)S(1)} %payload.1), channel_id=1, source_target_pairs={{0,24},{1,25},{2,26},{3,27},{4,28},{5,29},{6,30},{7,31},{8,0},{9,1... | collective-permute-start | bytes 98312 | tf_op jit(solution)/shard_map/ppermute | solution.py:310
  5.3 2.3 %collective-permute-start.3 = (bf16[32,512]{1,0:T(8,128)(2,1)S(1)}, bf16[32,512]{1,0:T(8,128)(2,1)S(1)}, u32[]{:S(2)}, u32[]{:S(2)}) collective-permute-start(bf16[32,512]{1,0:T(8,128)(2,1)S(1)} %payload.1), channel_id=1, source_target_pairs={{0,16},{1,17},{2,18},{3,19},{4,20},{5,21},{6,22},{7,23},{8,24},{9,... | collective-permute-start | bytes 98312 | tf_op jit(solution)/shard_map/ppermute | solution.py:310
  7.6 3.0 %collective-permute-start.9 = (bf16[2,32,512]{2,1,0:T(8,128)(2,1)S(1)}, bf16[2,32,512]{2,1,0:T(8,128)(2,1)S(1)}, u32[]{:S(2)}, u32[]{:S(2)}) collective-permute-start(bf16[2,32,512]{2,1,0:T(8,128)(2,1)S(1)} %pad_maximum_fusion.3), channel_id=1, source_target_pairs={{0,128},{32,160},{64,192},{96,224},{128,0},{160,32},{192,64},{224,... | collective-permute-start | bytes 196616 | tf_op jit(solution)/shard_map/ppermute | solution.py:306
  10.7 2.6 %collective-permute-start.8 = (bf16[2,32,512]{2,1,0:T(8,128)(2,1)S(1)}, bf16[2,32,512]{2,1,0:T(8,128)(2,1)S(1)}, u32[]{:S(2)}, u32[]{:S(2)}) collective-permute-start(bf16[2,32,512]{2,1,0:T(8,128)(2,1)S(1)} %pad_maximum_fusion.3), channel_id=1, source_target_pairs={{0,192},{32,224},{64,0},{96,32},{128,64},{160,96},{192,128},{224,1... | collective-permute-start | bytes 196616 | tf_op jit(solution)/shard_map/ppermute | solution.py:306
  13.4 6.4 %collective-permute-start.4 = (bf16[4,32,512]{2,1,0:T(8,128)(2,1)S(1)}, bf16[4,32,512]{2,1,0:T(8,128)(2,1)S(1)}, u32[]{:S(2)}, u32[]{:S(2)}) collective-permute-start(bf16[4,32,512]{2,1,0:T(8,128)(2,1)S(1)} %pad_maximum_fusion.2), channel_id=1, source_target_pairs={{0,4},{1,5},{2,6},{3,7},{4,0},{5,1},{6,2},{7,3},{8,12},{9,13},{10,... | collective-permute-start | bytes 393224 | tf_op jit(solution)/shard_map/ppermute | solution.py:314
  20.0 0.7 concatenate.40.a_ref
  20.7 4.0 %flux.5.refs_0_ = f32[48,4096]{1,0:T(8,128)S(1)} custom-call(bf16[2,32,512]{2,1,0:T(8,128)(2,1)S(1)} %pad_maximum_fusion.4.cols_ref, bf16[48,4096]{1,0:T(8,128)(2,1)S(1)} %concatenate.40.a_ref), custom_call_target="tpu_custom_call" | custom-call | flops 4294967296 | bytes 2097152 | tf_op jit(solution)/shard_map/flux/pallas_call | solution.py:199
  24.8 0.3 collective-permute-done.4
  25.1 2.1 %collective-permute-start.5 = (bf16[8,32,512]{2,1,0:T(8,128)(2,1)S(1)}, bf16[8,32,512]{2,1,0:T(8,128)(2,1)S(1)}, u32[]{:S(2)}, u32[]{:S(2)}) collective-permute-start(bf16[8,32,512]{2,1,0:T(8,128)(2,1)S(1)} %get-tuple-element.36), channel_id=1, source_target_pairs={{0,2},{1,3},{2,0},{3,1},{4,6},{5,7},{6,4},{7,5},{8,10},{9,11},{10,... | collective-permute-start | bytes 786440 | tf_op jit(solution)/shard_map/ppermute | solution.py:314
  27.2 11.1 %flux.6.refs_0_ = f32[48,4096]{1,0:T(8,128)S(1)} custom-call(bf16[6,32,512]{2,1,0:T(8,128)(2,1)S(1)} %pad_maximum_fusion.1.cols_ref, bf16[48,4096]{1,0:T(8,128)(2,1)S(1)} %concatenate.40.a_ref, f32[48,4096]{1,0:T(8,128)S(1)} %flux.5.refs_0_), custom_call_target="tpu_custom_call" | custom-call | flops 12884901888 | bytes 2097152 | tf_op jit(solution)/shard_map/flux/pallas_call | solution.py:199
  38.4 0.0 copy-start
  38.4 0.0 copy-start.2
  38.4 1.0 collective-permute-start.6
  39.4 14.6 %flux.7.refs_0_ = f32[48,4096]{1,0:T(8,128)S(1)} custom-call(bf16[8,32,512]{2,1,0:T(8,128)(2,1)S(1)} %collective-permute-done.5.cols_ref, bf16[48,4096]{1,0:T(8,128)(2,1)S(1)} %concatenate.40.a_ref, f32[48,4096]{1,0:T(8,128)S(1)} %flux.6.refs_0_), custom_call_target="tpu_custom_call" | custom-call | flops 17179869184 | bytes 2097152 | tf_op jit(solution)/shard_map/flux/pallas_call | solution.py:199
  54.0 0.0 copy-start.8
  54.0 0.0 copy-start.9
  54.1 0.6 copy-done.4
  54.7 23.6 %flux.8 = (f32[6,24,512]{2,1,0:T(8,128)S(1)}, f32[64,64]{1,0:T(8,128)S(1)}, f32[1,512]{1,0:T(1,128)S(1)}, f32[1,512]{1,0:T(1,128)}) custom-call(bf16[16,32,512]{2,1,0:T(8,128)(2,1)S(1)} %collective-permute-done.6.cols_ref, bf16[48,4096]{1,0:T(8,128)(2,1)S(1)} %concatenate.40.a_ref, f32[48,4096]{1,0:T(8,128)S(1)} %flux.7.refs_0_, ...), custom_call_target="tpu_custom_call" | custom-call | flops 25769803776 | bytes 1572864 | tf_op jit(solution)/shard_map/flux/pallas_call | solution.py:199
  78.3 2.1 %collective-permute-start.12 = (f32[2,24,512]{2,1,0:T(8,128)S(1)}, f32[2,24,512]{2,1,0:T(8,128)S(1)}, u32[]{:S(2)}, u32[]{:S(2)}) collective-permute-start(f32[2,24,512]{2,1,0:T(8,128)S(1)} %get-tuple-element.26), channel_id=1, source_target_pairs={{0,128},{32,160},{64,192},{96,224},{128,0},{160,32},{192,64},{224,... | collective-permute-start | bytes 294920 | tf_op jit(solution)/shard_map/ppermute | solution.py:306
  80.4 1.8 %collective-permute-start.11 = (f32[2,24,512]{2,1,0:T(8,128)S(1)}, f32[2,24,512]{2,1,0:T(8,128)S(1)}, u32[]{:S(2)}, u32[]{:S(2)}) collective-permute-start(f32[2,24,512]{2,1,0:T(8,128)S(1)} %get-tuple-element.27), channel_id=1, source_target_pairs={{0,64},{32,96},{64,128},{96,160},{128,192},{160,224},{192,0},{224,... | collective-permute-start | bytes 294920 | tf_op jit(solution)/shard_map/ppermute | solution.py:306
  82.2 1.4 %collective-permute-start.10 = (f32[2,24,512]{2,1,0:T(8,128)S(1)}, f32[2,24,512]{2,1,0:T(8,128)S(1)}, u32[]{:S(2)}, u32[]{:S(2)}) collective-permute-start(f32[2,24,512]{2,1,0:T(8,128)S(1)} %get-tuple-element.28), channel_id=1, source_target_pairs={{0,192},{32,224},{64,0},{96,32},{128,64},{160,96},{192,128},{224,1... | collective-permute-start | bytes 294920 | tf_op jit(solution)/shard_map/ppermute | solution.py:306
  83.7 7.8 %flux.9.mine_ref = f32[2,24,512]{2,1,0:T(8,128)S(1)} custom-call(bf16[16,32,512]{2,1,0:T(8,128)(2,1)S(1)} %collective-permute-done.6.cols_ref, bf16[48,4096]{1,0:T(8,128)(2,1)S(1)} %concatenate.40.a_ref, f32[48,4096]{1,0:T(8,128)S(1)} %flux.7.refs_0_, f32[8,8,512]{2,1,0:T(8,128)S(1)} %concatenate.42.refs_1_, f32[64,64]{1,0:T(8,128)S(1)} %get-tuple-element.18.refs_2_), custom_call_target="tpu_custom_call" | custom-call | flops 8589934592 | bytes 524288 | tf_op jit(solution)/shard_map/flux/pallas_call | solution.py:199
  91.5 0.1 collective-permute-start.13
  91.7 1.2 %collective-permute-done.13.swap_ref = f32[24,512]{1,0:T(8,128)S(1)} collective-permute-done((f32[24,512]{1,0:T(8,128)S(1)}, f32[24,512]{1,0:T(8,128)S(1)}, u32[]{:S(2)}, u32[]{:S(2)}) %collective-permute-start.13) | collective-permute-done | bytes 49184 | tf_op jit(solution)/shard_map/ppermute | solution.py:302
  92.9 0.3 image.1
  93.2 15.0 %all_to_all.10.in_ref = f32[16,16,128]{2,1,0:T(8,128)S(1)} all-to-all(f32[16,16,128]{2,1,0:T(8,128)S(1)} %get-tuple-element.21), channel_id=1, replica_groups={{0,1,2,3,4,5,6,7,32,33,34,35,36,37,38,39},{8,9,10,11,12,13,14,15,40,41,..., dimensions={0} | all-to-all | bytes 262144 | tf_op jit(solution)/shard_map/all_to_all | solution.py:369
  108.3 0.1 middle.1
  108.4 10.9 %all_to_all.11.stats_ref = f32[16,24,128]{2,1,0:T(8,128)S(1)} all-to-all(f32[16,24,128]{2,1,0:T(8,128)S(1)} %middle.1), channel_id=1, replica_groups={{0,8,16,24,64,72,80,88,128,136,144,152,192,200,208,216},{1,9,17,25,65,7..., dimensions={0} | all-to-all | bytes 393216 | tf_op jit(solution)/shard_map/all_to_all | solution.py:371
  119.2 2.4 %finish.1 = (f32[16,512]{1,0:T(8,128)}, f32[16,64]{1,0:T(8,128)}, f32[16,16]{1,0:T(8,128)}) custom-call(f32[64,512]{1,0:T(8,128)S(1)} %copy-done, f32[16,512]{1,0:T(8,128)S(1)} %get-tuple-element.20.image_ref, f32[16,24,128]{2,1,0:T(8,128)S(1)} %all_to_all.11.stats_ref), custom_call_target="tpu_custom_call" | custom-call | tf_op jit(solution)/shard_map/finish/pallas_call | solution.py:286
  (50 shorter events, 0.5 us)
Async XLA Ops:
  0.6 0.8 copy-start.1
  1.4 0.7 copy-start.3
  2.1 3.2 %collective-permute-start = (bf16[32,512]{1,0:T(8,128)(2,1)S(1)}, bf16[32,512]{1,0:T(8,128)(2,1)S(1)}, u32[]{:S(2)}, u32[]{:S(2)}) collective-permute-start(bf16[32,512]{1,0:T(8,128)(2,1)S(1)} %payload.1), channel_id=1, source_target_pairs={{0,32},{32,0},{64,96},{96,64},{128,160},{160,128},{192,224},{224,1... | collective-permute-start | bytes 98312 | tf_op jit(solution)/shard_map/ppermute | solution.py:302
  2.2 8.4 %collective-permute-start.2 = (bf16[32,512]{1,0:T(8,128)(2,1)S(1)}, bf16[32,512]{1,0:T(8,128)(2,1)S(1)}, u32[]{:S(2)}, u32[]{:S(2)}) collective-permute-start(bf16[32,512]{1,0:T(8,128)(2,1)S(1)} %payload.1), channel_id=1, source_target_pairs={{0,24},{1,25},{2,26},{3,27},{4,28},{5,29},{6,30},{7,31},{8,0},{9,1... | collective-permute-start | bytes 98312 | tf_op jit(solution)/shard_map/ppermute | solution.py:310
  5.3 5.3 %collective-permute-start.1 = (bf16[32,512]{1,0:T(8,128)(2,1)S(1)}, bf16[32,512]{1,0:T(8,128)(2,1)S(1)}, u32[]{:S(2)}, u32[]{:S(2)}) collective-permute-start(bf16[32,512]{1,0:T(8,128)(2,1)S(1)} %payload.1), channel_id=1, source_target_pairs={{0,8},{1,9},{2,10},{3,11},{4,12},{5,13},{6,14},{7,15},{8,16},{9,17... | collective-permute-start | bytes 98312 | tf_op jit(solution)/shard_map/ppermute | solution.py:310
  5.3 8.0 %collective-permute-start.3 = (bf16[32,512]{1,0:T(8,128)(2,1)S(1)}, bf16[32,512]{1,0:T(8,128)(2,1)S(1)}, u32[]{:S(2)}, u32[]{:S(2)}) collective-permute-start(bf16[32,512]{1,0:T(8,128)(2,1)S(1)} %payload.1), channel_id=1, source_target_pairs={{0,16},{1,17},{2,18},{3,19},{4,20},{5,21},{6,22},{7,23},{8,24},{9,... | collective-permute-start | bytes 98312 | tf_op jit(solution)/shard_map/ppermute | solution.py:310
  7.6 12.1 %collective-permute-start.9 = (bf16[2,32,512]{2,1,0:T(8,128)(2,1)S(1)}, bf16[2,32,512]{2,1,0:T(8,128)(2,1)S(1)}, u32[]{:S(2)}, u32[]{:S(2)}) collective-permute-start(bf16[2,32,512]{2,1,0:T(8,128)(2,1)S(1)} %pad_maximum_fusion.3), channel_id=1, source_target_pairs={{0,128},{32,160},{64,192},{96,224},{128,0},{160,32},{192,64},{224,... | collective-permute-start | bytes 196616 | tf_op jit(solution)/shard_map/ppermute | solution.py:306
  10.7 9.0 %collective-permute-start.8 = (bf16[2,32,512]{2,1,0:T(8,128)(2,1)S(1)}, bf16[2,32,512]{2,1,0:T(8,128)(2,1)S(1)}, u32[]{:S(2)}, u32[]{:S(2)}) collective-permute-start(bf16[2,32,512]{2,1,0:T(8,128)(2,1)S(1)} %pad_maximum_fusion.3), channel_id=1, source_target_pairs={{0,192},{32,224},{64,0},{96,32},{128,64},{160,96},{192,128},{224,1... | collective-permute-start | bytes 196616 | tf_op jit(solution)/shard_map/ppermute | solution.py:306
  13.3 6.4 %collective-permute-start.7 = (bf16[2,32,512]{2,1,0:T(8,128)(2,1)S(1)}, bf16[2,32,512]{2,1,0:T(8,128)(2,1)S(1)}, u32[]{:S(2)}, u32[]{:S(2)}) collective-permute-start(bf16[2,32,512]{2,1,0:T(8,128)(2,1)S(1)} %pad_maximum_fusion.3), channel_id=1, source_target_pairs={{0,64},{32,96},{64,128},{96,160},{128,192},{160,224},{192,0},{224,... | collective-permute-start | bytes 196616 | tf_op jit(solution)/shard_map/ppermute | solution.py:306
  13.4 11.7 %collective-permute-start.4 = (bf16[4,32,512]{2,1,0:T(8,128)(2,1)S(1)}, bf16[4,32,512]{2,1,0:T(8,128)(2,1)S(1)}, u32[]{:S(2)}, u32[]{:S(2)}) collective-permute-start(bf16[4,32,512]{2,1,0:T(8,128)(2,1)S(1)} %pad_maximum_fusion.2), channel_id=1, source_target_pairs={{0,4},{1,5},{2,6},{3,7},{4,0},{5,1},{6,2},{7,3},{8,12},{9,13},{10,... | collective-permute-start | bytes 393224 | tf_op jit(solution)/shard_map/ppermute | solution.py:314
  25.1 13.2 %collective-permute-start.5 = (bf16[8,32,512]{2,1,0:T(8,128)(2,1)S(1)}, bf16[8,32,512]{2,1,0:T(8,128)(2,1)S(1)}, u32[]{:S(2)}, u32[]{:S(2)}) collective-permute-start(bf16[8,32,512]{2,1,0:T(8,128)(2,1)S(1)} %get-tuple-element.36), channel_id=1, source_target_pairs={{0,2},{1,3},{2,0},{3,1},{4,6},{5,7},{6,4},{7,5},{8,10},{9,11},{10,... | collective-permute-start | bytes 786440 | tf_op jit(solution)/shard_map/ppermute | solution.py:314
  38.4 15.7 %copy-start = (f32[64,512]{1,0:T(8,128)S(1)}, f32[64,512]{1,0:T(8,128)}, u32[]{:S(2)}) copy-start(f32[64,512]{1,0:T(8,128)} %krylov_ref.3) | copy-start | bytes 393220
  38.4 15.7 %copy-start.2 = (f32[16,512]{1,0:T(8,128)S(1)}, f32[16,512]{1,0:T(8,128)}, u32[]{:S(2)}) copy-start(f32[16,512]{1,0:T(8,128)} %amps_ref.3) | copy-start | bytes 98308
  38.4 15.6 %collective-permute-start.6 = (bf16[16,32,512]{2,1,0:T(8,128)(2,1)S(1)}, bf16[16,32,512]{2,1,0:T(8,128)(2,1)S(1)}, u32[]{:S(2)}, u32[]{:S(2)}) collective-permute-start(bf16[16,32,512]{2,1,0:T(8,128)(2,1)S(1)} %constant_dynamic-update-slice_fusion.5), channel_id=1, source_target_pairs={{0,1},{1,0},{2,3},{3,2},{4,5},{5,4},{6,7},{7,6},{8,9},{9,8},{10,11... | collective-permute-start | bytes 1572872 | tf_op jit(solution)/shard_map/ppermute | solution.py:314
  39.4 14.6 %copy-start.5 = (f32[512]{0:T(512)S(1)}, f32[512]{0:T(512)}, u32[]{:S(2)}) copy-start(f32[512]{0:T(512)} %param.13) | copy-start | bytes 6148
  39.4 14.7 %copy-start.6 = (s32[512]{0:T(512)S(1)}, s32[512]{0:T(512)}, u32[]{:S(2)}) copy-start(s32[512]{0:T(512)} %param.14) | copy-start | bytes 6148
  39.4 14.7 %copy-start.7 = (s32[512]{0:T(512)S(1)}, s32[512]{0:T(512)}, u32[]{:S(2)}) copy-start(s32[512]{0:T(512)} %param.16) | copy-start | bytes 6148
  54.0 0.7 copy-start.4
  54.0 0.7 copy-start.8
  54.0 0.7 copy-start.9
  78.3 13.2 %collective-permute-start.12 = (f32[2,24,512]{2,1,0:T(8,128)S(1)}, f32[2,24,512]{2,1,0:T(8,128)S(1)}, u32[]{:S(2)}, u32[]{:S(2)}) collective-permute-start(f32[2,24,512]{2,1,0:T(8,128)S(1)} %get-tuple-element.26), channel_id=1, source_target_pairs={{0,128},{32,160},{64,192},{96,224},{128,0},{160,32},{192,64},{224,... | collective-permute-start | bytes 294920 | tf_op jit(solution)/shard_map/ppermute | solution.py:306
  80.4 11.1 %collective-permute-start.11 = (f32[2,24,512]{2,1,0:T(8,128)S(1)}, f32[2,24,512]{2,1,0:T(8,128)S(1)}, u32[]{:S(2)}, u32[]{:S(2)}) collective-permute-start(f32[2,24,512]{2,1,0:T(8,128)S(1)} %get-tuple-element.27), channel_id=1, source_target_pairs={{0,64},{32,96},{64,128},{96,160},{128,192},{160,224},{192,0},{224,... | collective-permute-start | bytes 294920 | tf_op jit(solution)/shard_map/ppermute | solution.py:306
  82.2 9.3 %collective-permute-start.10 = (f32[2,24,512]{2,1,0:T(8,128)S(1)}, f32[2,24,512]{2,1,0:T(8,128)S(1)}, u32[]{:S(2)}, u32[]{:S(2)}) collective-permute-start(f32[2,24,512]{2,1,0:T(8,128)S(1)} %get-tuple-element.28), channel_id=1, source_target_pairs={{0,192},{32,224},{64,0},{96,32},{128,64},{160,96},{192,128},{224,1... | collective-permute-start | bytes 294920 | tf_op jit(solution)/shard_map/ppermute | solution.py:306
  91.5 1.3 %collective-permute-start.13 = (f32[24,512]{1,0:T(8,128)S(1)}, f32[24,512]{1,0:T(8,128)S(1)}, u32[]{:S(2)}, u32[]{:S(2)}) collective-permute-start(f32[24,512]{1,0:T(8,128)S(1)} %fusion), channel_id=1, source_target_pairs={{0,32},{32,0},{64,96},{96,64},{128,160},{160,128},{192,224},{224,1... | collective-permute-start | bytes 147464 | tf_op jit(solution)/shard_map/ppermute | solution.py:302

commit v4 on v3

--- a/solution.py
+++ b/solution.py
@@ -74,14 +74,19 @@
     joule_ref[...] = rho * jnp.mean(amps * amps, axis=0, keepdims=True)
 
 
-def row_features(rows):
-    high, low = rows[0:3], rows[3:6]
-    zero = jnp.zeros_like(rows[0:1])
-    one = jnp.ones_like(zero)
-    first = [-2 * high, -2 * high, one, one, one] + [zero] * 6 + [rows[6:7]]
-    second = [-2 * low, -2 * low] + [zero] * 9 + [rows[7:8]]
-    third = [zero] * 15 + [rows[8:9]]
-    return jnp.concatenate(first + second + third, axis=0)
+def rows_body(x1_ref, x3_ref, x2_ref, pair_ref, a_ref, s_ref):
+    blocks = [ref[n] for ref in (x1_ref, x3_ref, x2_ref) for n in range(2)]
+    blocks += [pair_ref[1], pair_ref[0]]
+    width = s_ref.shape[2]
+    for n, block in enumerate(blocks):
+        geo = block[0:16].astype(F32)
+        high, low = -2.0 * geo[0:3], -2.0 * geo[3:6]
+        zero = jnp.zeros((15, width), F32)
+        one = jnp.ones((3, width), F32)
+        parts = [high, high, one, zero[0:6], geo[6:7]]
+        parts += [low, low, zero[0:9], geo[7:8], zero, geo[8:9]]
+        a_ref[:, n * width : (n + 1) * width] = jnp.concatenate(parts, axis=0).astype(BF16)
+        s_ref[n] = jnp.concatenate([geo[9:12] + geo[12:15], zero[0:5]], axis=0)
 
 
 def flux_body(kind, row0, group_rows, cols_ref, a_ref, *refs):
@@ -332,13 +337,12 @@
     ys = [shift_y(own, k) for k in (1, 3)]
     pair = jnp.stack([own, core_swap(own)])
     late, pair = lax.optimization_barrier((own, pair))
-    others = [shift_x(pair, k) for k in (1, 3, 2)]
+    others = [shift_x(pair, k) for k in (2, 3, 1)][::-1]
     column = jnp.stack([late] + ys + [shift_y(late, 2)])
 
-    rows = jnp.concatenate(others + [pair[::-1]], axis=0)
-    seg = rows[:, 9:12].astype(F32) + rows[:, 12:15].astype(F32)
-    seg = jnp.concatenate([seg, jnp.zeros((8, 5, seg.shape[2]), F32)], axis=1)
-    a = row_features(rows.transpose(1, 0, 2).reshape(32, -1))
+    a, seg = small_call(
+        rows_body, (*others, pair), [((48, 8 * width), BF16), ((8, 8, width), F32)], "rows"
+    )
     count = a.shape[1]
     far = swap_z(column, 4)
     acc = flux_call("first", column[:2], a, rows=count, group_rows=2048, step_chunks=2)
@@ -354,7 +358,7 @@
         warmer_kelvin_gain, region_threshold_kelvin,
         rows=3072, group_rows=1024, step_chunks=8,
     )
-    sent = [shift_x(away[2 * n : 2 * n + 2], -k) for n, k in enumerate((1, 3, 2))]
+    sent = [shift_x(away[2 * n : 2 * n + 2], -k) for n, k in ((2, 2), (1, 3), (0, 1))][::-1]
     mine = flux_call(
         "mine", near, a, acc, seg, kk, row0=3072, rows=1024, group_rows=1024, step_chunks=8
     )

time: 122 us -> 121 us (level)
  starting transfers between devices: 26 us -> 23.9 us
    ppermute x6, starting transfers between devices: 11 us -> 8.87 us  [shift_x(): return lax.ppermute(value, 'row', [(i, (i + 2 * k) % 8) for i in range(8)])]
    all_to_all x1, blocking collectives: 10.9 us -> 12.1 us  [local(): stats = lax.all_to_all(stats, ('row', 'col'), 0, 0, axis_index_groups=X_Y)]
  transfers between devices with their start and end apart: 14 -> 14, of which waited for: 2 -> 2; matrix products, arithmetic and copies ran while one was open for 1% -> 0% of each run, Pallas kernels for 31% -> 31%
where the time goes in v4:
time: 121 us
  Pallas kernels  64 us (53%)
  blocking collectives  26.9 us (22%)
  starting transfers between devices  23.9 us (20%)
  waiting for transfers between devices  2.5 us (2%)
  local copies, waits for them, and re-layouts  2.19 us (2%)
    pallas_call x5, Pallas kernels, flux_call(): pl.pallas_call(functools.partial(flux_body, kind, row0, group_rows), grid...  61.1 us
    all_to_all x1, blocking collectives, local(): lax.all_to_all(stats, ('row', 'col'), 0, 0, axis_index_groups=CORE_Z)  14.8 us
    all_to_all x1, blocking collectives, local(): stats = lax.all_to_all(stats, ('row', 'col'), 0, 0, axis_index_groups=X_Y)  12.1 us
    ppermute x3, starting transfers between devices, swap_z(): return lax.ppermute(value, 'col', [(i, i ^ k) for i in range(32)])  9.44 us
    ppermute x6, starting transfers between devices, shift_x(): return lax.ppermute(value, 'row', [(i, (i + 2 * k) % 8) for i in range(8)])  8.87 us
    ppermute x3, starting transfers between devices, shift_y(): lax.ppermute(value, 'col', [(i, (i + 8 * k) % 32) for i in range(32)])  5.38 us
    pallas_call x1, Pallas kernels, end_call(): pl.pallas_call(end_body, in_specs=[whole] * 3, out_specs=[whole] * 3, out...  2.42 us
  transfers between devices with their start and end apart: 14, of which 2 were waited for; matrix products, arithmetic and copies ran while one was open for 0% of the time, Pallas kernels for 31%

profile of v4, /device:TPU:32, one launch (start us, length us, event | category | flops | bytes accessed | tf_op | source)
XLA Modules:
  0.0 120.5 jit_solution(14671144939357145835)
XLA Ops:
  0.6 0.7 copy-done.1
  1.4 0.7 copy-done.3
  2.1 0.1 collective-permute-start
  2.2 1.7 %collective-permute-start.1 = (bf16[32,512]{1,0:T(8,128)(2,1)S(1)}, bf16[32,512]{1,0:T(8,128)(2,1)S(1)}, u32[]{:S(2)}, u32[]{:S(2)}) collective-permute-start(bf16[32,512]{1,0:T(8,128)(2,1)S(1)} %payload.1), channel_id=1, source_target_pairs={{0,8},{1,9},{2,10},{3,11},{4,12},{5,13},{6,14},{7,15},{8,16},{9,17... | collective-permute-start | bytes 98312 | tf_op jit(solution)/shard_map/ppermute | solution.py:315
  3.9 1.7 %collective-permute-start.2 = (bf16[32,512]{1,0:T(8,128)(2,1)S(1)}, bf16[32,512]{1,0:T(8,128)(2,1)S(1)}, u32[]{:S(2)}, u32[]{:S(2)}) collective-permute-start(bf16[32,512]{1,0:T(8,128)(2,1)S(1)} %payload.1), channel_id=1, source_target_pairs={{0,24},{1,25},{2,26},{3,27},{4,28},{5,29},{6,30},{7,31},{8,0},{9,1... | collective-permute-start | bytes 98312 | tf_op jit(solution)/shard_map/ppermute | solution.py:315
  5.6 2.1 %collective-permute-start.3 = (bf16[32,512]{1,0:T(8,128)(2,1)S(1)}, bf16[32,512]{1,0:T(8,128)(2,1)S(1)}, u32[]{:S(2)}, u32[]{:S(2)}) collective-permute-start(bf16[32,512]{1,0:T(8,128)(2,1)S(1)} %payload.1), channel_id=1, source_target_pairs={{0,16},{1,17},{2,18},{3,19},{4,20},{5,21},{6,22},{7,23},{8,24},{9,... | collective-permute-start | bytes 98312 | tf_op jit(solution)/shard_map/ppermute | solution.py:315
  7.7 1.5 %collective-permute-start.7 = (bf16[2,32,512]{2,1,0:T(8,128)(2,1)S(1)}, bf16[2,32,512]{2,1,0:T(8,128)(2,1)S(1)}, u32[]{:S(2)}, u32[]{:S(2)}) collective-permute-start(bf16[2,32,512]{2,1,0:T(8,128)(2,1)S(1)} %pad_maximum_fusion.2.pair_ref), channel_id=1, source_target_pairs={{0,64},{32,96},{64,128},{96,160},{128,192},{160,224},{192,0},{224,... | collective-permute-start | bytes 196616 | tf_op jit(solution)/shard_map/ppermute | solution.py:311
  9.1 1.7 %collective-permute-start.8 = (bf16[2,32,512]{2,1,0:T(8,128)(2,1)S(1)}, bf16[2,32,512]{2,1,0:T(8,128)(2,1)S(1)}, u32[]{:S(2)}, u32[]{:S(2)}) collective-permute-start(bf16[2,32,512]{2,1,0:T(8,128)(2,1)S(1)} %pad_maximum_fusion.2.pair_ref), channel_id=1, source_target_pairs={{0,192},{32,224},{64,0},{96,32},{128,64},{160,96},{192,128},{224,1... | collective-permute-start | bytes 196616 | tf_op jit(solution)/shard_map/ppermute | solution.py:311
  10.9 1.8 %collective-permute-start.9 = (bf16[2,32,512]{2,1,0:T(8,128)(2,1)S(1)}, bf16[2,32,512]{2,1,0:T(8,128)(2,1)S(1)}, u32[]{:S(2)}, u32[]{:S(2)}) collective-permute-start(bf16[2,32,512]{2,1,0:T(8,128)(2,1)S(1)} %pad_maximum_fusion.2.pair_ref), channel_id=1, source_target_pairs={{0,128},{32,160},{64,192},{96,224},{128,0},{160,32},{192,64},{224,... | collective-permute-start | bytes 196616 | tf_op jit(solution)/shard_map/ppermute | solution.py:311
  12.8 6.4 %collective-permute-start.4 = (bf16[4,32,512]{2,1,0:T(8,128)(2,1)S(1)}, bf16[4,32,512]{2,1,0:T(8,128)(2,1)S(1)}, u32[]{:S(2)}, u32[]{:S(2)}) collective-permute-start(bf16[4,32,512]{2,1,0:T(8,128)(2,1)S(1)} %pad_maximum_fusion.1), channel_id=1, source_target_pairs={{0,4},{1,5},{2,6},{3,7},{4,0},{5,1},{6,2},{7,3},{8,12},{9,13},{10,... | collective-permute-start | bytes 393224 | tf_op jit(solution)/shard_map/ppermute | solution.py:319
  19.2 0.1 rows.1
  19.3 4.0 %flux.5.refs_0_ = f32[48,4096]{1,0:T(8,128)S(1)} custom-call(bf16[2,32,512]{2,1,0:T(8,128)(2,1)S(1)} %pad_maximum_fusion.3.cols_ref, bf16[48,4096]{1,0:T(8,128)(2,1)S(1)} %get-tuple-element.19.a_ref), custom_call_target="tpu_custom_call" | custom-call | flops 4294967296 | bytes 2097152 | tf_op jit(solution)/shard_map/flux/pallas_call | solution.py:204
  23.3 1.3 %collective-permute-done.4 = bf16[4,32,512]{2,1,0:T(8,128)(2,1)S(1)} collective-permute-done((bf16[4,32,512]{2,1,0:T(8,128)(2,1)S(1)}, bf16[4,32,512]{2,1,0:T(8,128)(2,1)S(1)}, u32[]{:S(2)}, u32[]{:S(2)}) %collective-permute-start.4) | collective-permute-done | bytes 131104 | tf_op jit(solution)/shard_map/ppermute | solution.py:319
  24.5 1.8 %collective-permute-start.5 = (bf16[8,32,512]{2,1,0:T(8,128)(2,1)S(1)}, bf16[8,32,512]{2,1,0:T(8,128)(2,1)S(1)}, u32[]{:S(2)}, u32[]{:S(2)}) collective-permute-start(bf16[8,32,512]{2,1,0:T(8,128)(2,1)S(1)} %get-tuple-element.33), channel_id=1, source_target_pairs={{0,2},{1,3},{2,0},{3,1},{4,6},{5,7},{6,4},{7,5},{8,10},{9,11},{10,... | collective-permute-start | bytes 786440 | tf_op jit(solution)/shard_map/ppermute | solution.py:319
  26.4 11.1 %flux.6.refs_0_ = f32[48,4096]{1,0:T(8,128)S(1)} custom-call(bf16[6,32,512]{2,1,0:T(8,128)(2,1)S(1)} %pad_maximum_fusion.cols_ref, bf16[48,4096]{1,0:T(8,128)(2,1)S(1)} %get-tuple-element.19.a_ref, f32[48,4096]{1,0:T(8,128)S(1)} %flux.5.refs_0_), custom_call_target="tpu_custom_call" | custom-call | flops 12884901888 | bytes 2097152 | tf_op jit(solution)/shard_map/flux/pallas_call | solution.py:204
  37.6 0.0 copy-start.2
  37.6 1.2 %collective-permute-start.6 = (bf16[16,32,512]{2,1,0:T(8,128)(2,1)S(1)}, bf16[16,32,512]{2,1,0:T(8,128)(2,1)S(1)}, u32[]{:S(2)}, u32[]{:S(2)}) collective-permute-start(bf16[16,32,512]{2,1,0:T(8,128)(2,1)S(1)} %constant_dynamic-update-slice_fusion.5), channel_id=1, source_target_pairs={{0,1},{1,0},{2,3},{3,2},{4,5},{5,4},{6,7},{7,6},{8,9},{9,8},{10,11... | collective-permute-start | bytes 1572872 | tf_op jit(solution)/shard_map/ppermute | solution.py:319
  38.8 14.6 %flux.7.refs_0_ = f32[48,4096]{1,0:T(8,128)S(1)} custom-call(bf16[8,32,512]{2,1,0:T(8,128)(2,1)S(1)} %collective-permute-done.5.cols_ref, bf16[48,4096]{1,0:T(8,128)(2,1)S(1)} %get-tuple-element.19.a_ref, f32[48,4096]{1,0:T(8,128)S(1)} %flux.6.refs_0_), custom_call_target="tpu_custom_call" | custom-call | flops 17179869184 | bytes 2097152 | tf_op jit(solution)/shard_map/flux/pallas_call | solution.py:204
  53.4 0.0 copy-start.4
  53.5 0.6 copy-done.4
  54.1 23.6 %flux.8 = (f32[6,24,512]{2,1,0:T(8,128)S(1)}, f32[64,64]{1,0:T(8,128)S(1)}, f32[1,512]{1,0:T(1,128)S(1)}, f32[1,512]{1,0:T(1,128)}) custom-call(bf16[16,32,512]{2,1,0:T(8,128)(2,1)S(1)} %collective-permute-done.6.cols_ref, bf16[48,4096]{1,0:T(8,128)(2,1)S(1)} %get-tuple-element.19.a_ref, f32[48,4096]{1,0:T(8,128)S(1)} %flux.7.refs_0_, ...), custom_call_target="tpu_custom_call" | custom-call | flops 25769803776 | bytes 1572864 | tf_op jit(solution)/shard_map/flux/pallas_call | solution.py:204
  77.7 1.2 %collective-permute-start.10 = (f32[2,24,512]{2,1,0:T(8,128)S(1)}, f32[2,24,512]{2,1,0:T(8,128)S(1)}, u32[]{:S(2)}, u32[]{:S(2)}) collective-permute-start(f32[2,24,512]{2,1,0:T(8,128)S(1)} %get-tuple-element.32), channel_id=1, source_target_pairs={{0,192},{32,224},{64,0},{96,32},{128,64},{160,96},{192,128},{224,1... | collective-permute-start | bytes 294920 | tf_op jit(solution)/shard_map/ppermute | solution.py:311
  78.9 0.9 collective-permute-start.11
  79.8 1.7 %collective-permute-start.12 = (f32[2,24,512]{2,1,0:T(8,128)S(1)}, f32[2,24,512]{2,1,0:T(8,128)S(1)}, u32[]{:S(2)}, u32[]{:S(2)}) collective-permute-start(f32[2,24,512]{2,1,0:T(8,128)S(1)} %get-tuple-element.30), channel_id=1, source_target_pairs={{0,128},{32,160},{64,192},{96,224},{128,0},{160,32},{192,64},{224,... | collective-permute-start | bytes 294920 | tf_op jit(solution)/shard_map/ppermute | solution.py:311
  81.5 7.8 %flux.9.mine_ref = f32[2,24,512]{2,1,0:T(8,128)S(1)} custom-call(bf16[16,32,512]{2,1,0:T(8,128)(2,1)S(1)} %collective-permute-done.6.cols_ref, bf16[48,4096]{1,0:T(8,128)(2,1)S(1)} %get-tuple-element.19.a_ref, f32[48,4096]{1,0:T(8,128)S(1)} %flux.7.refs_0_, f32[8,8,512]{2,1,0:T(8,128)S(1)} %get-tuple-element.20.refs_1_, f32[64,64]{1,0:T(8,128)S(1)} %get-tuple-element.22.refs_2_), custom_call_target="tpu_custom_call" | custom-call | flops 8589934592 | bytes 524288 | tf_op jit(solution)/shard_map/flux/pallas_call | solution.py:204
  89.4 0.1 collective-permute-start.13
  89.5 1.2 %collective-permute-done.13.swap_ref = f32[24,512]{1,0:T(8,128)S(1)} collective-permute-done((f32[24,512]{1,0:T(8,128)S(1)}, f32[24,512]{1,0:T(8,128)S(1)}, u32[]{:S(2)}, u32[]{:S(2)}) %collective-permute-start.13) | collective-permute-done | bytes 49184 | tf_op jit(solution)/shard_map/ppermute | solution.py:307
  90.8 0.3 image.1
  91.1 14.8 %all_to_all.10.in_ref = f32[16,16,128]{2,1,0:T(8,128)S(1)} all-to-all(f32[16,16,128]{2,1,0:T(8,128)S(1)} %get-tuple-element.25), channel_id=1, replica_groups={{0,1,2,3,4,5,6,7,32,33,34,35,36,37,38,39},{8,9,10,11,12,13,14,15,40,41,..., dimensions={0} | all-to-all | bytes 262144 | tf_op jit(solution)/shard_map/all_to_all | solution.py:373
  105.9 0.1 middle.1
  106.0 12.1 %all_to_all.11.stats_ref = f32[16,24,128]{2,1,0:T(8,128)S(1)} all-to-all(f32[16,24,128]{2,1,0:T(8,128)S(1)} %middle.1), channel_id=1, replica_groups={{0,8,16,24,64,72,80,88,128,136,144,152,192,200,208,216},{1,9,17,25,65,7..., dimensions={0} | all-to-all | bytes 393216 | tf_op jit(solution)/shard_map/all_to_all | solution.py:375
  118.1 2.4 %finish.1 = (f32[16,512]{1,0:T(8,128)}, f32[16,64]{1,0:T(8,128)}, f32[16,16]{1,0:T(8,128)}) custom-call(f32[64,512]{1,0:T(8,128)S(1)} %copy-done, f32[16,512]{1,0:T(8,128)S(1)} %get-tuple-element.24.image_ref, f32[16,24,128]{2,1,0:T(8,128)S(1)} %all_to_all.11.stats_ref), custom_call_target="tpu_custom_call" | custom-call | tf_op jit(solution)/shard_map/finish/pallas_call | solution.py:291
  (40 shorter events, 0.3 us)
Async XLA Ops:
  0.6 0.8 copy-start.1
  1.4 0.7 copy-start.3
  2.1 3.4 %collective-permute-start = (bf16[32,512]{1,0:T(8,128)(2,1)S(1)}, bf16[32,512]{1,0:T(8,128)(2,1)S(1)}, u32[]{:S(2)}, u32[]{:S(2)}) collective-permute-start(bf16[32,512]{1,0:T(8,128)(2,1)S(1)} %payload.1), channel_id=1, source_target_pairs={{0,32},{32,0},{64,96},{96,64},{128,160},{160,128},{192,224},{224,1... | collective-permute-start | bytes 98312 | tf_op jit(solution)/shard_map/ppermute | solution.py:307
  2.2 8.7 %collective-permute-start.1 = (bf16[32,512]{1,0:T(8,128)(2,1)S(1)}, bf16[32,512]{1,0:T(8,128)(2,1)S(1)}, u32[]{:S(2)}, u32[]{:S(2)}) collective-permute-start(bf16[32,512]{1,0:T(8,128)(2,1)S(1)} %payload.1), channel_id=1, source_target_pairs={{0,8},{1,9},{2,10},{3,11},{4,12},{5,13},{6,14},{7,15},{8,16},{9,17... | collective-permute-start | bytes 98312 | tf_op jit(solution)/shard_map/ppermute | solution.py:315
  3.9 8.8 %collective-permute-start.2 = (bf16[32,512]{1,0:T(8,128)(2,1)S(1)}, bf16[32,512]{1,0:T(8,128)(2,1)S(1)}, u32[]{:S(2)}, u32[]{:S(2)}) collective-permute-start(bf16[32,512]{1,0:T(8,128)(2,1)S(1)} %payload.1), channel_id=1, source_target_pairs={{0,24},{1,25},{2,26},{3,27},{4,28},{5,29},{6,30},{7,31},{8,0},{9,1... | collective-permute-start | bytes 98312 | tf_op jit(solution)/shard_map/ppermute | solution.py:315
  5.6 7.2 %collective-permute-start.3 = (bf16[32,512]{1,0:T(8,128)(2,1)S(1)}, bf16[32,512]{1,0:T(8,128)(2,1)S(1)}, u32[]{:S(2)}, u32[]{:S(2)}) collective-permute-start(bf16[32,512]{1,0:T(8,128)(2,1)S(1)} %payload.1), channel_id=1, source_target_pairs={{0,16},{1,17},{2,18},{3,19},{4,20},{5,21},{6,22},{7,23},{8,24},{9,... | collective-permute-start | bytes 98312 | tf_op jit(solution)/shard_map/ppermute | solution.py:315
  7.7 11.5 %collective-permute-start.7 = (bf16[2,32,512]{2,1,0:T(8,128)(2,1)S(1)}, bf16[2,32,512]{2,1,0:T(8,128)(2,1)S(1)}, u32[]{:S(2)}, u32[]{:S(2)}) collective-permute-start(bf16[2,32,512]{2,1,0:T(8,128)(2,1)S(1)} %pad_maximum_fusion.2.pair_ref), channel_id=1, source_target_pairs={{0,64},{32,96},{64,128},{96,160},{128,192},{160,224},{192,0},{224,... | collective-permute-start | bytes 196616 | tf_op jit(solution)/shard_map/ppermute | solution.py:311
  9.1 10.0 %collective-permute-start.8 = (bf16[2,32,512]{2,1,0:T(8,128)(2,1)S(1)}, bf16[2,32,512]{2,1,0:T(8,128)(2,1)S(1)}, u32[]{:S(2)}, u32[]{:S(2)}) collective-permute-start(bf16[2,32,512]{2,1,0:T(8,128)(2,1)S(1)} %pad_maximum_fusion.2.pair_ref), channel_id=1, source_target_pairs={{0,192},{32,224},{64,0},{96,32},{128,64},{160,96},{192,128},{224,1... | collective-permute-start | bytes 196616 | tf_op jit(solution)/shard_map/ppermute | solution.py:311
  10.9 8.3 %collective-permute-start.9 = (bf16[2,32,512]{2,1,0:T(8,128)(2,1)S(1)}, bf16[2,32,512]{2,1,0:T(8,128)(2,1)S(1)}, u32[]{:S(2)}, u32[]{:S(2)}) collective-permute-start(bf16[2,32,512]{2,1,0:T(8,128)(2,1)S(1)} %pad_maximum_fusion.2.pair_ref), channel_id=1, source_target_pairs={{0,128},{32,160},{64,192},{96,224},{128,0},{160,32},{192,64},{224,... | collective-permute-start | bytes 196616 | tf_op jit(solution)/shard_map/ppermute | solution.py:311
  12.8 11.7 %collective-permute-start.4 = (bf16[4,32,512]{2,1,0:T(8,128)(2,1)S(1)}, bf16[4,32,512]{2,1,0:T(8,128)(2,1)S(1)}, u32[]{:S(2)}, u32[]{:S(2)}) collective-permute-start(bf16[4,32,512]{2,1,0:T(8,128)(2,1)S(1)} %pad_maximum_fusion.1), channel_id=1, source_target_pairs={{0,4},{1,5},{2,6},{3,7},{4,0},{5,1},{6,2},{7,3},{8,12},{9,13},{10,... | collective-permute-start | bytes 393224 | tf_op jit(solution)/shard_map/ppermute | solution.py:319
  24.5 13.0 %collective-permute-start.5 = (bf16[8,32,512]{2,1,0:T(8,128)(2,1)S(1)}, bf16[8,32,512]{2,1,0:T(8,128)(2,1)S(1)}, u32[]{:S(2)}, u32[]{:S(2)}) collective-permute-start(bf16[8,32,512]{2,1,0:T(8,128)(2,1)S(1)} %get-tuple-element.33), channel_id=1, source_target_pairs={{0,2},{1,3},{2,0},{3,1},{4,6},{5,7},{6,4},{7,5},{8,10},{9,11},{10,... | collective-permute-start | bytes 786440 | tf_op jit(solution)/shard_map/ppermute | solution.py:319
  37.5 15.9 %copy-start = (f32[64,512]{1,0:T(8,128)S(1)}, f32[64,512]{1,0:T(8,128)}, u32[]{:S(2)}) copy-start(f32[64,512]{1,0:T(8,128)} %krylov_ref.3) | copy-start | bytes 393220
  37.6 15.9 %copy-start.2 = (f32[16,512]{1,0:T(8,128)S(1)}, f32[16,512]{1,0:T(8,128)}, u32[]{:S(2)}) copy-start(f32[16,512]{1,0:T(8,128)} %amps_ref.3) | copy-start | bytes 98308
  37.6 15.8 %collective-permute-start.6 = (bf16[16,32,512]{2,1,0:T(8,128)(2,1)S(1)}, bf16[16,32,512]{2,1,0:T(8,128)(2,1)S(1)}, u32[]{:S(2)}, u32[]{:S(2)}) collective-permute-start(bf16[16,32,512]{2,1,0:T(8,128)(2,1)S(1)} %constant_dynamic-update-slice_fusion.5), channel_id=1, source_target_pairs={{0,1},{1,0},{2,3},{3,2},{4,5},{5,4},{6,7},{7,6},{8,9},{9,8},{10,11... | collective-permute-start | bytes 1572872 | tf_op jit(solution)/shard_map/ppermute | solution.py:319
  38.8 14.6 %copy-start.5 = (f32[512]{0:T(512)S(1)}, f32[512]{0:T(512)}, u32[]{:S(2)}) copy-start(f32[512]{0:T(512)} %param.13) | copy-start | bytes 6148
  38.8 14.6 %copy-start.6 = (s32[512]{0:T(512)S(1)}, s32[512]{0:T(512)}, u32[]{:S(2)}) copy-start(s32[512]{0:T(512)} %param.14) | copy-start | bytes 6148
  38.8 14.7 %copy-start.7 = (s32[512]{0:T(512)S(1)}, s32[512]{0:T(512)}, u32[]{:S(2)}) copy-start(s32[512]{0:T(512)} %param.16) | copy-start | bytes 6148
  53.4 0.7 copy-start.4
  53.4 0.7 copy-start.8
  53.4 0.7 copy-start.9
  77.7 11.7 %collective-permute-start.10 = (f32[2,24,512]{2,1,0:T(8,128)S(1)}, f32[2,24,512]{2,1,0:T(8,128)S(1)}, u32[]{:S(2)}, u32[]{:S(2)}) collective-permute-start(f32[2,24,512]{2,1,0:T(8,128)S(1)} %get-tuple-element.32), channel_id=1, source_target_pairs={{0,192},{32,224},{64,0},{96,32},{128,64},{160,96},{192,128},{224,1... | collective-permute-start | bytes 294920 | tf_op jit(solution)/shard_map/ppermute | solution.py:311
  78.9 10.4 %collective-permute-start.11 = (f32[2,24,512]{2,1,0:T(8,128)S(1)}, f32[2,24,512]{2,1,0:T(8,128)S(1)}, u32[]{:S(2)}, u32[]{:S(2)}) collective-permute-start(f32[2,24,512]{2,1,0:T(8,128)S(1)} %get-tuple-element.31), channel_id=1, source_target_pairs={{0,64},{32,96},{64,128},{96,160},{128,192},{160,224},{192,0},{224,... | collective-permute-start | bytes 294920 | tf_op jit(solution)/shard_map/ppermute | solution.py:311
  79.8 9.6 %collective-permute-start.12 = (f32[2,24,512]{2,1,0:T(8,128)S(1)}, f32[2,24,512]{2,1,0:T(8,128)S(1)}, u32[]{:S(2)}, u32[]{:S(2)}) collective-permute-start(f32[2,24,512]{2,1,0:T(8,128)S(1)} %get-tuple-element.30), channel_id=1, source_target_pairs={{0,128},{32,160},{64,192},{96,224},{128,0},{160,32},{192,64},{224,... | collective-permute-start | bytes 294920 | tf_op jit(solution)/shard_map/ppermute | solution.py:311
  89.4 1.3 %collective-permute-start.13 = (f32[24,512]{1,0:T(8,128)S(1)}, f32[24,512]{1,0:T(8,128)S(1)}, u32[]{:S(2)}, u32[]{:S(2)}) collective-permute-start(f32[24,512]{1,0:T(8,128)S(1)} %fusion), channel_id=1, source_target_pairs={{0,32},{32,0},{64,96},{96,64},{128,160},{160,128},{192,224},{224,1... | collective-permute-start | bytes 147464 | tf_op jit(solution)/shard_map/ppermute | solution.py:307

commit v5 on v4

--- a/solution.py
+++ b/solution.py
@@ -27,14 +27,14 @@
 BLOCKS = ((1, 0), (1, 1), (3, 0), (3, 1), (2, 0), (2, 1), (0, 1), (0, 0))
 
 
-def small_call(body, args, shapes, name, limit=16):
+def small_call(body, args, shapes, name):
     whole = pl.BlockSpec(memory_space=pltpu.VMEM)
     return pl.pallas_call(
         body,
         in_specs=[whole] * len(args),
         out_specs=[whole] * len(shapes),
         out_shape=[jax.ShapeDtypeStruct(shape, dtype) for shape, dtype in shapes],
-        compiler_params=pltpu.CompilerParams(vmem_limit_bytes=limit * 2**20),
+        compiler_params=pltpu.CompilerParams(vmem_limit_bytes=16 * 2**20),
         name=name,
     )(*args)
 
@@ -62,8 +62,9 @@
 def heat(kelvin_ref, ohmic_ref, warmer_ref, region_ref, amps_ref, gain_ref, limit_ref, rho_ref, joule_ref):
     def entries(ids, table_ref):
         out = jnp.zeros(ids.shape, F32)
-        for level in range(table_ref.shape[0]):
-            out = jnp.where(ids == level, table_ref[level], out)
+        table = table_ref[...]
+        for level in range(table.shape[1]):
+            out = jnp.where(ids == level, table[:, level : level + 1], out)
         return out
 
     warm = entries(warmer_ref[...], gain_ref)
@@ -74,7 +75,9 @@
     joule_ref[...] = rho * jnp.mean(amps * amps, axis=0, keepdims=True)
 
 
-def rows_body(x1_ref, x3_ref, x2_ref, pair_ref, a_ref, s_ref):
+def rows_body(x1_ref, x3_ref, x2_ref, pair_ref, *refs):
+    a_ref, s_ref = refs[7:9]
+    heat(*refs[:7], *refs[9:])
     blocks = [ref[n] for ref in (x1_ref, x3_ref, x2_ref) for n in range(2)]
     blocks += [pair_ref[1], pair_ref[0]]
     width = s_ref.shape[2]
@@ -97,12 +100,12 @@
     if finish:
         s_ref, refs = refs[0], refs[1:]
     if kind == "away":
-        krylov_ref, heat_in, refs = refs[0], refs[1:8], refs[8:]
+        krylov_ref, refs = refs[0], refs[1:]
     if kind == "mine":
         kk_ref, refs = refs[0], refs[1:]
     out_ref, refs = refs[0], refs[1:]
     if kind == "away":
-        kk_ref, heat_out, refs = refs[0], refs[1:3], refs[3:]
+        kk_ref, refs = refs[0], refs[1:]
     b_scr, w_scr = refs[:2]
     total = refs[2] if finish else out_ref
     step, group = pl.program_id(0), pl.program_id(1)
@@ -172,7 +175,6 @@
                 kk_ref[...] = lax.dot_general(
                     krylov, krylov, NT, precision=HI, preferred_element_type=F32
                 )
-                heat(*heat_in, *heat_out)
             me = lax.axis_index("row")
             for n in range(out_ref.shape[0]):
                 shift, swap = BLOCKS[row0 // width + n]
@@ -185,7 +187,6 @@
     chunks, _, width = cols.shape
     finish = kind in ("away", "mine")
     whole = pl.BlockSpec(memory_space=pltpu.VMEM)
-    scalar = pl.BlockSpec(memory_space=pltpu.SMEM)
     args = [cols, a, *more]
     specs = [whole] * len(args)
     if finish:
@@ -193,9 +194,7 @@
     else:
         shapes = [jax.ShapeDtypeStruct((3 * SECTIONS, rows), F32)]
     if kind == "away":
-        specs[-2:] = [scalar] * 2
-        shapes += [jax.ShapeDtypeStruct((64, 64), F32)]
-        shapes += [jax.ShapeDtypeStruct((1, width), F32)] * 2
+        shapes.append(jax.ShapeDtypeStruct((64, 64), F32))
     span = step_chunks * width
     scratch = [pltpu.VMEM((span, 48), BF16), pltpu.VMEM((48, span), BF16)]
     if finish:
@@ -340,8 +339,13 @@
     others = [shift_x(pair, k) for k in (2, 3, 1)][::-1]
     column = jnp.stack([late] + ys + [shift_y(late, 2)])
 
-    a, seg = small_call(
-        rows_body, (*others, pair), [((48, 8 * width), BF16), ((8, 8, width), F32)], "rows"
+    flat = (strand_kelvin, strand_ohmic_value, strand_warmer_slot, strand_region_slot)
+    a, seg, rho, joule = small_call(
+        rows_body,
+        (*others, pair, *(v[None] for v in flat), strand_amperes_panel, warmer_kelvin_gain[None],
+         region_threshold_kelvin[None]),
+        [((48, 8 * width), BF16), ((8, 8, width), F32), ((1, width), F32), ((1, width), F32)],
+        "rows",
     )
     count = a.shape[1]
     far = swap_z(column, 4)
@@ -352,15 +356,12 @@
     whole = jnp.concatenate([whole, middle], axis=0)
     near = swap_z(whole, 1)
     acc = flux_call("next", middle, a, acc, rows=count, group_rows=1024, step_chunks=8)
-    flat = (strand_kelvin, strand_ohmic_value, strand_warmer_slot, strand_region_slot)
-    away, kk, rho, joule = flux_call(
-        "away", near, a, acc, seg, krylov_vectors, *(v[None] for v in flat), strand_amperes_panel,
-        warmer_kelvin_gain, region_threshold_kelvin,
-        rows=3072, group_rows=1024, step_chunks=8,
+    away, kk = flux_call(
+        "away", near, a, acc, seg, krylov_vectors, rows=3072, group_rows=1024, step_chunks=16
     )
     sent = [shift_x(away[2 * n : 2 * n + 2], -k) for n, k in ((2, 2), (1, 3), (0, 1))][::-1]
     mine = flux_call(
-        "mine", near, a, acc, seg, kk, row0=3072, rows=1024, group_rows=1024, step_chunks=8
+        "mine", near, a, acc, seg, kk, row0=3072, rows=1024, group_rows=1024, step_chunks=16
     )
     swapped = core_swap(sent[0][1] + sent[1][1] + sent[2][1] + mine[0])
 

time: 121 us -> 118 us (0.975)
  Pallas kernels: 64 us -> 62.4 us
  waiting for transfers between devices: 2.5 us -> 1.25 us
    pallas_call x5, Pallas kernels: 61.1 us -> 58.8 us  [flux_call(): pl.pallas_call(functools.partial(flux_body, kind, row0, group_rows), grid...]
    ppermute x3, waiting for transfers between devices: 1.26 us -> 0.01 us  [swap_z(): return lax.ppermute(value, 'col', [(i, i ^ k) for i in range(32)])]
  transfers between devices with their start and end apart: 14 -> 14, of which waited for: 2 -> 1; matrix products, arithmetic and copies ran while one was open for 0% -> 0% of each run, Pallas kernels for 31% -> 32%
where the time goes in v5:
time: 118 us
  Pallas kernels  62.4 us (53%)
  blocking collectives  26.4 us (22%)
  starting transfers between devices  24.2 us (21%)
  local copies, waits for them, and re-layouts  2.26 us (2%)
  waiting for transfers between devices  1.25 us (1%)
    pallas_call x5, Pallas kernels, flux_call(): pl.pallas_call(functools.partial(flux_body, kind, row0, group_rows), grid...  58.8 us
    all_to_all x1, blocking collectives, local(): lax.all_to_all(stats, ('row', 'col'), 0, 0, axis_index_groups=CORE_Z)  14.3 us
    all_to_all x1, blocking collectives, local(): stats = lax.all_to_all(stats, ('row', 'col'), 0, 0, axis_index_groups=X_Y)  12.1 us
    ppermute x3, starting transfers between devices, swap_z(): return lax.ppermute(value, 'col', [(i, i ^ k) for i in range(32)])  9.78 us
    ppermute x6, starting transfers between devices, shift_x(): return lax.ppermute(value, 'row', [(i, (i + 2 * k) % 8) for i in range(8)])  8.87 us
    ppermute x3, starting transfers between devices, shift_y(): lax.ppermute(value, 'col', [(i, (i + 8 * k) % 32) for i in range(32)])  5.38 us
    pallas_call x1, Pallas kernels, end_call(): pl.pallas_call(end_body, in_specs=[whole] * 3, out_specs=[whole] * 3, out...  2.42 us
  transfers between devices with their start and end apart: 14, of which 1 were waited for; matrix products, arithmetic and copies ran while one was open for 0% of the time, Pallas kernels for 32%

profile of v5, /device:TPU:32, one launch (start us, length us, event | category | flops | bytes accessed | tf_op | source)
XLA Modules:
  0.0 117.5 jit_solution(3016641799876005138)
XLA Ops:
  0.6 0.0 copy-start.1
  0.6 0.7 copy-done.1
  1.4 0.7 copy-done.3
  2.1 0.1 collective-permute-start
  2.2 1.7 %collective-permute-start.1 = (bf16[32,512]{1,0:T(8,128)(2,1)S(1)}, bf16[32,512]{1,0:T(8,128)(2,1)S(1)}, u32[]{:S(2)}, u32[]{:S(2)}) collective-permute-start(bf16[32,512]{1,0:T(8,128)(2,1)S(1)} %payload.1), channel_id=1, source_target_pairs={{0,8},{1,9},{2,10},{3,11},{4,12},{5,13},{6,14},{7,15},{8,16},{9,17... | collective-permute-start | bytes 98312 | tf_op jit(solution)/shard_map/ppermute | solution.py:314
  3.9 1.7 %collective-permute-start.2 = (bf16[32,512]{1,0:T(8,128)(2,1)S(1)}, bf16[32,512]{1,0:T(8,128)(2,1)S(1)}, u32[]{:S(2)}, u32[]{:S(2)}) collective-permute-start(bf16[32,512]{1,0:T(8,128)(2,1)S(1)} %payload.1), channel_id=1, source_target_pairs={{0,24},{1,25},{2,26},{3,27},{4,28},{5,29},{6,30},{7,31},{8,0},{9,1... | collective-permute-start | bytes 98312 | tf_op jit(solution)/shard_map/ppermute | solution.py:314
  5.6 2.1 %collective-permute-start.3 = (bf16[32,512]{1,0:T(8,128)(2,1)S(1)}, bf16[32,512]{1,0:T(8,128)(2,1)S(1)}, u32[]{:S(2)}, u32[]{:S(2)}) collective-permute-start(bf16[32,512]{1,0:T(8,128)(2,1)S(1)} %payload.1), channel_id=1, source_target_pairs={{0,16},{1,17},{2,18},{3,19},{4,20},{5,21},{6,22},{7,23},{8,24},{9,... | collective-permute-start | bytes 98312 | tf_op jit(solution)/shard_map/ppermute | solution.py:314
  7.7 1.5 %collective-permute-start.7 = (bf16[2,32,512]{2,1,0:T(8,128)(2,1)S(1)}, bf16[2,32,512]{2,1,0:T(8,128)(2,1)S(1)}, u32[]{:S(2)}, u32[]{:S(2)}) collective-permute-start(bf16[2,32,512]{2,1,0:T(8,128)(2,1)S(1)} %pad_maximum_fusion.2.pair_ref), channel_id=1, source_target_pairs={{0,64},{32,96},{64,128},{96,160},{128,192},{160,224},{192,0},{224,... | collective-permute-start | bytes 196616 | tf_op jit(solution)/shard_map/ppermute | solution.py:310
  9.1 1.7 %collective-permute-start.8 = (bf16[2,32,512]{2,1,0:T(8,128)(2,1)S(1)}, bf16[2,32,512]{2,1,0:T(8,128)(2,1)S(1)}, u32[]{:S(2)}, u32[]{:S(2)}) collective-permute-start(bf16[2,32,512]{2,1,0:T(8,128)(2,1)S(1)} %pad_maximum_fusion.2.pair_ref), channel_id=1, source_target_pairs={{0,192},{32,224},{64,0},{96,32},{128,64},{160,96},{192,128},{224,1... | collective-permute-start | bytes 196616 | tf_op jit(solution)/shard_map/ppermute | solution.py:310
  10.9 1.8 %collective-permute-start.9 = (bf16[2,32,512]{2,1,0:T(8,128)(2,1)S(1)}, bf16[2,32,512]{2,1,0:T(8,128)(2,1)S(1)}, u32[]{:S(2)}, u32[]{:S(2)}) collective-permute-start(bf16[2,32,512]{2,1,0:T(8,128)(2,1)S(1)} %pad_maximum_fusion.2.pair_ref), channel_id=1, source_target_pairs={{0,128},{32,160},{64,192},{96,224},{128,0},{160,32},{192,64},{224,... | collective-permute-start | bytes 196616 | tf_op jit(solution)/shard_map/ppermute | solution.py:310
  12.8 6.4 %collective-permute-start.4 = (bf16[4,32,512]{2,1,0:T(8,128)(2,1)S(1)}, bf16[4,32,512]{2,1,0:T(8,128)(2,1)S(1)}, u32[]{:S(2)}, u32[]{:S(2)}) collective-permute-start(bf16[4,32,512]{2,1,0:T(8,128)(2,1)S(1)} %pad_maximum_fusion.1), channel_id=1, source_target_pairs={{0,4},{1,5},{2,6},{3,7},{4,0},{5,1},{6,2},{7,3},{8,12},{9,13},{10,... | collective-permute-start | bytes 393224 | tf_op jit(solution)/shard_map/ppermute | solution.py:318
  19.2 0.0 copy-start.4
  19.2 0.0 copy-start.8
  19.3 0.7 copy-done.2
  20.0 0.7 rows.1
  20.7 3.9 %flux.5.refs_0_ = f32[48,4096]{1,0:T(8,128)S(1)} custom-call(bf16[2,32,512]{2,1,0:T(8,128)(2,1)S(1)} %pad_maximum_fusion.3.cols_ref, bf16[48,4096]{1,0:T(8,128)(2,1)S(1)} %get-tuple-element.19.a_ref), custom_call_target="tpu_custom_call" | custom-call | flops 4294967296 | bytes 2097152 | tf_op jit(solution)/shard_map/flux/pallas_call | solution.py:203
  24.7 1.7 %collective-permute-start.5 = (bf16[8,32,512]{2,1,0:T(8,128)(2,1)S(1)}, bf16[8,32,512]{2,1,0:T(8,128)(2,1)S(1)}, u32[]{:S(2)}, u32[]{:S(2)}) collective-permute-start(bf16[8,32,512]{2,1,0:T(8,128)(2,1)S(1)} %get-tuple-element.33), channel_id=1, source_target_pairs={{0,2},{1,3},{2,0},{3,1},{4,6},{5,7},{6,4},{7,5},{8,10},{9,11},{10,... | collective-permute-start | bytes 786440 | tf_op jit(solution)/shard_map/ppermute | solution.py:318
  26.4 11.1 %flux.6.refs_0_ = f32[48,4096]{1,0:T(8,128)S(1)} custom-call(bf16[6,32,512]{2,1,0:T(8,128)(2,1)S(1)} %pad_maximum_fusion.cols_ref, bf16[48,4096]{1,0:T(8,128)(2,1)S(1)} %get-tuple-element.19.a_ref, f32[48,4096]{1,0:T(8,128)S(1)} %flux.5.refs_0_), custom_call_target="tpu_custom_call" | custom-call | flops 12884901888 | bytes 2097152 | tf_op jit(solution)/shard_map/flux/pallas_call | solution.py:203
  37.6 1.7 %collective-permute-start.6 = (bf16[16,32,512]{2,1,0:T(8,128)(2,1)S(1)}, bf16[16,32,512]{2,1,0:T(8,128)(2,1)S(1)}, u32[]{:S(2)}, u32[]{:S(2)}) collective-permute-start(bf16[16,32,512]{2,1,0:T(8,128)(2,1)S(1)} %constant_dynamic-update-slice_fusion.5), channel_id=1, source_target_pairs={{0,1},{1,0},{2,3},{3,2},{4,5},{5,4},{6,7},{7,6},{8,9},{9,8},{10,11... | collective-permute-start | bytes 1572872 | tf_op jit(solution)/shard_map/ppermute | solution.py:318
  39.3 14.6 %flux.7.refs_0_ = f32[48,4096]{1,0:T(8,128)S(1)} custom-call(bf16[8,32,512]{2,1,0:T(8,128)(2,1)S(1)} %collective-permute-done.5.cols_ref, bf16[48,4096]{1,0:T(8,128)(2,1)S(1)} %get-tuple-element.19.a_ref, f32[48,4096]{1,0:T(8,128)S(1)} %flux.6.refs_0_), custom_call_target="tpu_custom_call" | custom-call | flops 17179869184 | bytes 2097152 | tf_op jit(solution)/shard_map/flux/pallas_call | solution.py:203
  53.9 21.8 %flux.8 = (f32[6,24,512]{2,1,0:T(8,128)S(1)}, f32[64,64]{1,0:T(8,128)S(1)}) custom-call(bf16[16,32,512]{2,1,0:T(8,128)(2,1)S(1)} %collective-permute-done.6.cols_ref, bf16[48,4096]{1,0:T(8,128)(2,1)S(1)} %get-tuple-element.19.a_ref, f32[48,4096]{1,0:T(8,128)S(1)} %flux.7.refs_0_, f32[8,8,512]{2,1,0:T(8,128)S(1)} %get-tuple-element.20.refs_1_, ...), custom_call_target="tpu_custom_call" | custom-call | flops 25769803776 | bytes 1572864 | tf_op jit(solution)/shard_map/flux/pallas_call | solution.py:203
  75.8 1.2 %collective-permute-start.10 = (f32[2,24,512]{2,1,0:T(8,128)S(1)}, f32[2,24,512]{2,1,0:T(8,128)S(1)}, u32[]{:S(2)}, u32[]{:S(2)}) collective-permute-start(f32[2,24,512]{2,1,0:T(8,128)S(1)} %get-tuple-element.32), channel_id=1, source_target_pairs={{0,192},{32,224},{64,0},{96,32},{128,64},{160,96},{192,128},{224,1... | collective-permute-start | bytes 294920 | tf_op jit(solution)/shard_map/ppermute | solution.py:310
  77.0 0.9 collective-permute-start.11
  77.9 1.7 %collective-permute-start.12 = (f32[2,24,512]{2,1,0:T(8,128)S(1)}, f32[2,24,512]{2,1,0:T(8,128)S(1)}, u32[]{:S(2)}, u32[]{:S(2)}) collective-permute-start(f32[2,24,512]{2,1,0:T(8,128)S(1)} %get-tuple-element.30), channel_id=1, source_target_pairs={{0,128},{32,160},{64,192},{96,224},{128,0},{160,32},{192,64},{224,... | collective-permute-start | bytes 294920 | tf_op jit(solution)/shard_map/ppermute | solution.py:310
  79.6 7.3 %flux.9.mine_ref = f32[2,24,512]{2,1,0:T(8,128)S(1)} custom-call(bf16[16,32,512]{2,1,0:T(8,128)(2,1)S(1)} %collective-permute-done.6.cols_ref, bf16[48,4096]{1,0:T(8,128)(2,1)S(1)} %get-tuple-element.19.a_ref, f32[48,4096]{1,0:T(8,128)S(1)} %flux.7.refs_0_, f32[8,8,512]{2,1,0:T(8,128)S(1)} %get-tuple-element.20.refs_1_, f32[64,64]{1,0:T(8,128)S(1)} %get-tuple-element.22.refs_2_), custom_call_target="tpu_custom_call" | custom-call | flops 8589934592 | bytes 524288 | tf_op jit(solution)/shard_map/flux/pallas_call | solution.py:203
  86.9 0.1 collective-permute-start.13
  87.0 1.2 %collective-permute-done.13.swap_ref = f32[24,512]{1,0:T(8,128)S(1)} collective-permute-done((f32[24,512]{1,0:T(8,128)S(1)}, f32[24,512]{1,0:T(8,128)S(1)}, u32[]{:S(2)}, u32[]{:S(2)}) %collective-permute-start.13) | collective-permute-done | bytes 49184 | tf_op jit(solution)/shard_map/ppermute | solution.py:306
  88.2 0.3 image.1
  88.6 14.3 %all_to_all.10.in_ref = f32[16,16,128]{2,1,0:T(8,128)S(1)} all-to-all(f32[16,16,128]{2,1,0:T(8,128)S(1)} %get-tuple-element.25), channel_id=1, replica_groups={{0,1,2,3,4,5,6,7,32,33,34,35,36,37,38,39},{8,9,10,11,12,13,14,15,40,41,..., dimensions={0} | all-to-all | bytes 262144 | tf_op jit(solution)/shard_map/all_to_all | solution.py:374
  102.9 0.1 middle.1
  103.0 12.1 %all_to_all.11.stats_ref = f32[16,24,128]{2,1,0:T(8,128)S(1)} all-to-all(f32[16,24,128]{2,1,0:T(8,128)S(1)} %middle.1), channel_id=1, replica_groups={{0,8,16,24,64,72,80,88,128,136,144,152,192,200,208,216},{1,9,17,25,65,7..., dimensions={0} | all-to-all | bytes 393216 | tf_op jit(solution)/shard_map/all_to_all | solution.py:376
  115.1 2.4 %finish.1 = (f32[16,512]{1,0:T(8,128)}, f32[16,64]{1,0:T(8,128)}, f32[16,16]{1,0:T(8,128)}) custom-call(f32[64,512]{1,0:T(8,128)S(1)} %copy-done, f32[16,512]{1,0:T(8,128)S(1)} %get-tuple-element.24.image_ref, f32[16,24,128]{2,1,0:T(8,128)S(1)} %all_to_all.11.stats_ref), custom_call_target="tpu_custom_call" | custom-call | tf_op jit(solution)/shard_map/finish/pallas_call | solution.py:290
  (40 shorter events, 0.3 us)
Async XLA Ops:
  0.6 0.8 copy-start.1
  1.4 0.7 copy-start.3
  2.1 3.4 %collective-permute-start = (bf16[32,512]{1,0:T(8,128)(2,1)S(1)}, bf16[32,512]{1,0:T(8,128)(2,1)S(1)}, u32[]{:S(2)}, u32[]{:S(2)}) collective-permute-start(bf16[32,512]{1,0:T(8,128)(2,1)S(1)} %payload.1), channel_id=1, source_target_pairs={{0,32},{32,0},{64,96},{96,64},{128,160},{160,128},{192,224},{224,1... | collective-permute-start | bytes 98312 | tf_op jit(solution)/shard_map/ppermute | solution.py:306
  2.2 8.7 %collective-permute-start.1 = (bf16[32,512]{1,0:T(8,128)(2,1)S(1)}, bf16[32,512]{1,0:T(8,128)(2,1)S(1)}, u32[]{:S(2)}, u32[]{:S(2)}) collective-permute-start(bf16[32,512]{1,0:T(8,128)(2,1)S(1)} %payload.1), channel_id=1, source_target_pairs={{0,8},{1,9},{2,10},{3,11},{4,12},{5,13},{6,14},{7,15},{8,16},{9,17... | collective-permute-start | bytes 98312 | tf_op jit(solution)/shard_map/ppermute | solution.py:314
  3.9 8.8 %collective-permute-start.2 = (bf16[32,512]{1,0:T(8,128)(2,1)S(1)}, bf16[32,512]{1,0:T(8,128)(2,1)S(1)}, u32[]{:S(2)}, u32[]{:S(2)}) collective-permute-start(bf16[32,512]{1,0:T(8,128)(2,1)S(1)} %payload.1), channel_id=1, source_target_pairs={{0,24},{1,25},{2,26},{3,27},{4,28},{5,29},{6,30},{7,31},{8,0},{9,1... | collective-permute-start | bytes 98312 | tf_op jit(solution)/shard_map/ppermute | solution.py:314
  5.6 7.2 %collective-permute-start.3 = (bf16[32,512]{1,0:T(8,128)(2,1)S(1)}, bf16[32,512]{1,0:T(8,128)(2,1)S(1)}, u32[]{:S(2)}, u32[]{:S(2)}) collective-permute-start(bf16[32,512]{1,0:T(8,128)(2,1)S(1)} %payload.1), channel_id=1, source_target_pairs={{0,16},{1,17},{2,18},{3,19},{4,20},{5,21},{6,22},{7,23},{8,24},{9,... | collective-permute-start | bytes 98312 | tf_op jit(solution)/shard_map/ppermute | solution.py:314
  7.7 11.5 %collective-permute-start.7 = (bf16[2,32,512]{2,1,0:T(8,128)(2,1)S(1)}, bf16[2,32,512]{2,1,0:T(8,128)(2,1)S(1)}, u32[]{:S(2)}, u32[]{:S(2)}) collective-permute-start(bf16[2,32,512]{2,1,0:T(8,128)(2,1)S(1)} %pad_maximum_fusion.2.pair_ref), channel_id=1, source_target_pairs={{0,64},{32,96},{64,128},{96,160},{128,192},{160,224},{192,0},{224,... | collective-permute-start | bytes 196616 | tf_op jit(solution)/shard_map/ppermute | solution.py:310
  9.1 10.1 %collective-permute-start.8 = (bf16[2,32,512]{2,1,0:T(8,128)(2,1)S(1)}, bf16[2,32,512]{2,1,0:T(8,128)(2,1)S(1)}, u32[]{:S(2)}, u32[]{:S(2)}) collective-permute-start(bf16[2,32,512]{2,1,0:T(8,128)(2,1)S(1)} %pad_maximum_fusion.2.pair_ref), channel_id=1, source_target_pairs={{0,192},{32,224},{64,0},{96,32},{128,64},{160,96},{192,128},{224,1... | collective-permute-start | bytes 196616 | tf_op jit(solution)/shard_map/ppermute | solution.py:310
  10.9 8.3 %collective-permute-start.9 = (bf16[2,32,512]{2,1,0:T(8,128)(2,1)S(1)}, bf16[2,32,512]{2,1,0:T(8,128)(2,1)S(1)}, u32[]{:S(2)}, u32[]{:S(2)}) collective-permute-start(bf16[2,32,512]{2,1,0:T(8,128)(2,1)S(1)} %pad_maximum_fusion.2.pair_ref), channel_id=1, source_target_pairs={{0,128},{32,160},{64,192},{96,224},{128,0},{160,32},{192,64},{224,... | collective-permute-start | bytes 196616 | tf_op jit(solution)/shard_map/ppermute | solution.py:310
  12.8 11.9 %collective-permute-start.4 = (bf16[4,32,512]{2,1,0:T(8,128)(2,1)S(1)}, bf16[4,32,512]{2,1,0:T(8,128)(2,1)S(1)}, u32[]{:S(2)}, u32[]{:S(2)}) collective-permute-start(bf16[4,32,512]{2,1,0:T(8,128)(2,1)S(1)} %pad_maximum_fusion.1), channel_id=1, source_target_pairs={{0,4},{1,5},{2,6},{3,7},{4,0},{5,1},{6,2},{7,3},{8,12},{9,13},{10,... | collective-permute-start | bytes 393224 | tf_op jit(solution)/shard_map/ppermute | solution.py:318
  19.2 0.8 copy-start.2
  19.2 0.8 copy-start.6
  19.2 0.8 copy-start.7
  19.2 0.7 copy-start.5
  19.2 0.7 copy-start.4
  19.2 0.7 copy-start.8
  19.2 0.7 copy-start.9
  24.7 12.8 %collective-permute-start.5 = (bf16[8,32,512]{2,1,0:T(8,128)(2,1)S(1)}, bf16[8,32,512]{2,1,0:T(8,128)(2,1)S(1)}, u32[]{:S(2)}, u32[]{:S(2)}) collective-permute-start(bf16[8,32,512]{2,1,0:T(8,128)(2,1)S(1)} %get-tuple-element.33), channel_id=1, source_target_pairs={{0,2},{1,3},{2,0},{3,1},{4,6},{5,7},{6,4},{7,5},{8,10},{9,11},{10,... | collective-permute-start | bytes 786440 | tf_op jit(solution)/shard_map/ppermute | solution.py:318
  37.5 16.3 %copy-start = (f32[64,512]{1,0:T(8,128)S(1)}, f32[64,512]{1,0:T(8,128)}, u32[]{:S(2)}) copy-start(f32[64,512]{1,0:T(8,128)} %krylov_ref.3) | copy-start | bytes 393220
  37.6 16.3 %collective-permute-start.6 = (bf16[16,32,512]{2,1,0:T(8,128)(2,1)S(1)}, bf16[16,32,512]{2,1,0:T(8,128)(2,1)S(1)}, u32[]{:S(2)}, u32[]{:S(2)}) collective-permute-start(bf16[16,32,512]{2,1,0:T(8,128)(2,1)S(1)} %constant_dynamic-update-slice_fusion.5), channel_id=1, source_target_pairs={{0,1},{1,0},{2,3},{3,2},{4,5},{5,4},{6,7},{7,6},{8,9},{9,8},{10,11... | collective-permute-start | bytes 1572872 | tf_op jit(solution)/shard_map/ppermute | solution.py:318
  75.8 11.1 %collective-permute-start.10 = (f32[2,24,512]{2,1,0:T(8,128)S(1)}, f32[2,24,512]{2,1,0:T(8,128)S(1)}, u32[]{:S(2)}, u32[]{:S(2)}) collective-permute-start(f32[2,24,512]{2,1,0:T(8,128)S(1)} %get-tuple-element.32), channel_id=1, source_target_pairs={{0,192},{32,224},{64,0},{96,32},{128,64},{160,96},{192,128},{224,1... | collective-permute-start | bytes 294920 | tf_op jit(solution)/shard_map/ppermute | solution.py:310
  77.0 9.9 %collective-permute-start.11 = (f32[2,24,512]{2,1,0:T(8,128)S(1)}, f32[2,24,512]{2,1,0:T(8,128)S(1)}, u32[]{:S(2)}, u32[]{:S(2)}) collective-permute-start(f32[2,24,512]{2,1,0:T(8,128)S(1)} %get-tuple-element.31), channel_id=1, source_target_pairs={{0,64},{32,96},{64,128},{96,160},{128,192},{160,224},{192,0},{224,... | collective-permute-start | bytes 294920 | tf_op jit(solution)/shard_map/ppermute | solution.py:310
  77.9 9.0 %collective-permute-start.12 = (f32[2,24,512]{2,1,0:T(8,128)S(1)}, f32[2,24,512]{2,1,0:T(8,128)S(1)}, u32[]{:S(2)}, u32[]{:S(2)}) collective-permute-start(f32[2,24,512]{2,1,0:T(8,128)S(1)} %get-tuple-element.30), channel_id=1, source_target_pairs={{0,128},{32,160},{64,192},{96,224},{128,0},{160,32},{192,64},{224,... | collective-permute-start | bytes 294920 | tf_op jit(solution)/shard_map/ppermute | solution.py:310
  86.9 1.3 %collective-permute-start.13 = (f32[24,512]{1,0:T(8,128)S(1)}, f32[24,512]{1,0:T(8,128)S(1)}, u32[]{:S(2)}, u32[]{:S(2)}) collective-permute-start(f32[24,512]{1,0:T(8,128)S(1)} %fusion), channel_id=1, source_target_pairs={{0,32},{32,0},{64,96},{96,64},{128,160},{160,128},{192,224},{224,1... | collective-permute-start | bytes 147464 | tf_op jit(solution)/shard_map/ppermute | solution.py:306
